TPU v7x, 32 devices: a whole 2x2x4 slice. The times are simulated.
32 devices in a mesh: section: 4 (over y, x), dp: 8 (over z, core).
Axes of the slice: x: 2, y: 2, z: 4, core: 2. Of those that a mesh axis runs over, the one named last changes fastest.
Arguments:
- text_rows: bfloat16 [32, 2, 300, 768], P(('section', 'dp')), may hold values from -6 to 6
- memory_init: bfloat16 [10, 768], replicated, may hold values from -6 to 6
- cotangent: bfloat16 [32, 2, 320, 768], P(('section', 'dp')), may hold values from -6 to 6
- w_qkv: bfloat16 [4, 384, 2304], P('section'), may hold values from -0.21875 to 0.21875
- w_out: bfloat16 [4, 384, 768], P('section'), may hold values from -0.875 to 0.875
- w_in: bfloat16 [4, 384, 3072], P('section'), may hold values from -0.21875 to 0.21875
- w_hid: bfloat16 [4, 1536, 768], P('section'), may hold values from -0.109375 to 0.109375
- biases: bfloat16 [4, 3840], P('section'), may hold values from -1.5 to 1.5
- norm_gains: bfloat16 [4, 768], P('section'), may hold values from 0.25 to 1.75
- boundaries: int32 [32, 2, 300], P(('section', 'dp')), may hold values 0 or 1
- mem_resets: int32 [32, 2], P(('section', 'dp')), may hold values 0 or 1
- seg_counts: int32 [32], P(('section', 'dp')), may hold values from 1 to 2, as said below
Outputs:
- activations: bfloat16 [32, 2, 320, 768], P(('section', 'dp'))
- input_grads: bfloat16 [32, 2, 320, 768], P(('section', 'dp'))
- memory_grad: float32 [10, 768], replicated
- qkv_grad: float32 [4, 384, 2304], P('section', None, 'dp')
- proj_grad: float32 [4, 384, 768], P('section', None, 'dp')
- up_grad: float32 [4, 384, 3072], P('section', None, 'dp')
- down_grad: float32 [4, 1536, 768], P('section', None, 'dp')
- bias_grad: float32 [4, 3840], P('section', 'dp')
- gain_grad: float32 [4, 768], P('section', 'dp')
Inputs may be any that keep to these rules, and one draw needn't show every extreme that they name: `seg_counts`: every item has at least one segment, and some item has 2.
All inputs are finite; a program needn't handle non-finite values. No bound on the sum of `boundaries` or of `mem_resets` on one device may be relied on, other than what follows from the above.
Results may differ from a plain program's by a relative error of at most 0.02.
Values may be sent and summed in bfloat16 or wider, within the bound.
A program may use at most 512 MiB of HBM per device.

v0:
```python
from functools import partial

import jax
import jax.numpy as jnp
from jax import lax
from jax.sharding import PartitionSpec as P

HEADS = 12
HEAD_DIM = 64


EPS = 1e-05
MASKED = -1e30


def partner(block, axis, distance):
    count = lax.axis_size(axis)
    route = []
    for low in range(count):
        high = low | 1 << distance
        if high != low and high < count:
            route += [(low, high), (high, low)]
    return lax.ppermute(block, axis, route)


def norm_rows(values, scale_vec, shift_vec):
    centre = jnp.mean(values, axis=-1, keepdims=True)
    offset = values - centre
    spread = jnp.mean(offset * offset, axis=-1, keepdims=True)
    return offset * lax.rsqrt(spread + EPS) * scale_vec + shift_vec


def exact_gelu(values):
    return jax.nn.gelu(values, approximate=False)


def split_vector(vector, width, hidden):
    vector = vector.astype(jnp.float32)
    bounds_list = [
        0,
        width,
        2 * width,
        3 * width,
        4 * width,
        4 * width + hidden,
        5 * width + hidden,
        6 * width + hidden,
    ]
    return [vector[bounds_list[number] : bounds_list[number + 1]] for number in range(7)]


def doc_allowed(bounds, mem_rows):
    numbers = jnp.cumsum(bounds, axis=-1)
    filler = jnp.full(bounds.shape[:-1] + (mem_rows,), -1, jnp.int32)
    labels = jnp.concatenate([filler, numbers, filler], axis=-1)
    row_side = labels[..., :, None]
    col_side = labels[..., None, :]
    return (row_side == col_side) | (row_side < 0) | (col_side < 0)


def split_heads(mixed_b, width):
    rows = mixed_b.shape[0]
    queries = mixed_b[:, :width].reshape(rows, HEADS, HEAD_DIM)
    keys_b = mixed_b[:, width : 2 * width].reshape(rows, HEADS, HEAD_DIM)
    values_b = mixed_b[:, 2 * width :].reshape(rows, HEADS, HEAD_DIM)
    return (queries, keys_b, values_b)


def masked_scores(queries, keys_b, allowed):
    scores = jnp.einsum(
        "qhd,khd->hqk", queries, keys_b, preferred_element_type=jnp.float32
    ) * HEAD_DIM ** (-0.5)
    return jnp.where(allowed[None], scores, MASKED)


def layer_forward(inputs, weights, allowed):
    w_mix, w_proj, w_up, w_down, vector, gain_pair = weights
    rows, width = inputs.shape
    hidden = w_up.shape[1]
    bias_q, bias_v, bias_o, shift_one, bias_in, bias_hid, shift_two = split_vector(
        vector, width, hidden
    )
    gain_pair = gain_pair.astype(jnp.float32)
    mixed = jnp.dot(inputs, w_mix, preferred_element_type=jnp.float32)
    mixed = mixed + jnp.concatenate([bias_q, jnp.zeros_like(bias_q), bias_v])
    mixed_b = mixed.astype(jnp.bfloat16)
    queries, keys_b, values_b = split_heads(mixed_b, width)
    scores = masked_scores(queries, keys_b, allowed)
    peak = jnp.max(scores, axis=-1, keepdims=True)
    expo = jnp.exp(scores - peak)
    totals = jnp.sum(expo, axis=-1, keepdims=True)
    probs_b = (expo / totals).astype(jnp.bfloat16)
    log_total = peak + jnp.log(totals)
    heads_b = (
        jnp.einsum("hqk,khd->qhd", probs_b, values_b, preferred_element_type=jnp.float32)
        .reshape(rows, width)
        .astype(jnp.bfloat16)
    )
    attn = jnp.dot(heads_b, w_proj, preferred_element_type=jnp.float32) + bias_o
    resid = inputs.astype(jnp.float32) + attn
    first = norm_rows(resid, gain_pair[:width], shift_one)
    first_b = first.astype(jnp.bfloat16)
    inner = jnp.dot(first_b, w_up, preferred_element_type=jnp.float32) + bias_in
    active_b = exact_gelu(inner).astype(jnp.bfloat16)
    branch = jnp.dot(active_b, w_down, preferred_element_type=jnp.float32) + bias_hid
    second = first + branch
    output = norm_rows(second, gain_pair[width:], shift_two)
    return (
        output,
        (inputs, mixed_b, log_total, heads_b, resid, first, first_b, inner, active_b, second),
    )


def layer_backward(grad_out, stored, weights, allowed):
    w_mix, w_proj, w_up, w_down, vector, gain_pair = weights
    inputs, mixed_b, log_total, heads_b, resid, first, first_b, inner, active_b, second = stored
    rows, width = inputs.shape
    hidden = w_up.shape[1]
    bias_q, bias_v, bias_o, shift_one, bias_in, bias_hid, shift_two = split_vector(
        vector, width, hidden
    )
    gain_pair = gain_pair.astype(jnp.float32)
    gain_one = gain_pair[:width]
    gain_two = gain_pair[width:]
    fl_type = jnp.float32
    bf_type = jnp.bfloat16
    _, pull_two = jax.vjp(norm_rows, second, gain_two, shift_two)
    grad_second, grad_gain_two, grad_shift_two = pull_two(grad_out)
    grad_branch = grad_second.astype(bf_type)
    grad_bias_hid = jnp.sum(grad_branch.astype(fl_type), axis=0)
    grad_down = jnp.einsum("rf,rd->fd", active_b, grad_branch, preferred_element_type=fl_type)
    grad_active = jnp.einsum("rd,fd->rf", grad_branch, w_down, preferred_element_type=fl_type)
    _, pull_gelu = jax.vjp(exact_gelu, inner)
    grad_inner = pull_gelu(grad_active)[0].astype(bf_type)
    grad_bias_in = jnp.sum(grad_inner.astype(fl_type), axis=0)
    grad_up = jnp.einsum("rd,rf->df", first_b, grad_inner, preferred_element_type=fl_type)
    grad_first = grad_second + jnp.einsum(
        "rf,df->rd", grad_inner, w_up, preferred_element_type=fl_type
    )
    _, pull_one = jax.vjp(norm_rows, resid, gain_one, shift_one)
    grad_resid, grad_gain_one, grad_shift_one = pull_one(grad_first)
    grad_attn = grad_resid.astype(bf_type)
    grad_bias_o = jnp.sum(grad_attn.astype(fl_type), axis=0)
    grad_proj = jnp.einsum("rd,re->de", heads_b, grad_attn, preferred_element_type=fl_type)
    grad_heads = jnp.einsum("re,de->rd", grad_attn, w_proj, preferred_element_type=fl_type).astype(
        bf_type
    )
    grad_heads = grad_heads.reshape(rows, HEADS, HEAD_DIM)
    queries, keys_b, values_b = split_heads(mixed_b, width)
    scores = masked_scores(queries, keys_b, allowed)
    probs = jnp.exp(scores - log_total)
    probs_b = probs.astype(bf_type)
    grad_value = jnp.einsum("hqk,qhd->khd", probs_b, grad_heads, preferred_element_type=fl_type)
    grad_probs = jnp.einsum("qhd,khd->hqk", grad_heads, values_b, preferred_element_type=fl_type)
    centre = jnp.sum(probs * grad_probs, axis=-1, keepdims=True)
    grad_scores = (probs * (grad_probs - centre)).astype(bf_type)
    grad_query = jnp.einsum(
        "hqk,khd->qhd", grad_scores, keys_b, preferred_element_type=fl_type
    ) * HEAD_DIM ** (-0.5)
    grad_key = jnp.einsum(
        "hqk,qhd->khd", grad_scores, queries, preferred_element_type=fl_type
    ) * HEAD_DIM ** (-0.5)
    grad_mixed = jnp.concatenate(
        [
            grad_query.reshape(rows, width),
            grad_key.reshape(rows, width),
            grad_value.reshape(rows, width),
        ],
        axis=1,
    ).astype(bf_type)
    grad_bias_q = jnp.sum(grad_mixed[:, :width].astype(fl_type), axis=0)
    grad_bias_v = jnp.sum(grad_mixed[:, 2 * width :].astype(fl_type), axis=0)
    grad_mix = jnp.einsum("rd,re->de", inputs, grad_mixed, preferred_element_type=fl_type)
    grad_inputs = (
        grad_resid + jnp.einsum("re,de->rd", grad_mixed, w_mix, preferred_element_type=fl_type)
    ).astype(bf_type)
    grad_vector = jnp.concatenate(
        [
            grad_bias_q,
            grad_bias_v,
            grad_bias_o,
            grad_shift_one,
            grad_bias_in,
            grad_bias_hid,
            grad_shift_two,
        ]
    )
    grad_gain = jnp.concatenate([grad_gain_one, grad_gain_two])
    return (grad_inputs, (grad_mix, grad_proj, grad_up, grad_down, grad_vector, grad_gain))


def blank_forward(rows, width, hidden):
    fl_type = jnp.float32
    bf_type = jnp.bfloat16
    stored = (
        jnp.zeros((rows, width), bf_type),
        jnp.zeros((rows, 3 * width), bf_type),
        jnp.zeros((HEADS, rows, 1), fl_type),
        jnp.zeros((rows, width), bf_type),
        jnp.zeros((rows, width), fl_type),
        jnp.zeros((rows, width), fl_type),
        jnp.zeros((rows, width), bf_type),
        jnp.zeros((rows, hidden), fl_type),
        jnp.zeros((rows, hidden), bf_type),
        jnp.zeros((rows, width), fl_type),
    )
    return (jnp.zeros((rows, width), fl_type), stored)


def blank_backward(rows, width, hidden, vector_len):
    fl_type = jnp.float32
    grads = (
        jnp.zeros((width, 3 * width), fl_type),
        jnp.zeros((width, width), fl_type),
        jnp.zeros((width, hidden), fl_type),
        jnp.zeros((hidden, width), fl_type),
        jnp.zeros((vector_len,), fl_type),
        jnp.zeros((2 * width,), fl_type),
    )
    return (jnp.zeros((rows, width), jnp.bfloat16), grads)


def own_half(values, which):
    half_rows = values.shape[0] // 2
    return lax.dynamic_slice_in_dim(values, which * half_rows, half_rows, 0)


def per_device(
    text_rows,
    memory_init,
    cotangent,
    w_qkv,
    w_out,
    w_in,
    w_hid,
    biases,
    norm_gains,
    boundaries,
    mem_resets,
    seg_counts,
):
    fl_type = jnp.float32
    bf_type = jnp.bfloat16
    section_place = lax.axis_index("section")
    section_role = section_place % 2
    item_group = section_place // 2
    first_rank = section_role == 0
    held_blocks = (w_qkv[0], w_out[0], w_in[0], w_hid[0], biases[0], norm_gains[0])
    partner_blocks = partner(
        (w_qkv[0], w_out[0], w_in[0], w_hid[0], biases[0], norm_gains[0]), "section", 1
    )
    weights = tuple(
        (
            jnp.where(
                item_group == 0,
                jnp.concatenate([mine, theirs], axis=0),
                jnp.concatenate([theirs, mine], axis=0),
            )
            for mine, theirs in zip(held_blocks, partner_blocks)
        )
    )
    held_items = text_rows.shape[0]
    segs = text_rows.shape[1]
    text_len = text_rows.shape[2]
    mem_rows = memory_init.shape[0]
    width = memory_init.shape[1]
    seg_rows = text_len + 2 * mem_rows
    hidden = w_in.shape[2]
    vector_len = 2 * biases.shape[1]
    padded = jnp.pad(text_rows, ((0, 0), (0, 0), (mem_rows, mem_rows), (0, 0)))
    outgoing = jnp.where(first_rank, cotangent, padded)
    got_rows, got_bounds, got_resets, got_counts = partner(
        (
            outgoing,
            boundaries.astype(bf_type),
            mem_resets.astype(bf_type),
            seg_counts.astype(bf_type),
        ),
        "section",
        0,
    )
    text_pair = jnp.concatenate([padded, got_rows], axis=0)
    cot_pair = jnp.concatenate([got_rows, cotangent], axis=0)

    def in_order(mine, theirs):
        theirs = theirs.astype(jnp.int32)
        return jnp.where(
            first_rank,
            jnp.concatenate([mine, theirs], axis=0),
            jnp.concatenate([theirs, mine], axis=0),
        )

    bounds_pair = in_order(boundaries, got_bounds)
    resets_pair = in_order(mem_resets, got_resets)
    counts_pair = in_order(seg_counts, got_counts)
    allowed_all = doc_allowed(bounds_pair, mem_rows)
    pair_items = 2 * held_items
    micro = pair_items * segs
    zero_rows = jnp.zeros((seg_rows, width), bf_type)
    memories = [memory_init for number in range(pair_items)]
    incoming = zero_rows
    stored_list = []
    live_list = []
    out_list = [zero_rows for number in range(micro)]
    for tick_index in range(micro + 1):
        if tick_index < micro:
            item_zero = tick_index % pair_items
            seg_zero = tick_index // pair_items
            if seg_zero == 0:
                mem_now = memory_init
            else:
                mem_now = jnp.where(
                    resets_pair[item_zero, seg_zero] > 0, memory_init, memories[item_zero]
                )
            middle_rows = text_pair[item_zero, seg_zero, mem_rows : mem_rows + text_len]
            input_zero = jnp.concatenate([mem_now, middle_rows, mem_now], axis=0)
            live_zero = seg_zero < counts_pair[item_zero]
            mask_zero = allowed_all[item_zero, seg_zero]
        else:
            input_zero = zero_rows
            live_zero = jnp.asarray(False)
            mask_zero = allowed_all[0, 0]
        if tick_index >= 1:
            item_one = (tick_index - 1) % pair_items
            seg_one = (tick_index - 1) // pair_items
            live_one = seg_one < counts_pair[item_one]
            mask_one = allowed_all[item_one, seg_one]
        else:
            live_one = jnp.asarray(False)
            mask_one = allowed_all[0, 0]
        layer_in = jnp.where(first_rank, input_zero, incoming)
        live_now = jnp.where(first_rank, live_zero, live_one)
        mask_now = jnp.where(first_rank, mask_zero, mask_one)
        result, stored = lax.cond(
            live_now,
            partial(layer_forward, layer_in, weights, mask_now),
            partial(blank_forward, seg_rows, width, hidden),
        )
        result_b = result.astype(bf_type)
        received = partner(result_b, "section", 0)
        if tick_index >= 1:
            out_list[tick_index - 1] = result_b
            memories[(tick_index - 1) % pair_items] = received[seg_rows - mem_rows :]
        incoming = received
        stored_list.append(stored)
        live_list.append(live_now)

    def fold_memory(grad_rows):
        summed = grad_rows[:mem_rows].astype(fl_type) + grad_rows[seg_rows - mem_rows :].astype(
            fl_type
        )
        return summed.astype(bf_type).astype(fl_type)

    grad_in = zero_rows
    mem_grads = [jnp.zeros((mem_rows, width), fl_type) for number in range(pair_items)]
    input_list = [zero_rows for number in range(micro)]
    init_grad = jnp.zeros((mem_rows, width), fl_type)
    totals = blank_backward(seg_rows, width, hidden, vector_len)[1]
    for step_back in range(micro + 1):
        tick_index = micro - step_back
        micro_one = micro - 1 - step_back
        micro_zero = micro - step_back
        if micro_one >= 0:
            item_one = micro_one % pair_items
            seg_one = micro_one // pair_items
            cot_now = cot_pair[item_one, seg_one].astype(fl_type)
            upper_part = cot_now[: seg_rows - mem_rows]
            lower_part = cot_now[seg_rows - mem_rows :] + mem_grads[item_one]
            grad_one = jnp.concatenate([upper_part, lower_part], axis=0).astype(bf_type)
            mask_one = allowed_all[item_one, seg_one]
        else:
            grad_one = zero_rows
            mask_one = allowed_all[0, 0]
        if micro_zero < micro:
            mask_zero = allowed_all[micro_zero % pair_items, micro_zero // pair_items]
        else:
            mask_zero = allowed_all[0, 0]
        grad_now = jnp.where(first_rank, grad_in, grad_one).astype(fl_type)
        mask_now = jnp.where(first_rank, mask_zero, mask_one)
        grad_rows_now, grads = lax.cond(
            live_list[tick_index],
            partial(layer_backward, grad_now, stored_list[tick_index], weights, mask_now),
            partial(blank_backward, seg_rows, width, hidden, vector_len),
        )
        received = partner(grad_rows_now, "section", 0)
        grad_in = received
        totals = jax.tree.map(jnp.add, totals, grads)
        if micro_zero < micro:
            item_zero = micro_zero % pair_items
            seg_zero = micro_zero // pair_items
            if seg_zero == 0:
                fresh_now = jnp.asarray(True)
            else:
                fresh_now = resets_pair[item_zero, seg_zero] > 0
            init_grad = init_grad + jnp.where(
                first_rank & fresh_now, fold_memory(grad_rows_now), 0.0
            )
            if seg_zero >= 1:
                mem_grads[item_zero] = jnp.where(fresh_now, 0.0, fold_memory(received))
            input_list[micro_zero] = grad_rows_now
    acts_all = jnp.stack(
        [
            jnp.stack([out_list[seg_index * pair_items + item_index] for seg_index in range(segs)])
            for item_index in range(pair_items)
        ]
    )
    grads_all = jnp.stack(
        [
            jnp.stack(
                [input_list[seg_index * pair_items + item_index] for seg_index in range(segs)]
            )
            for item_index in range(pair_items)
        ]
    )
    sending = jnp.where(first_rank, grads_all[held_items:], acts_all[:held_items])
    returned = partner(sending, "section", 0)
    activations = jnp.where(first_rank, returned, acts_all[held_items:])
    input_grads = jnp.where(first_rank, grads_all[:held_items], returned)
    memory_grad = lax.psum(init_grad, ("section", "dp"))
    grad_mix, grad_proj, grad_up, grad_down, grad_vector, grad_gain = totals
    grad_vector = grad_vector.reshape(2, -1)
    grad_gain = grad_gain.reshape(2, -1)
    scattered = (
        lax.psum_scatter(grad_mix, "dp", scatter_dimension=1, tiled=True),
        lax.psum_scatter(grad_proj, "dp", scatter_dimension=1, tiled=True),
        lax.psum_scatter(grad_up, "dp", scatter_dimension=1, tiled=True),
        lax.psum_scatter(grad_down, "dp", scatter_dimension=1, tiled=True),
        lax.psum_scatter(grad_vector, "dp", scatter_dimension=1, tiled=True),
        lax.psum_scatter(grad_gain, "dp", scatter_dimension=1, tiled=True),
    )
    kept_half = [own_half(piece, item_group) for piece in scattered]
    given_half = [own_half(piece, 1 - item_group) for piece in scattered]
    partner_half = (
        partner(given_half[0].astype(jnp.bfloat16), "section", 1).astype(jnp.float32),
        partner(given_half[1].astype(jnp.bfloat16), "section", 1).astype(jnp.float32),
        partner(given_half[2].astype(jnp.bfloat16), "section", 1).astype(jnp.float32),
        partner(given_half[3].astype(jnp.bfloat16), "section", 1).astype(jnp.float32),
        partner(given_half[4].astype(jnp.bfloat16), "section", 1).astype(jnp.float32),
        partner(given_half[5].astype(jnp.bfloat16), "section", 1).astype(jnp.float32),
    )
    final = [mine + theirs for mine, theirs in zip(kept_half, partner_half)]
    return (
        activations,
        input_grads,
        memory_grad,
        final[0][None],
        final[1][None],
        final[2][None],
        final[3][None],
        final[4],
        final[5],
    )


def solution(mesh):
    in_specs = (
        P(("section", "dp"), None, None, None),
        P(),
        P(("section", "dp"), None, None, None),
        P("section", None, None),
        P("section", None, None),
        P("section", None, None),
        P("section", None, None),
        P("section", None),
        P("section", None),
        P(("section", "dp"), None, None),
        P(("section", "dp"), None),
        P(("section", "dp")),
    )
    out_specs = (
        P(("section", "dp"), None, None, None),
        P(("section", "dp"), None, None, None),
        P(),
        P("section", None, "dp"),
        P("section", None, "dp"),
        P("section", None, "dp"),
        P("section", None, "dp"),
        P("section", "dp"),
        P("section", "dp"),
    )
    return jax.shard_map(
        per_device, mesh=mesh, in_specs=in_specs, out_specs=out_specs, check_vma=False
    )
```

profile of v0, /device:TPU:0, one launch (start us, length us, event | category | flops | bytes accessed | tf_op | source)
XLA Modules:
  0.0 1317.0 jit_solution(1890574863736444280)
XLA Ops:
  25.2 15.7 %collective-permute-done.6 = bf16[1,2,300]{2,1,0:T(2,128)(2,1)S(1)} collective-permute-done((bf16[1,2,300]{2,1,0:T(2,128)(2,1)S(1)}, bf16[1,2,300]{2,1,0:T(2,128)(2,1)S(1)}, u32[]{:S(2)}, u32[]{:S(2)}) %collective-permute-start.6) | collective-permute-done | bytes 1232 | tf_op jit(solution)/shard_map/ppermute | solution.py:23
  45.0 114.0 %collective-permute-done.5 = bf16[3840]{0:T(1024)(128)(2,1)S(1)} collective-permute-done((bf16[3840]{0:T(1024)(128)(2,1)S(1)}, bf16[3840]{0:T(1024)(128)(2,1)S(1)}, u32[]{:S(2)}, u32[]{:S(2)}) %collective-permute-start.5) | collective-permute-done | bytes 7712 | tf_op jit(solution)/shard_map/ppermute | solution.py:23
  160.2 12.2 collective-permute-done.7
  180.9 7.9 maximum_select_fusion
  188.8 6.2 maximum_select_fusion.1
  195.8 37.2 %conditional.10 = (f32[320,768]{1,0:T(8,128)S(1)}, bf16[320,768]{1,0:T(8,128)(2,1)}, bf16[320,2304]{1,0:T(8,128)(2,1)}, f32[12,320,1]{1,0,2:T(8,128)S(1)}, bf16[...) conditional(s32[]{:T(128)} %convert_element_type.563, ...), branch_computations={%region_2.3_spmd, %region_3.10_spmd} | conditional | flops 4932404224 | bytes 101358888 | solution.py:334
  213.9 11.6 fusion.5
  235.8 7.4 collective-permute-done.10
  243.3 39.8 %conditional.11 = (bf16[320,768]{1,0:T(8,128)(2,1)S(1)}, bf16[320,2304]{1,0:T(8,128)(2,1)S(1)}, f32[12,320,1]{1,0,2:T(8,128)S(1)}, bf16[320,768]{0,1:T(8,128)(2,...) conditional(s32[]{:T(128)} %convert_element_type.555, ...), branch_computations={%region_10.11_spmd, %region_11.18_spmd} | conditional | flops 4933879296 | bytes 139706368 | solution.py:334
  262.6 11.7 fusion.25
  286.7 6.8 collective-permute-done.2
  296.1 9.7 conditional.12
  305.8 32.5 %collective-permute-start.12 = (bf16[320,768]{1,0:T(8,128)(2,1)}, bf16[320,768]{1,0:T(8,128)(2,1)S(1)}, u32[]{:S(2)}, u32[]{:S(2)}) collective-permute-start(bf16[320,768]{1,0:T(8,128)(2,1)} %get-tuple-element.506), channel_id=1, source_target_pairs={{0,8},{8,0},{16,24},{24,16},{1,9},{9,1},{17,25},{25,17},{2,10},{10... | collective-permute-start | bytes 1474568 | tf_op jit(solution)/shard_map/ppermute | solution.py:23
  339.6 5.7 collective-permute-done.12
  346.5 8.9 conditional.13
  357.6 6.8 collective-permute-done.13
  364.4 9.8 conditional.14
  375.3 27.2 %conditional.15 = (bf16[320,768]{1,0:T(8,128)(2,1)S(1)}, f32[768,2304]{0,1:T(8,128)}, f32[768,768]{0,1:T(8,128)}, f32[3072,768]{0,1:T(8,128)}, f32[7680]{0:T(102...) conditional(s32[]{:T(128)} %convert_element_type.558, () %tuple.99, (bf16[1536]{0:T(1024)(128)(2,1)S(1)}, ...), branch_computations={%region_42.43_spmd, %region_43.62_spmd} | conditional | flops 9962610688 | bytes 238590112 | solution.py:380
  385.5 4.8 broadcast.1678
  390.9 4.8 broadcast.1677.clone
  404.6 6.8 collective-permute-done.14
  413.5 22.6 %conditional.16 = (bf16[320,768]{1,0:T(8,128)(2,1)}, f32[768,2304]{0,1:T(8,128)}, f32[768,768]{0,1:T(8,128)}, f32[3072,768]{0,1:T(8,128)}, f32[7680]{0:T(1024)}, /*index=5*/f32[1536]{0:T(1024)S(1)}, f32[768,3072]{1,0:T(8,128)}) conditional(s32[]{:T(128)} %convert_element_type.557, () %tuple.98, (bf16[1536]{0:T(1024)(128)(2,1)S(1)}, ...), branch_computations={%region_62.63_spmd, %region_63.82_spmd} | conditional | flops 9961138176 | bytes 227284960 | solution.py:380
  419.2 4.8 broadcast.1721
  439.2 6.0 collective-permute-done.15
  447.0 21.9 %conditional.17 = (bf16[320,768]{1,0:T(8,128)(2,1)S(1)}, f32[768,2304]{0,1:T(8,128)}, f32[768,768]{0,1:T(8,128)}, f32[3072,768]{0,1:T(8,128)}, f32[7680]{0:T(102...) conditional(s32[]{:T(128)} %convert_element_type.556, () %tuple.97, (bf16[1536]{0:T(1024)(128)(2,1)S(1)}, ...), branch_computations={%region_82.83_spmd, %region_83.102_spmd} | conditional | flops 9961138176 | bytes 235149408 | solution.py:380
  469.0 67.1 %collective-permute-start.16 = (bf16[320,768]{1,0:T(8,128)(2,1)S(1)}, bf16[320,768]{1,0:T(8,128)(2,1)S(1)}, u32[]{:S(2)}, u32[]{:S(2)}) collective-permute-start(bf16[320,768]{1,0:T(8,128)(2,1)S(1)} %get-tuple-element.537), channel_id=1, source_target_pairs={{0,8},{8,0},{16,24},{24,16},{1,9},{9,1},{17,25},{25,17},{2,10},{10... | collective-permute-start | bytes 1474568 | tf_op jit(solution)/shard_map/ppermute | solution.py:23
  537.1 10.7 collective-permute-done.16
  548.8 78.2 %conditional.18 = (bf16[320,768]{1,0:T(8,128)(2,1)}, f32[768,2304]{0,1:T(8,128)}, f32[768,768]{0,1:T(8,128)}, f32[3072,768]{0,1:T(8,128)}, f32[7680]{0:T(1024)}, /*index=5*/f32[1536]{0:T(1024)S(1)}, f32[768,3072]{1,0:T(8,128)}) conditional(s32[]{:T(128)} %convert_element_type.555, () %tuple.96, (bf16[1536]{0:T(1024)(128)(2,1)S(1)}, ...), branch_computations={%region_102.103_spmd, %region_103.122_spmd} | conditional | flops 9961138176 | bytes 233183296 | solution.py:380
  555.7 12.4 convert_reduce_fusion.16
  586.4 4.8 convolution_bitcast_fusion.14
  593.4 6.9 convolution_bitcast_fusion.12
  609.1 7.8 convolution_bitcast_fusion.13
  617.0 9.6 copy.251
  629.3 7.3 collective-permute-done.18
  636.7 85.3 %conditional.19 = (bf16[320,768]{1,0:T(8,128)(2,1)}, f32[768,2304]{0,1:T(8,128)}, f32[768,768]{0,1:T(8,128)}, f32[3072,768]{0,1:T(8,128)}, f32[7680]{0:T(1024)}, /*index=5*/f32[1536]{0:T(1024)S(1)}, f32[768,3072]{1,0:T(8,128)}) conditional(s32[]{:T(128)} %convert_element_type.563, () %tuple.114, (bf16[1536]{0:T(1024)(128)(2,1)S(1)}, ...), branch_computations={%region_122.123_spmd, %region_123.142_spmd} | conditional | flops 9961138176 | bytes 235149344 | solution.py:380
  645.1 12.4 convert_reduce_fusion.21
  679.6 5.9 convolution_bitcast_fusion.18
  688.9 6.7 convolution_bitcast_fusion.16
  704.4 7.8 convolution_bitcast_fusion.17
  712.2 9.6 copy.253
  725.9 6.6 add_add_fusion.13
  732.6 15.4 %add_add_fusion.12 = f32[768,2304]{0,1:T(8,128)} fusion(f32[768,2304]{0,1:T(8,128)} %get-tuple-element.566, f32[768,2304]{0,1:T(8,128)} %get-tuple-element.565, f32[768,2304]{0,1:T(8,128)} %get-tuple-element.564, f32[768,2304]{0,1:T(8,128)} %get-tuple-element.562, f32[768,2304]{0,1:T(8,128)} %get-tuple-element.563), kind=kLoop, calls=%fused_computation.635 | loop fusion | flops 7077888 | bytes 42467328 | tf_op jit(solution)/shard_map/add | solution.py:387
  748.1 20.5 %add_add_fusion.11 = f32[768,3072]{1,0:T(8,128)} fusion(f32[768,3072]{1,0:T(8,128)} %get-tuple-element.1009, f32[768,3072]{1,0:T(8,128)} %get-tuple-element.1008, f32[768,3072]{1,0:T(8,128)} %get-tuple-element.1007, f32[768,3072]{1,0:T(8,128)} %get-tuple-element.1005, f32[768,3072]{1,0:T(8,128)} %get-tuple-element.1006), kind=kLoop, calls=%fused_computation.634 | loop fusion | flops 9437184 | bytes 56623104 | tf_op jit(solution)/shard_map/add | solution.py:387
  768.7 20.5 %add_add_fusion.10 = f32[3072,768]{0,1:T(8,128)} fusion(f32[3072,768]{0,1:T(8,128)} %get-tuple-element.581, f32[3072,768]{0,1:T(8,128)} %get-tuple-element.580, f32[3072,768]{0,1:T(8,128)} %get-tuple-element.579, f32[3072,768]{0,1:T(8,128)} %get-tuple-element.577, f32[3072,768]{0,1:T(8,128)} %get-tuple-element.578), kind=kLoop, calls=%fused_computation.633 | loop fusion | flops 9437184 | bytes 56623104 | tf_op jit(solution)/shard_map/add | solution.py:387
  792.6 242.7 %psum.7 = f32[10,768]{1,0:T(8,128)} all-reduce(f32[10,768]{1,0:T(8,128)S(1)} %select_add_fusion), channel_id=1, replica_groups=mesh['section'=4,'dp'=8] {'section','dp'}, use_global_device_ids=true, to_apply=%region_142.143 | all-reduce | flops 7680 | bytes 61440 | tf_op jit(solution)/shard_map/psum | solution.py:419
  1052.4 47.5 %reduce-scatter.11.cloned.1.call-done = f32[768,288]{0,1:T(8,128)} async-done(((f32[768,2304]{0,1:T(8,128)}), f32[768,288]{0,1:T(8,128)}) %reduce-scatter.11.cloned.1.call-update) | async-done | bytes 884752 | tf_op jit(solution)/shard_map/reduce_scatter | solution.py:424
  1102.5 97.5 %reduce-scatter.15.cloned.1.call-done = f32[768,384]{1,0:T(8,128)} async-done(((f32[768,3072]{1,0:T(8,128)}), f32[768,384]{1,0:T(8,128)}) %reduce-scatter.15.cloned.1.call-update) | async-done | bytes 1179664 | tf_op jit(solution)/shard_map/reduce_scatter | solution.py:426
  1202.6 97.4 %reduce-scatter.17.cloned.1.call-done = f32[3072,96]{0,1:T(8,128)} async-done(((f32[3072,768]{0,1:T(8,128)}), f32[3072,96]{0,1:T(8,128)}) %reduce-scatter.17.cloned.1.call-update) | async-done | bytes 1179664 | tf_op jit(solution)/shard_map/reduce_scatter | solution.py:427
  (520 shorter events, 285.0 us)
Async XLA Ops:
  7.2 1028.2 %reduce-scatter.21.cloned.1.call-start = ((), (), s32[]{:S(2)}) async-start(), calls=%async_computation.11 | async-start | bytes 442368
  7.9 13.8 %collective-permute-start = (bf16[1]{0:T(256)(128)(2,1)}, bf16[1]{0:T(256)(128)(2,1)}, u32[]{:S(2)}, u32[]{:S(2)}) collective-permute-start(bf16[1]{0:T(256)(128)(2,1)} %convert_element_type.553), channel_id=1, source_target_pairs={{0,8},{8,0},{16,24},{24,16},{1,9},{9,1},{17,25},{25,17},{2,10},{10... | collective-permute-start | bytes 14 | tf_op jit(solution)/shard_map/ppermute | solution.py:23
  12.9 30.5 %collective-permute-start.1 = (bf16[768]{0:T(1024)(128)(2,1)S(1)}, bf16[768]{0:T(1024)(128)(2,1)S(1)}, u32[]{:S(2)}, u32[]{:S(2)}) collective-permute-start(bf16[768]{0:T(1024)(128)(2,1)S(1)} %reduce.1), channel_id=1, source_target_pairs={{0,16},{16,0},{8,24},{24,8},{1,17},{17,1},{9,25},{25,9},{2,18},{18... | collective-permute-start | bytes 4616 | tf_op jit(solution)/shard_map/ppermute | solution.py:23
  18.3 157.8 %copy-start.138 = (bf16[10,768]{1,0:T(8,128)(2,1)S(1)}, bf16[10,768]{1,0:T(8,128)(2,1)}, u32[]{:S(2)}) copy-start(bf16[10,768]{1,0:T(8,128)(2,1)} %param.33) | copy-start | bytes 46084
  18.3 156.7 %collective-permute-start.3 = (bf16[1,2,320,768]{3,2,1,0:T(8,128)(2,1)}, bf16[1,2,320,768]{3,2,1,0:T(8,128)(2,1)S(1)}, u32[]{:S(2)}, u32[]{:S(2)}) collective-permute-start(bf16[1,2,320,768]{3,2,1,0:T(8,128)(2,1)} %pad_select_fusion), channel_id=1, source_target_pairs={{0,8},{8,0},{16,24},{24,16},{1,9},{9,1},{17,25},{25,17},{2,10},{10... | collective-permute-start | bytes 2949128 | tf_op jit(solution)/shard_map/ppermute | solution.py:23
  18.3 158.9 %collective-permute-start.4 = (bf16[384,2304]{1,0:T(8,128)(2,1)}, bf16[384,2304]{1,0:T(8,128)(2,1)}, u32[]{:S(2)}, u32[]{:S(2)}) collective-permute-start(bf16[384,2304]{1,0:T(8,128)(2,1)} %bitcast.132), channel_id=1, source_target_pairs={{0,16},{16,0},{8,24},{24,8},{1,17},{17,1},{9,25},{25,9},{2,18},{18... | collective-permute-start | bytes 5308424 | tf_op jit(solution)/shard_map/ppermute | solution.py:23
  18.8 22.1 %collective-permute-start.6 = (bf16[1,2,300]{2,1,0:T(2,128)(2,1)S(1)}, bf16[1,2,300]{2,1,0:T(2,128)(2,1)S(1)}, u32[]{:S(2)}, u32[]{:S(2)}) collective-permute-start(bf16[1,2,300]{2,1,0:T(2,128)(2,1)S(1)} %convert_element_type.564), channel_id=1, source_target_pairs={{0,8},{8,0},{16,24},{24,16},{1,9},{9,1},{17,25},{25,17},{2,10},{10... | collective-permute-start | bytes 3608 | tf_op jit(solution)/shard_map/ppermute | solution.py:23
  21.7 159.1 %collective-permute-start.8 = (bf16[384,3072]{1,0:T(8,128)(2,1)}, bf16[384,3072]{1,0:T(8,128)(2,1)}, u32[]{:S(2)}, u32[]{:S(2)}) collective-permute-start(bf16[384,3072]{1,0:T(8,128)(2,1)} %bitcast.549), channel_id=1, source_target_pairs={{0,16},{16,0},{8,24},{24,8},{1,17},{17,1},{9,25},{25,9},{2,18},{18... | collective-permute-start | bytes 7077896 | tf_op jit(solution)/shard_map/ppermute | solution.py:23
  40.9 147.9 %collective-permute-start.9 = (bf16[1536,768]{1,0:T(8,128)(2,1)}, bf16[1536,768]{1,0:T(8,128)(2,1)}, u32[]{:S(2)}, u32[]{:S(2)}) collective-permute-start(bf16[1536,768]{1,0:T(8,128)(2,1)} %bitcast.551), channel_id=1, source_target_pairs={{0,16},{16,0},{8,24},{24,8},{1,17},{17,1},{9,25},{25,9},{2,18},{18... | collective-permute-start | bytes 7077896 | tf_op jit(solution)/shard_map/ppermute | solution.py:23
  43.4 115.6 %collective-permute-start.5 = (bf16[3840]{0:T(1024)(128)(2,1)S(1)}, bf16[3840]{0:T(1024)(128)(2,1)S(1)}, u32[]{:S(2)}, u32[]{:S(2)}) collective-permute-start(bf16[3840]{0:T(1024)(128)(2,1)S(1)} %reduce.2), channel_id=1, source_target_pairs={{0,16},{16,0},{8,24},{24,8},{1,17},{17,1},{9,25},{25,9},{2,18},{18... | collective-permute-start | bytes 23048 | tf_op jit(solution)/shard_map/ppermute | solution.py:23
  159.0 13.3 %collective-permute-start.7 = (bf16[384,768]{1,0:T(8,128)(2,1)}, bf16[384,768]{1,0:T(8,128)(2,1)S(1)}, u32[]{:S(2)}, u32[]{:S(2)}) collective-permute-start(bf16[384,768]{1,0:T(8,128)(2,1)} %bitcast.134), channel_id=1, source_target_pairs={{0,16},{16,0},{8,24},{24,8},{1,17},{17,1},{9,25},{25,9},{2,18},{18... | collective-permute-start | bytes 1769480 | tf_op jit(solution)/shard_map/ppermute | solution.py:23
  233.1 10.2 collective-permute-start.10
  235.8 60.2 %copy-start.59 = (pred[320,320]{0,1:T(8,128)(4,1)}, pred[320,320]{0,1:T(8,128)(4,1)S(1)}, u32[]{:S(2)}) copy-start(pred[320,320]{0,1:T(8,128)(4,1)S(1)} %get-tuple-element.1248) | copy-start | bytes 307204
  243.3 40.7 %copy-start.156 = (s32[1,2]{1,0:T(1,128)S(1)}, s32[1,2]{1,0:T(1,128)}, u32[]{:S(2)}) copy-start(s32[1,2]{1,0:T(1,128)} %param.42) | copy-start | bytes 28
  283.9 10.9 collective-permute-start.11
  284.0 9.5 collective-permute-start.2
  305.8 40.7 %copy-start.123 = (bf16[1,320,768]{2,1,0:T(8,128)(2,1)}, bf16[1,320,768]{2,1,0:T(8,128)(2,1)S(1)}, u32[]{:S(2)}) copy-start(bf16[1,320,768]{2,1,0:T(8,128)(2,1)S(1)} %get-tuple-element.550) | copy-start | bytes 1474564
  305.8 40.7 %copy-start.16 = (bf16[320,2304]{1,0:T(8,128)(2,1)}, bf16[320,2304]{1,0:T(8,128)(2,1)S(1)}, u32[]{:S(2)}) copy-start(bf16[320,2304]{1,0:T(8,128)(2,1)S(1)} %get-tuple-element.531) | copy-start | bytes 4423684
  305.8 40.7 %copy-start.141 = (f32[12,320,1]{1,0,2:T(8,128)}, f32[12,320,1]{1,0,2:T(8,128)S(1)}, u32[]{:S(2)}) copy-start(f32[12,320,1]{1,0,2:T(8,128)S(1)} %get-tuple-element.532) | copy-start | bytes 46084
  305.8 39.5 %collective-permute-start.12 = (bf16[320,768]{1,0:T(8,128)(2,1)}, bf16[320,768]{1,0:T(8,128)(2,1)S(1)}, u32[]{:S(2)}, u32[]{:S(2)}) collective-permute-start(bf16[320,768]{1,0:T(8,128)(2,1)} %get-tuple-element.506), channel_id=1, source_target_pairs={{0,8},{8,0},{16,24},{24,16},{1,9},{9,1},{17,25},{25,17},{2,10},{10... | collective-permute-start | bytes 1474568 | tf_op jit(solution)/shard_map/ppermute | solution.py:23
  355.5 8.9 collective-permute-start.13
  375.3 38.2 %copy-start.144 = (f32[12,320,1]{1,0,2:T(8,128)S(1)}, f32[12,320,1]{1,0,2:T(8,128)}, u32[]{:S(2)}) copy-start(f32[12,320,1]{1,0,2:T(8,128)} %copy-done.143) | copy-start | bytes 46084
  402.5 8.9 collective-permute-start.14
  436.1 9.1 collective-permute-start.15
  447.0 101.7 %copy-start.1 = (f32[320,768]{1,0:T(8,128)S(1)}, f32[320,768]{1,0:T(8,128)}, u32[]{:S(2)}) copy-start(f32[320,768]{1,0:T(8,128)} %get-tuple-element.540) | copy-start | bytes 2949124
  447.0 101.7 %copy-start.13 = (bf16[320,2304]{1,0:T(8,128)(2,1)S(1)}, bf16[320,2304]{1,0:T(8,128)(2,1)}, u32[]{:S(2)}) copy-start(bf16[320,2304]{1,0:T(8,128)(2,1)} %copy-done.12) | copy-start | bytes 4423684
  447.0 101.7 %copy-start.140 = (f32[12,320,1]{1,0,2:T(8,128)S(1)}, f32[12,320,1]{1,0,2:T(8,128)}, u32[]{:S(2)}) copy-start(f32[12,320,1]{1,0,2:T(8,128)} %copy-done.139) | copy-start | bytes 46084
  468.9 78.9 %copy-start.83 = (bf16[320,768]{1,0:T(8,128)(2,1)}, bf16[320,768]{1,0:T(8,128)(2,1)S(1)}, u32[]{:S(2)}) copy-start(bf16[320,768]{1,0:T(8,128)(2,1)S(1)} %get-tuple-element.537) | copy-start | bytes 1474564
  468.9 79.8 %copy-start.152 = (f32[1536]{0:T(1024)}, f32[1536]{0:T(1024)S(1)}, u32[]{:S(2)}) copy-start(f32[1536]{0:T(1024)S(1)} %get-tuple-element.589) | copy-start | bytes 18436
  469.0 78.9 %collective-permute-start.16 = (bf16[320,768]{1,0:T(8,128)(2,1)S(1)}, bf16[320,768]{1,0:T(8,128)(2,1)S(1)}, u32[]{:S(2)}, u32[]{:S(2)}) collective-permute-start(bf16[320,768]{1,0:T(8,128)(2,1)S(1)} %get-tuple-element.537), channel_id=1, source_target_pairs={{0,8},{8,0},{16,24},{24,16},{1,9},{9,1},{17,25},{25,17},{2,10},{10... | collective-permute-start | bytes 1474568 | tf_op jit(solution)/shard_map/ppermute | solution.py:23
  548.8 87.9 %copy-start.146 = (f32[12,320,1]{1,0,2:T(8,128)S(1)}, f32[12,320,1]{1,0,2:T(8,128)}, u32[]{:S(2)}) copy-start(f32[12,320,1]{1,0,2:T(8,128)} %copy-done.145) | copy-start | bytes 46084
  627.0 9.5 collective-permute-start.18
  636.6 85.4 %copy-start.149 = (f32[1536]{0:T(1024)S(1)}, f32[1536]{0:T(1024)}, u32[]{:S(2)}) copy-start(f32[1536]{0:T(1024)} %copy-done.148) | copy-start | bytes 18436
  636.6 85.4 %copy-start.151 = (f32[1536]{0:T(1024)S(1)}, f32[1536]{0:T(1024)}, u32[]{:S(2)}) copy-start(f32[1536]{0:T(1024)} %copy-done.150) | copy-start | bytes 18436
  636.7 85.4 %copy-start.153 = (f32[1536]{0:T(1024)S(1)}, f32[1536]{0:T(1024)}, u32[]{:S(2)}) copy-start(f32[1536]{0:T(1024)} %copy-done.152) | copy-start | bytes 18436
  723.0 317.6 %reduce-scatter.19.cloned.1.call-start = ((), (), s32[]{:S(2)}) async-start(), calls=%async_computation.10 | async-start | bytes 2211840
  725.9 320.1 %reduce-scatter.13.cloned.1.call-start = ((), (), s32[]{:S(2)}) async-start(), calls=%async_computation.7 | async-start | bytes 2654208 | tf_op jit(solution)/shard_map/reduce_scatter | solution.py:425
  732.6 367.4 %reduce-scatter.11.cloned.1.call-start = ((), (), s32[]{:S(2)}) async-start(), calls=%async_computation.6 | async-start | bytes 7962624 | tf_op jit(solution)/shard_map/reduce_scatter | solution.py:424
  748.0 452.0 %reduce-scatter.15.cloned.1.call-start = ((), (), s32[]{:S(2)}) async-start(), calls=%async_computation.8 | async-start | bytes 10616832 | tf_op jit(solution)/shard_map/reduce_scatter | solution.py:426
  768.6 531.4 %reduce-scatter.17.cloned.1.call-start = ((), (), s32[]{:S(2)}) async-start(), calls=%async_computation.9 | async-start | bytes 10616832 | tf_op jit(solution)/shard_map/reduce_scatter | solution.py:427
  789.2 259.9 %copy-start.124 = (bf16[1,320,768]{2,1,0:T(8,128)(2,1)S(1)}, bf16[1,320,768]{2,1,0:T(8,128)(2,1)}, u32[]{:S(2)}) copy-start(bf16[1,320,768]{2,1,0:T(8,128)(2,1)} %copy-done.123) | copy-start | bytes 1474564
  791.7 257.4 %collective-permute-start.17 = (bf16[1,2,320,768]{3,2,1,0:T(8,128)(2,1)S(1)}, bf16[1,2,320,768]{3,2,1,0:T(8,128)(2,1)S(1)}, u32[]{:S(2)}, u32[]{:S(2)}) collective-permute-start(bf16[1,2,320,768]{3,2,1,0:T(8,128)(2,1)S(1)} %maximum_select_fusion.4), channel_id=1, source_target_pairs={{0,8},{8,0},{16,24},{24,16},{1,9},{9,1},{17,25},{25,17},{2,10},{10... | collective-permute-start | bytes 2949128 | tf_op jit(solution)/shard_map/ppermute | solution.py:23
  1036.3 3.8 collective-permute-start.24
  1041.8 3.6 collective-permute-start.23
  1047.0 4.7 collective-permute-start.20
  1101.0 201.7 %collective-permute-start.19 = (bf16[384,288]{0,1:T(8,128)(2,1)S(1)}, bf16[384,288]{0,1:T(8,128)(2,1)S(1)}, u32[]{:S(2)}, u32[]{:S(2)}) collective-permute-start(bf16[384,288]{0,1:T(8,128)(2,1)S(1)} %dynamic-slice_convert_fusion.2), channel_id=1, source_target_pairs={{0,16},{16,0},{8,24},{24,8},{1,17},{17,1},{9,25},{25,9},{2,18},{18... | collective-permute-start | bytes 663560 | tf_op jit(solution)/shard_map/ppermute | solution.py:23
  1201.1 103.4 %collective-permute-start.21 = (bf16[384,384]{1,0:T(8,128)(2,1)S(1)}, bf16[384,384]{1,0:T(8,128)(2,1)S(1)}, u32[]{:S(2)}, u32[]{:S(2)}) collective-permute-start(bf16[384,384]{1,0:T(8,128)(2,1)S(1)} %dynamic-slice_convert_fusion.1), channel_id=1, source_target_pairs={{0,16},{16,0},{8,24},{24,8},{1,17},{17,1},{9,25},{25,9},{2,18},{18... | collective-permute-start | bytes 884744 | tf_op jit(solution)/shard_map/ppermute | solution.py:23
  1301.2 6.8 collective-permute-start.22
  (87 other events, 761.7 us)
Sparse Core Ops, SparseCore 0:
  723.2 224.9 reduce-scatter.20
  950.6 33.6 reduce-scatter.18
  986.5 34.6 reduce-scatter.12
  1023.4 76.5 reduce-scatter.10
  1102.1 97.8 reduce-scatter.14
  1202.2 97.8 reduce-scatter.16
where the time goes:
time: 1330 us; the launch traced here: 1320 us
  waiting for transfers between devices  444 us (33%)
  blocking collectives  243 us (18%)
  local copies, waits for them, and re-layouts  151 us (11%)
  other arithmetic  150 us (11%)
  matrix products  146 us (11%)
  starting transfers between devices  134 us (10%)
  loops' own time  28.7 us (2%)
  between operations  20.4 us (2%)
    psum x1, blocking collectives, per_device(): memory_grad = lax.psum(init_grad, ('section', 'dp'))  243 us
    ppermute x25, waiting for transfers between devices, partner(): return lax.ppermute(block, axis, route)  202 us
    ppermute x25, starting transfers between devices, partner(): return lax.ppermute(block, axis, route)  134 us
    reduce_scatter x1, waiting for transfers between devices, per_device(): lax.psum_scatter(grad_up, 'dp', scatter_dimension=1, tiled=True)  97.5 us
    reduce_scatter x1, waiting for transfers between devices, per_device(): lax.psum_scatter(grad_down, 'dp', scatter_dimension=1, tiled=True)  97.4 us
    another operation x57, local copies, waits for them, and re-layouts  75.4 us
    add x6, other arithmetic, per_device(): totals = jax.tree.map(jnp.add, totals, grads)  63.8 us
    reduce_scatter x1, waiting for transfers between devices, per_device(): lax.psum_scatter(grad_mix, 'dp', scatter_dimension=1, tiled=True)  47.5 us
  transfers between devices with their start and end apart: 31, of which 17 were waited for; matrix products, arithmetic and copies ran while one was open for 9% of the time, Pallas kernels for 0%

commit v1 on v0

v1 whole, which is shorter than its diff:
```python
from functools import partial

import jax
import jax.numpy as jnp
from jax import lax
from jax.sharding import PartitionSpec as P

HEADS = 12
HEAD_DIM = 64


EPS = 1e-05
MASKED = -1e30


def norm_rows(values, scale_vec, shift_vec):
    centre = jnp.mean(values, axis=-1, keepdims=True)
    offset = values - centre
    spread = jnp.mean(offset * offset, axis=-1, keepdims=True)
    return offset * lax.rsqrt(spread + EPS) * scale_vec + shift_vec


def exact_gelu(values):
    return jax.nn.gelu(values, approximate=False)


def split_vector(vector, width, hidden):
    vector = vector.astype(jnp.float32)
    bounds_list = [
        0,
        width,
        2 * width,
        3 * width,
        4 * width,
        4 * width + hidden,
        5 * width + hidden,
        6 * width + hidden,
    ]
    return [vector[bounds_list[number] : bounds_list[number + 1]] for number in range(7)]


def doc_allowed(bounds, mem_rows):
    numbers = jnp.cumsum(bounds, axis=-1)
    filler = jnp.full(bounds.shape[:-1] + (mem_rows,), -1, jnp.int32)
    labels = jnp.concatenate([filler, numbers, filler], axis=-1)
    row_side = labels[..., :, None]
    col_side = labels[..., None, :]
    return (row_side == col_side) | (row_side < 0) | (col_side < 0)


def split_heads(mixed_b, width):
    rows = mixed_b.shape[0]
    queries = mixed_b[:, :width].reshape(rows, HEADS, HEAD_DIM)
    keys_b = mixed_b[:, width : 2 * width].reshape(rows, HEADS, HEAD_DIM)
    values_b = mixed_b[:, 2 * width :].reshape(rows, HEADS, HEAD_DIM)
    return (queries, keys_b, values_b)


def masked_scores(queries, keys_b, allowed):
    scores = jnp.einsum(
        "qhd,khd->hqk", queries, keys_b, preferred_element_type=jnp.float32
    ) * HEAD_DIM ** (-0.5)
    return jnp.where(allowed[None], scores, MASKED)


def layer_forward(inputs, weights, allowed):
    w_mix, w_proj, w_up, w_down, vector, gain_pair = weights
    rows, width = inputs.shape
    hidden = w_up.shape[1]
    bias_q, bias_v, bias_o, shift_one, bias_in, bias_hid, shift_two = split_vector(
        vector, width, hidden
    )
    gain_pair = gain_pair.astype(jnp.float32)
    mixed = jnp.dot(inputs, w_mix, preferred_element_type=jnp.float32)
    mixed = mixed + jnp.concatenate([bias_q, jnp.zeros_like(bias_q), bias_v])
    mixed_b = mixed.astype(jnp.bfloat16)
    queries, keys_b, values_b = split_heads(mixed_b, width)
    scores = masked_scores(queries, keys_b, allowed)
    peak = jnp.max(scores, axis=-1, keepdims=True)
    expo = jnp.exp(scores - peak)
    totals = jnp.sum(expo, axis=-1, keepdims=True)
    probs_b = (expo / totals).astype(jnp.bfloat16)
    log_total = peak + jnp.log(totals)
    heads_b = (
        jnp.einsum("hqk,khd->qhd", probs_b, values_b, preferred_element_type=jnp.float32)
        .reshape(rows, width)
        .astype(jnp.bfloat16)
    )
    attn = jnp.dot(heads_b, w_proj, preferred_element_type=jnp.float32) + bias_o
    resid = inputs.astype(jnp.float32) + attn
    first = norm_rows(resid, gain_pair[:width], shift_one)
    first_b = first.astype(jnp.bfloat16)
    inner = jnp.dot(first_b, w_up, preferred_element_type=jnp.float32) + bias_in
    active_b = exact_gelu(inner).astype(jnp.bfloat16)
    branch = jnp.dot(active_b, w_down, preferred_element_type=jnp.float32) + bias_hid
    second = first + branch
    output = norm_rows(second, gain_pair[width:], shift_two)
    return (
        output,
        (inputs, mixed_b, log_total, heads_b, resid, first, first_b, inner, active_b, second),
    )


def layer_backward(grad_out, stored, weights, allowed):
    w_mix, w_proj, w_up, w_down, vector, gain_pair = weights
    inputs, mixed_b, log_total, heads_b, resid, first, first_b, inner, active_b, second = stored
    rows, width = inputs.shape
    hidden = w_up.shape[1]
    shift_one, shift_two = [split_vector(vector, width, hidden)[at] for at in (3, 6)]
    gain_pair = gain_pair.astype(jnp.float32)
    gain_one = gain_pair[:width]
    gain_two = gain_pair[width:]
    fl_type = jnp.float32
    bf_type = jnp.bfloat16
    _, pull_two = jax.vjp(norm_rows, second, gain_two, shift_two)
    grad_second, grad_gain_two, grad_shift_two = pull_two(grad_out)
    grad_branch = grad_second.astype(bf_type)
    grad_active = jnp.einsum("rd,fd->rf", grad_branch, w_down, preferred_element_type=fl_type)
    _, pull_gelu = jax.vjp(exact_gelu, inner)
    grad_inner = pull_gelu(grad_active)[0].astype(bf_type)
    grad_first = grad_second + jnp.einsum(
        "rf,df->rd", grad_inner, w_up, preferred_element_type=fl_type
    )
    _, pull_one = jax.vjp(norm_rows, resid, gain_one, shift_one)
    grad_resid, grad_gain_one, grad_shift_one = pull_one(grad_first)
    grad_attn = grad_resid.astype(bf_type)
    grad_heads = jnp.einsum("re,de->rd", grad_attn, w_proj, preferred_element_type=fl_type).astype(
        bf_type
    )
    grad_heads = grad_heads.reshape(rows, HEADS, HEAD_DIM)
    queries, keys_b, values_b = split_heads(mixed_b, width)
    scores = masked_scores(queries, keys_b, allowed)
    probs = jnp.exp(scores - log_total)
    probs_b = probs.astype(bf_type)
    grad_value = jnp.einsum("hqk,qhd->khd", probs_b, grad_heads, preferred_element_type=fl_type)
    grad_probs = jnp.einsum("qhd,khd->hqk", grad_heads, values_b, preferred_element_type=fl_type)
    centre = jnp.sum(probs * grad_probs, axis=-1, keepdims=True)
    grad_scores = (probs * (grad_probs - centre)).astype(bf_type)
    grad_query = jnp.einsum(
        "hqk,khd->qhd", grad_scores, keys_b, preferred_element_type=fl_type
    ) * HEAD_DIM ** (-0.5)
    grad_key = jnp.einsum(
        "hqk,qhd->khd", grad_scores, queries, preferred_element_type=fl_type
    ) * HEAD_DIM ** (-0.5)
    grad_mixed = jnp.concatenate(
        [
            grad_query.reshape(rows, width),
            grad_key.reshape(rows, width),
            grad_value.reshape(rows, width),
        ],
        axis=1,
    ).astype(bf_type)
    grad_inputs = (
        grad_resid + jnp.einsum("re,de->rd", grad_mixed, w_mix, preferred_element_type=fl_type)
    ).astype(bf_type)
    pairs = (
        (inputs, grad_mixed),
        (heads_b, grad_attn),
        (first_b, grad_inner),
        (active_b, grad_branch),
    )
    sums = (grad_gain_one, grad_gain_two, grad_shift_one, grad_shift_two)
    return (grad_inputs, pairs, sums)


def weight_grads(records):
    fl_type = jnp.float32
    mats = []
    cols = []
    for number in range(4):
        left = jnp.concatenate([pairs[number][0] for pairs, _ in records], axis=0)
        right = jnp.concatenate([pairs[number][1] for pairs, _ in records], axis=0)
        mats.append(jnp.einsum("rd,re->de", left, right, preferred_element_type=fl_type))
        cols.append(jnp.sum(right.astype(fl_type), axis=0))
    gain_one, gain_two, shift_one, shift_two = [
        sum(sums[number] for _, sums in records) for number in range(4)
    ]
    width = cols[1].shape[0]
    vector = jnp.concatenate(
        [
            cols[0][:width],
            cols[0][2 * width :],
            cols[1],
            shift_one,
            cols[2],
            cols[3],
            shift_two,
        ]
    )
    return (*mats, vector, jnp.concatenate([gain_one, gain_two]))


def per_device(
    text_rows,
    memory_init,
    cotangent,
    w_qkv,
    w_out,
    w_in,
    w_hid,
    biases,
    norm_gains,
    boundaries,
    mem_resets,
    seg_counts,
):
    fl_type = jnp.float32
    bf_type = jnp.bfloat16
    items, segs, text_len, width = text_rows.shape
    mem_rows = memory_init.shape[0]
    seg_rows = text_len + 2 * mem_rows
    blocks = [
        lax.all_gather(block[0], "section")
        for block in (w_qkv, w_out, w_in, w_hid, biases, norm_gains)
    ]
    layers = [
        tuple(jnp.concatenate([block[at], block[2 + at]], axis=0) for block in blocks)
        for at in range(2)
    ]
    allowed = doc_allowed(boundaries, mem_rows)
    live = jnp.arange(segs)[None] < seg_counts[:, None]
    fresh = (jnp.arange(segs)[None] == 0) | (mem_resets > 0)
    stored = {}
    tops = {}
    for item in range(items):
        memory = memory_init
        for seg in range(segs):
            mem_now = jnp.where(fresh[item, seg], memory_init, memory)
            rows_now = jnp.concatenate([mem_now, text_rows[item, seg], mem_now], axis=0)
            for at in range(2):
                result, stored[item, seg, at] = layer_forward(
                    rows_now, layers[at], allowed[item, seg]
                )
                rows_now = result.astype(bf_type)
            tops[item, seg] = jnp.where(live[item, seg], rows_now, 0)
            memory = rows_now[seg_rows - mem_rows :]
    records = {0: [], 1: []}
    input_grads = {}
    memory_grad = jnp.zeros((mem_rows, width), fl_type)
    for item in range(items):
        carried = jnp.zeros((mem_rows, width), fl_type)
        for seg in reversed(range(segs)):
            grad_now = jnp.where(live[item, seg], cotangent[item, seg].astype(fl_type), 0.0)
            grad_now = jnp.concatenate(
                [grad_now[: seg_rows - mem_rows], grad_now[seg_rows - mem_rows :] + carried],
                axis=0,
            ).astype(bf_type)
            for at in (1, 0):
                grad_now, pairs, sums = layer_backward(
                    grad_now.astype(fl_type), stored[item, seg, at], layers[at], allowed[item, seg]
                )
                records[at].append((pairs, sums))
            input_grads[item, seg] = grad_now
            folded = grad_now[:mem_rows].astype(fl_type) + grad_now[
                seg_rows - mem_rows :
            ].astype(fl_type)
            folded = folded.astype(bf_type).astype(fl_type)
            memory_grad = memory_grad + jnp.where(fresh[item, seg], folded, 0.0)
            carried = jnp.where(fresh[item, seg], 0.0, folded)

    def stacked(table):
        return jnp.stack(
            [jnp.stack([table[item, seg] for seg in range(segs)]) for item in range(items)]
        )

    totals = [weight_grads(records[at]) for at in range(2)]

    def reduce_blocks(one, two):
        halves = jnp.stack([one, two])
        halves = halves.reshape(2, 2, -1, halves.shape[-1])
        ordered = halves.transpose(1, 0, 2, 3).reshape(4, -1, halves.shape[-1]).astype(bf_type)
        mine = lax.psum_scatter(ordered, "section", scatter_dimension=0, tiled=True)
        return lax.psum_scatter(mine, "dp", scatter_dimension=2, tiled=True).astype(fl_type)

    reduced = [reduce_blocks(totals[0][number], totals[1][number]) for number in range(4)]
    vector = [totals[at][4].reshape(2, -1) for at in range(2)]
    gain = [totals[at][5].reshape(2, -1) for at in range(2)]
    small = [reduce_blocks(*vector)[:, 0], reduce_blocks(*gain)[:, 0]]
    return (
        stacked(tops),
        stacked(input_grads),
        lax.psum(memory_grad, ("section", "dp")),
        *reduced,
        *small,
    )


def solution(mesh):
    in_specs = (
        P(("section", "dp"), None, None, None),
        P(),
        P(("section", "dp"), None, None, None),
        P("section", None, None),
        P("section", None, None),
        P("section", None, None),
        P("section", None, None),
        P("section", None),
        P("section", None),
        P(("section", "dp"), None, None),
        P(("section", "dp"), None),
        P(("section", "dp")),
    )
    out_specs = (
        P(("section", "dp"), None, None, None),
        P(("section", "dp"), None, None, None),
        P(),
        P("section", None, "dp"),
        P("section", None, "dp"),
        P("section", None, "dp"),
        P("section", None, "dp"),
        P("section", "dp"),
        P("section", "dp"),
    )
    return jax.shard_map(
        per_device, mesh=mesh, in_specs=in_specs, out_specs=out_specs, check_vma=False
    )
```

time: 1330 us -> 1110 us (0.83)
  blocking collectives: 243 us -> 74.3 us
  starting transfers between devices: 134 us -> 1.19 us
  waiting for transfers between devices: 444 us -> 552 us
  matrix products: 146 us -> 239 us
  other arithmetic: 150 us -> 79.7 us
  loops' own time: 28.7 us -> 0 us
    all_gather x0 -> x4, waiting for transfers between devices: none -> 246 us  [per_device(): lax.all_gather(block[0], 'section')]
    unnamed x8 -> x21, waiting for transfers between devices: 0.1 us -> 209 us
    psum x1, blocking collectives: 243 us -> 40.3 us  [per_device(): lax.psum(memory_grad, ('section', 'dp'))]
    ppermute x25 -> x0, waiting for transfers between devices: 202 us -> none  [partner(): return lax.ppermute(block, axis, route)]
    reduce_scatter x4 -> x3, waiting for transfers between devices: 242 us -> 97.7 us  [reduce_blocks(): lax.psum_scatter(mine, 'dp', scatter_dimension=2, tiled=True)]
    ppermute x25 -> x0, starting transfers between devices: 134 us -> none  [partner(): return lax.ppermute(block, axis, route)]
    another operation x60 -> x10, local copies, waits for them, and re-layouts: 76.3 us -> 0.2 us
    add x10 -> x1, other arithmetic: 67.2 us -> 2.08 us  [per_device(): memory_grad = memory_grad + jnp.where(fresh[item, seg], folded, 0.0)]
  transfers between devices with their start and end apart: 31 -> 14, of which waited for: 17 -> 11; matrix products, arithmetic and copies ran while one was open for 9% -> 21% of each run, Pallas kernels for 0% -> 0%
where the time goes in v1:
time: 1110 us; the launch traced here: 1100 us
  waiting for transfers between devices  552 us (50%)
  matrix products  239 us (22%)
  local copies, waits for them, and re-layouts  138 us (12%)
  other arithmetic  79.7 us (7%)
  blocking collectives  74.3 us (7%)
  between operations  18.7 us (2%)
    all_gather x4, waiting for transfers between devices, per_device(): lax.all_gather(block[0], 'section')  246 us
    unnamed x21, waiting for transfers between devices  209 us
    reduce_scatter x3, waiting for transfers between devices, reduce_blocks(): lax.psum_scatter(mine, 'dp', scatter_dimension=2, tiled=True)  97.7 us
    dot_general x8, matrix products, weight_grads(): jnp.einsum('rd,re->de', left, right, preferred_element_type=fl_type)  66.8 us
    unnamed x573, local copies, waits for them, and re-layouts  51.6 us
    dot_general x4, matrix products, layer_forward(): inner = jnp.dot(first_b, w_up, preferred_element_type=jnp.float32) + bias_in  48.3 us
    psum x1, blocking collectives, per_device(): lax.psum(memory_grad, ('section', 'dp'))  40.3 us
    dot_general x4, matrix products, layer_backward(): jnp.einsum('rd,fd->rf', grad_branch, w_down, preferred_element_type=fl_type)  36 us
  transfers between devices with their start and end apart: 14, of which 11 were waited for; matrix products, arithmetic and copies ran while one was open for 21% of the time, Pallas kernels for 0%

profile of v1, /device:TPU:0, one launch (start us, length us, event | category | flops | bytes accessed | tf_op | source)
XLA Modules:
  0.0 1103.5 jit_solution(1535905569928696138)
XLA Ops:
  10.1 9.7 all-gather
  23.0 8.2 all-gather.1
  42.2 8.0 all-gather.9.cloned.1.call-done
  53.0 75.7 %all-gather.7.cloned.1.call-done = bf16[4,384,2304]{2,1,0:T(8,128)(2,1)} async-done(((bf16[1,384,2304]{2,1,0:T(8,128)(2,1)}), bf16[4,384,2304]{2,1,0:T(8,128)(2,1)}) %all-gather.7.cloned.1.call-update) | async-done | bytes 7077904 | tf_op jit(solution)/shard_map/all_gather | solution.py:213
  128.7 5.3 slice_bitcast_fusion.9
  143.8 83.2 %all-gather.11.cloned.1.call-done = bf16[4,384,3072]{2,1,0:T(8,128)(2,1)} async-done(((bf16[1,384,3072]{2,1,0:T(8,128)(2,1)}), bf16[4,384,3072]{2,1,0:T(8,128)(2,1)}) %all-gather.11.cloned.1.call-update) | async-done | bytes 9437200 | tf_op jit(solution)/shard_map/all_gather | solution.py:213
  227.0 5.8 slice_bitcast_fusion.3
  234.1 11.9 %multiply_convert_fusion.7 = (bf16[320,3072]{1,0:T(8,128)(2,1)}, f32[320,3072]{1,0:T(8,128)}, f32[320,3072]{1,0:T(8,128)}) fusion(f32[3072]{0:T(1024)S(1)} %copy-done.216, bf16[320,768]{1,0:T(8,128)(2,1)S(1)} %copy-done.132, bf16[384,3072]{1,0:T(8,128)(2,1)S(1)} %get-tuple-element.92, bf16[384,3072]{1,0:T(8,128)(2,1)S(1)} %get-tuple-element.93), kind=kOutput, calls=%fused_computation.120 | convolution fusion | flops 1584267264 | bytes 15052800 | tf_op jit(solution)/shard_map/dot_general | solution.py:93
  246.0 79.1 %all-gather.13.cloned.1.call-done = bf16[4,1536,768]{2,1,0:T(8,128)(2,1)} async-done(((bf16[1,1536,768]{2,1,0:T(8,128)(2,1)}), bf16[4,1536,768]{2,1,0:T(8,128)(2,1)}) %all-gather.13.cloned.1.call-update) | async-done | bytes 9437200 | tf_op jit(solution)/shard_map/all_gather | solution.py:213
  325.0 5.9 slice_bitcast_fusion.1
  349.0 12.3 %multiply_convert_fusion.6 = (bf16[320,3072]{1,0:T(8,128)(2,1)S(1)}, f32[320,3072]{1,0:T(8,128)}, f32[320,3072]{1,0:T(8,128)}) fusion(f32[3072]{0:T(1024)S(1)} %copy-done.214, bf16[320,768]{1,0:T(8,128)(2,1)S(1)} %fusion.168, bf16[384,3072]{1,0:T(8,128)(2,1)S(1)} %copy-done.51, bf16[384,3072]{1,0:T(8,128)(2,1)S(1)} %copy-done.48), kind=kOutput, calls=%fused_computation.107 | convolution fusion | flops 1584267264 | bytes 15052800 | tf_op jit(solution)/shard_map/dot_general | solution.py:93
  379.6 11.9 %multiply_convert_fusion.5 = (bf16[320,3072]{1,0:T(8,128)(2,1)S(1)}, f32[320,3072]{1,0:T(8,128)}, f32[320,3072]{1,0:T(8,128)}) fusion(f32[3072]{0:T(1024)S(1)} %copy-done.217, bf16[320,768]{1,0:T(8,128)(2,1)S(1)} %fusion.169, bf16[384,3072]{1,0:T(8,128)(2,1)S(1)} %get-tuple-element.92, bf16[384,3072]{1,0:T(8,128)(2,1)S(1)} %copy-done.37), kind=kOutput, calls=%fused_computation.94 | convolution fusion | flops 1584267264 | bytes 15052800 | tf_op jit(solution)/shard_map/dot_general | solution.py:93
  406.5 12.2 %multiply_convert_fusion.4 = (bf16[320,3072]{1,0:T(8,128)(2,1)S(1)}, f32[320,3072]{1,0:T(8,128)S(1)}, f32[320,3072]{1,0:T(8,128)}) fusion(f32[3072]{0:T(1024)S(1)} %copy-done.215, bf16[320,768]{1,0:T(8,128)(2,1)S(1)} %fusion.170, bf16[384,3072]{1,0:T(8,128)(2,1)S(1)} %copy-done.52, bf16[384,3072]{1,0:T(8,128)(2,1)S(1)} %copy-done.49), kind=kOutput, calls=%fused_computation.81 | convolution fusion | flops 1584267264 | bytes 15052800 | tf_op jit(solution)/shard_map/dot_general | solution.py:93
  425.8 8.9 fusion.252
  443.7 4.0 fusion.102
  447.8 4.3 multiply_reduce_fusion.3
  460.2 9.3 fusion.254
  475.0 3.9 fusion.105
  478.9 4.3 multiply_reduce_fusion.2
  493.6 9.2 fusion.253
  507.1 3.9 fusion.108
  511.0 4.3 multiply_reduce_fusion.1
  524.4 8.7 fusion.255
  543.9 9.6 concatenate.169
  553.9 4.3 multiply_reduce_fusion
  564.3 17.9 %convolution_convert_fusion.4 = bf16[768,2304]{1,0:T(8,128)(2,1)S(1)} fusion(bf16[320,768]{0,1:T(8,128)(2,1)S(1)} %bitcast.360, bf16[320,768]{0,1:T(8,128)(2,1)S(1)} %bitcast.363, bf16[320,768]{0,1:T(8,128)(2,1)S(1)} %bitcast.366, bf16[320,768]{0,1:T(8,128)(2,1)S(1)} %bitcast.332, bf16[320,768]{0,1:T(8,128)(2,1)S(1)} %bitcast.335, ...), kind=kOutput, calls=%fused_computation.39 | convolution fusion | flops 2286354432 | bytes 7471104 | tf_op jit(solution)/shard_map/rd,re->de/dot_general | solution.py:173
  582.3 18.1 %convolution_convert_fusion.5 = bf16[768,2304]{1,0:T(8,128)(2,1)S(1)} fusion(bf16[640,768]{1,0:T(8,128)(2,1)S(1)} %copy-done.116, bf16[320,768]{0,1:T(8,128)(2,1)S(1)} %bitcast.349, bf16[320,768]{0,1:T(8,128)(2,1)S(1)} %bitcast.343, bf16[320,768]{0,1:T(8,128)(2,1)S(1)} %bitcast.346, bf16[320,768]{0,1:T(8,128)(2,1)S(1)} %bitcast.341, ...), kind=kOutput, calls=%fused_computation.40 | convolution fusion | flops 2284388352 | bytes 7471104 | tf_op jit(solution)/shard_map/rd,re->de/dot_general | solution.py:173
  603.8 10.3 copy.188
  614.3 8.6 convolution_convert_fusion.2
  623.0 5.6 convolution_convert_fusion.3
  628.6 8.6 maximum_bitcast_fusion
  637.2 8.7 copy.190
  646.2 8.7 convolution_convert_fusion
  655.0 5.6 convolution_convert_fusion.1
  660.6 9.1 maximum_bitcast_fusion.1
  669.7 12.7 %copy.191 = bf16[2,2,1536,768]{2,3,1,0:T(8,128)(2,1)} copy(bf16[2,2,1536,768]{3,2,0,1:T(8,128)(2,1)} %maximum_bitcast_fusion.1) | data formatting | bytes 18874368 | tf_op jit(solution)/shard_map/convert_element_type | solution.py:271
  691.3 16.2 %all-reduce.7 = (bf16[4,1,3840]{2,0,1:T(4,128)(2,1)S(1)}, bf16[4,1,768]{2,0,1:T(4,128)(2,1)S(1)}) all-reduce(bf16[4,1,3840]{2,0,1:T(4,128)(2,1)S(1)} %convert_element_type.479, bf16[4,1,768]{2,0,1:T(4,128)(2,1)S(1)} %convert_element_type.482), channel_id=10, replica_groups=mesh['section'=4,'dp'=8] {'section'}, use_global_device_ids=true, to_apply=%region_71.72.clone | all-reduce | flops 18432 | bytes 73728
  714.0 75.5 %reduce-scatter.43.cloned.1.call-done = bf16[1,384,3072]{2,1,0:T(8,128)(2,1)} async-done(((bf16[4,384,3072]{2,1,0:T(8,128)(2,1)}), bf16[1,384,3072]{2,1,0:T(8,128)(2,1)}) %reduce-scatter.43.cloned.1.call-update) | async-done | bytes 2359312
  789.5 10.8 copy.210
  800.3 4.2 copy.230
  804.5 83.1 %reduce-scatter.45.cloned.1.call-done = bf16[1,1536,768]{1,2,0:T(8,128)(2,1)} async-done(((bf16[4,1536,768]{1,2,0:T(8,128)(2,1)}), bf16[1,1536,768]{1,2,0:T(8,128)(2,1)}) %reduce-scatter.45.cloned.1.call-update) | async-done | bytes 2359312
  887.7 3.9 fusion.121
  894.5 40.3 %psum.7 = f32[10,768]{1,0:T(8,128)} all-reduce(f32[10,768]{1,0:T(8,128)S(1)} %fusion.180), channel_id=1, replica_groups=mesh['section'=4,'dp'=8] {'section','dp'}, use_global_device_ids=true, to_apply=%region_46.47 | all-reduce | flops 7680 | bytes 61440 | tf_op jit(solution)/shard_map/psum | solution.py:282
  942.2 11.3 %reduce-scatter.35.cloned.1.call-done = bf16[480,1]{1,0:T(8,128)(2,1)} async-done(((bf16[3840,1]{1,0:T(8,128)(2,1)}), bf16[480,1]{1,0:T(8,128)(2,1)}) %reduce-scatter.35.cloned.1.call-update) | async-done | bytes 976
  955.8 29.3 %reduce-scatter.29.cloned.1.call-done = bf16[1,384,96]{1,2,0:T(8,128)(2,1)} async-done(((bf16[1,384,768]{1,2,0:T(8,128)(2,1)}), bf16[1,384,96]{1,2,0:T(8,128)(2,1)}) %reduce-scatter.29.cloned.1.call-update) | async-done | bytes 73744 | tf_op jit(solution)/shard_map/reduce_scatter | solution.py:273
  986.6 33.7 %reduce-scatter.27.cloned.1.call-done = bf16[1,384,288]{1,2,0:T(8,128)(2,1)} async-done(((bf16[1,384,2304]{1,2,0:T(8,128)(2,1)}), bf16[1,384,288]{1,2,0:T(8,128)(2,1)}) %reduce-scatter.27.cloned.1.call-update) | async-done | bytes 221200 | tf_op jit(solution)/shard_map/reduce_scatter | solution.py:273
  1022.0 34.9 %reduce-scatter.33.cloned.1.call-done = bf16[384,384]{1,0:T(8,128)(2,1)} async-done(((bf16[3072,384]{1,0:T(8,128)(2,1)}), bf16[384,384]{1,0:T(8,128)(2,1)}) %reduce-scatter.33.cloned.1.call-update) | async-done | bytes 294928
  1059.9 34.7 %reduce-scatter.31.cloned.1.call-done = bf16[1,1536,96]{1,2,0:T(8,128)(2,1)} async-done(((bf16[1,1536,768]{1,2,0:T(8,128)(2,1)}), bf16[1,1536,96]{1,2,0:T(8,128)(2,1)}) %reduce-scatter.31.cloned.1.call-update) | async-done | bytes 294928 | tf_op jit(solution)/shard_map/reduce_scatter | solution.py:273
  (835 shorter events, 189.5 us)
Async XLA Ops:
  7.2 14.7 %copy-start.242 = (s32[1,2,300]{2,1,0:T(2,128)S(1)}, s32[1,2,300]{2,1,0:T(2,128)}, u32[]{:S(2)}) copy-start(s32[1,2,300]{2,1,0:T(2,128)} %param.21) | copy-start | bytes 7204
  7.2 15.8 %copy-start.243 = (bf16[1,768]{1,0:T(2,128)(2,1)S(1)}, bf16[1,768]{1,0:T(2,128)(2,1)}, u32[]{:S(2)}) copy-start(bf16[1,768]{1,0:T(2,128)(2,1)} %param.20) | copy-start | bytes 4612
  7.2 24.7 %copy-start.244 = (s32[1,2]{1,0:T(1,128)S(1)}, s32[1,2]{1,0:T(1,128)}, u32[]{:S(2)}) copy-start(s32[1,2]{1,0:T(1,128)} %param.22) | copy-start | bytes 28
  7.2 43.0 %all-gather.9.cloned.1.call-start = ((), (), s32[]{:S(2)}) async-start(), calls=%async_computation.11 | async-start | bytes 2949120 | tf_op jit(solution)/shard_map/all_gather | solution.py:213
  8.0 28.1 %copy-start.28 = (bf16[1,2,320,768]{3,2,1,0:T(8,128)(2,1)S(1)}, bf16[1,2,320,768]{3,2,1,0:T(8,128)(2,1)}, u32[]{:S(2)}) copy-start(bf16[1,2,320,768]{3,2,1,0:T(8,128)(2,1)} %param.14) | copy-start | bytes 2949124
  8.0 120.8 %all-gather.7.cloned.1.call-start = ((), (), s32[]{:S(2)}) async-start(), calls=%async_computation.10 | async-start | bytes 8847360 | tf_op jit(solution)/shard_map/all_gather | solution.py:213
  8.7 218.2 %all-gather.11.cloned.1.call-start = ((), (), s32[]{:S(2)}) async-start(), calls=%async_computation.12 | async-start | bytes 11796480 | tf_op jit(solution)/shard_map/all_gather | solution.py:213
  9.4 30.4 %copy-start.32 = (bf16[1,2,300,768]{3,1,2,0:T(2,128)(2,1)S(1)}, bf16[1,2,300,768]{3,1,2,0:T(2,128)(2,1)}, u32[]{:S(2)}) copy-start(bf16[1,2,300,768]{3,1,2,0:T(2,128)(2,1)} %param.12) | copy-start | bytes 2764804
  9.5 315.6 %all-gather.13.cloned.1.call-start = ((), (), s32[]{:S(2)}) async-start(), calls=%async_computation.13 | async-start | bytes 11796480 | tf_op jit(solution)/shard_map/all_gather | solution.py:213
  10.0 702.7 %reduce-scatter.41.cloned.1.call-start = ((), (), s32[]{:S(2)}) async-start(), calls=%async_computation.21 | async-start | bytes 2949120
  33.2 330.3 %copy-start.174 = (f32[768]{0:T(1024)}, f32[768]{0:T(1024)S(1)}, u32[]{:S(2)}) copy-start(f32[768]{0:T(1024)S(1)} %get-tuple-element.121) | copy-start | bytes 9220
  33.8 108.9 %copy-start.180 = (f32[768]{0:T(1024)}, f32[768]{0:T(1024)S(1)}, u32[]{:S(2)}) copy-start(f32[768]{0:T(1024)S(1)} %get-tuple-element.128) | copy-start | bytes 9220
  34.4 99.6 %copy-start.220 = (f32[2304]{0:T(1024)}, f32[2304]{0:T(1024)S(1)}, u32[]{:S(2)}) copy-start(f32[2304]{0:T(1024)S(1)} %get-tuple-element.141) | copy-start | bytes 27652
  36.0 100.8 %copy-start.115 = (pred[320,320]{0,1:T(8,128)(4,1)}, pred[320,320]{0,1:T(8,128)(4,1)S(1)}, u32[]{:S(2)}) copy-start(pred[320,320]{0,1:T(8,128)(4,1)S(1)} %get-tuple-element.119) | copy-start | bytes 307204
  42.2 98.9 %copy-start.98 = (bf16[300,768]{1,0:T(8,128)(2,1)}, bf16[300,768]{1,0:T(8,128)(2,1)S(1)}, u32[]{:S(2)}) copy-start(bf16[300,768]{1,0:T(8,128)(2,1)S(1)} %get-tuple-element.201) | copy-start | bytes 1382404
  53.0 88.0 %copy-start.120 = (bf16[384,768]{1,0:T(8,128)(2,1)}, bf16[384,768]{1,0:T(8,128)(2,1)S(1)}, u32[]{:S(2)}) copy-start(bf16[384,768]{1,0:T(8,128)(2,1)S(1)} %get-tuple-element.100) | copy-start | bytes 1769476
  53.0 81.0 %copy-start.156 = (bf16[10,768]{1,0:T(8,128)(2,1)S(1)}, bf16[10,768]{1,0:T(8,128)(2,1)}, u32[]{:S(2)}) copy-start(bf16[10,768]{1,0:T(8,128)(2,1)} %param.13) | copy-start | bytes 46084
  141.8 189.2 %copy-start.8 = (f32[320,768]{1,0:T(8,128)}, f32[320,768]{1,0:T(8,128)S(1)}, u32[]{:S(2)}) copy-start(f32[320,768]{1,0:T(8,128)S(1)} %get-tuple-element.149) | copy-start | bytes 2949124
  141.8 189.2 %copy-start.187 = (f32[320]{0:T(512)}, f32[320]{0:T(512)S(1)}, u32[]{:S(2)}) copy-start(f32[320]{0:T(512)S(1)} %broadcast_multiply_fusion.7) | copy-start | bytes 3844
  142.1 90.7 %copy-start.195 = (f32[320]{0:T(512)}, f32[320]{0:T(512)S(1)}, u32[]{:S(2)}) copy-start(f32[320]{0:T(512)S(1)} %multiply_reduce_fusion.19) | copy-start | bytes 3844
  142.1 188.9 %copy-start.205 = (f32[320]{0:T(512)}, f32[320]{0:T(512)S(1)}, u32[]{:S(2)}) copy-start(f32[320]{0:T(512)S(1)} %fusion.183) | copy-start | bytes 3844
  143.8 90.3 %copy-start.216 = (f32[3072]{0:T(1024)S(1)}, f32[3072]{0:T(1024)}, u32[]{:S(2)}) copy-start(f32[3072]{0:T(1024)} %slice.403) | copy-start | bytes 36868
  232.7 146.5 %copy-start.33 = (bf16[384,3072]{1,0:T(8,128)(2,1)}, bf16[384,3072]{1,0:T(8,128)(2,1)S(1)}, u32[]{:S(2)}) copy-start(bf16[384,3072]{1,0:T(8,128)(2,1)S(1)} %get-tuple-element.92) | copy-start | bytes 7077892
  246.0 85.0 %copy-start.181 = (f32[768]{0:T(1024)S(1)}, f32[768]{0:T(1024)}, u32[]{:S(2)}) copy-start(f32[768]{0:T(1024)} %copy-done.180) | copy-start | bytes 9220
  246.0 85.0 %copy-start.232 = (f32[768]{0:T(1024)S(1)}, f32[768]{0:T(1024)}, u32[]{:S(2)}) copy-start(f32[768]{0:T(1024)} %get-tuple-element.127) | copy-start | bytes 9220
  541.8 171.7 %reduce-scatter.39.cloned.1.call-start = ((), (), s32[]{:S(2)}) async-start(), calls=%async_computation.20 | async-start | bytes 8847360
  561.1 21.1 %copy-start.76 = (bf16[12,64,320]{2,1,0:T(8,128)(2,1)}, bf16[12,64,320]{2,1,0:T(8,128)(2,1)S(1)}, u32[]{:S(2)}) copy-start(bf16[12,64,320]{2,1,0:T(8,128)(2,1)S(1)} %fusion.97) | copy-start | bytes 1474564
  561.7 20.5 %copy-start.79 = (bf16[12,64,320]{2,1,0:T(8,128)(2,1)}, bf16[12,64,320]{2,1,0:T(8,128)(2,1)S(1)}, u32[]{:S(2)}) copy-start(bf16[12,64,320]{2,1,0:T(8,128)(2,1)S(1)} %fusion.96) | copy-start | bytes 1474564
  564.3 18.0 %copy-start.82 = (bf16[12,64,320]{2,1,0:T(8,128)(2,1)}, bf16[12,64,320]{2,1,0:T(8,128)(2,1)S(1)}, u32[]{:S(2)}) copy-start(bf16[12,64,320]{2,1,0:T(8,128)(2,1)S(1)} %fusion.111) | copy-start | bytes 1474564
  564.3 18.0 %copy-start.75 = (bf16[12,64,320]{2,1,0:T(8,128)(2,1)S(1)}, bf16[12,64,320]{2,1,0:T(8,128)(2,1)}, u32[]{:S(2)}) copy-start(bf16[12,64,320]{2,1,0:T(8,128)(2,1)} %copy-done.74) | copy-start | bytes 1474564
  564.3 18.0 %copy-start.85 = (bf16[12,64,320]{2,1,0:T(8,128)(2,1)S(1)}, bf16[12,64,320]{2,1,0:T(8,128)(2,1)}, u32[]{:S(2)}) copy-start(bf16[12,64,320]{2,1,0:T(8,128)(2,1)} %copy-done.84) | copy-start | bytes 1474564
  564.3 18.0 %copy-start.87 = (bf16[12,64,320]{2,1,0:T(8,128)(2,1)S(1)}, bf16[12,64,320]{2,1,0:T(8,128)(2,1)}, u32[]{:S(2)}) copy-start(bf16[12,64,320]{2,1,0:T(8,128)(2,1)} %copy-done.86) | copy-start | bytes 1474564
  564.3 18.0 %copy-start.116 = (bf16[640,768]{1,0:T(8,128)(2,1)S(1)}, bf16[640,768]{1,0:T(8,128)(2,1)}, u32[]{:S(2)}) copy-start(bf16[640,768]{1,0:T(8,128)(2,1)} %concatenate.169) | copy-start | bytes 2949124
  614.1 175.4 %reduce-scatter.43.cloned.1.call-start = ((), (), s32[]{:S(2)}) async-start(), calls=%async_computation.22 | async-start | bytes 11796480
  645.9 241.7 %reduce-scatter.45.cloned.1.call-start = ((), (), s32[]{:S(2)}) async-start(), calls=%async_computation.23 | async-start | bytes 11796480
  682.5 258.0 %reduce-scatter.37.cloned.1.call-start = ((), (), s32[]{:S(2)}) async-start(), calls=%async_computation.19 | async-start | bytes 221184
  709.3 244.2 %reduce-scatter.35.cloned.1.call-start = ((), (), s32[]{:S(2)}) async-start(), calls=%async_computation.18 | async-start | bytes 1105920
  712.6 272.5 %reduce-scatter.29.cloned.1.call-start = ((), (), s32[]{:S(2)}) async-start(), calls=%async_computation.15 | async-start | bytes 663552 | tf_op jit(solution)/shard_map/reduce_scatter | solution.py:273
  713.4 306.9 %reduce-scatter.27.cloned.1.call-start = ((), (), s32[]{:S(2)}) async-start(), calls=%async_computation.14 | async-start | bytes 1990656 | tf_op jit(solution)/shard_map/reduce_scatter | solution.py:273
  713.9 343.0 %reduce-scatter.33.cloned.1.call-start = ((), (), s32[]{:S(2)}) async-start(), calls=%async_computation.17 | async-start | bytes 2654208
  804.5 83.2 %copy-start.78 = (bf16[12,64,320]{2,1,0:T(8,128)(2,1)S(1)}, bf16[12,64,320]{2,1,0:T(8,128)(2,1)}, u32[]{:S(2)}) copy-start(bf16[12,64,320]{2,1,0:T(8,128)(2,1)} %copy-done.76) | copy-start | bytes 1474564
  804.5 83.2 %copy-start.81 = (bf16[12,64,320]{2,1,0:T(8,128)(2,1)S(1)}, bf16[12,64,320]{2,1,0:T(8,128)(2,1)}, u32[]{:S(2)}) copy-start(bf16[12,64,320]{2,1,0:T(8,128)(2,1)} %copy-done.79) | copy-start | bytes 1474564
  804.5 290.2 %reduce-scatter.31.cloned.1.call-start = ((), (), s32[]{:S(2)}) async-start(), calls=%async_computation.16 | async-start | bytes 2654208 | tf_op jit(solution)/shard_map/reduce_scatter | solution.py:273
  887.7 47.1 %copy-start.5 = (f32[320,768]{1,0:T(8,128)S(1)}, f32[320,768]{1,0:T(8,128)}, u32[]{:S(2)}) copy-start(f32[320,768]{1,0:T(8,128)} %copy-done.4) | copy-start | bytes 2949124
  887.7 47.1 %copy-start.171 = (f32[320]{0:T(512)S(1)}, f32[320]{0:T(512)}, u32[]{:S(2)}) copy-start(f32[320]{0:T(512)} %copy-done.170) | copy-start | bytes 3844
  887.7 47.1 %copy-start.175 = (f32[768]{0:T(1024)S(1)}, f32[768]{0:T(1024)}, u32[]{:S(2)}) copy-start(f32[768]{0:T(1024)} %copy-done.174) | copy-start | bytes 9220
  887.7 47.1 %copy-start.186 = (f32[320]{0:T(512)S(1)}, f32[320]{0:T(512)}, u32[]{:S(2)}) copy-start(f32[320]{0:T(512)} %copy-done.185) | copy-start | bytes 3844
  891.6 46.8 %copy-start.118 = (bf16[320,768]{1,0:T(8,128)(2,1)S(1)}, bf16[320,768]{1,0:T(8,128)(2,1)}, u32[]{:S(2)}) copy-start(bf16[320,768]{1,0:T(8,128)(2,1)} %copy-done.117) | copy-start | bytes 1474564
  (240 other events, 1094.3 us)
Sparse Core Ops, SparseCore 0:
  9.9 40.2 all-gather.8
  52.0 76.6 all-gather.6
  130.6 96.3 all-gather.10
  228.7 96.3 all-gather.12
  541.9 37.3 reduce-scatter.40
  614.2 76.7 reduce-scatter.38
  694.1 95.2 reduce-scatter.42
  792.6 95.0 reduce-scatter.44
  890.5 30.3 reduce-scatter.36
  923.1 30.3 reduce-scatter.34
  955.7 29.3 reduce-scatter.28
  987.3 33.0 reduce-scatter.26
  1022.6 34.2 reduce-scatter.32
  1059.1 35.5 reduce-scatter.30

commit v2 on v1

v2 whole, which is shorter than its diff:
```python
import functools

import jax
import jax.numpy as jnp
from jax import lax
from jax.experimental import pallas as pl
from jax.experimental.pallas import tpu as pltpu
from jax.sharding import PartitionSpec as P

HEADS = 12
HEAD_DIM = 64
EPS = 1e-05
MASKED = -1e30
VMEM_BYTES = 63 * 2**20
F32 = jnp.float32
BF16 = jnp.bfloat16


def dot_nn(one, two):
    return jnp.dot(one, two, preferred_element_type=F32)


def dot_nt(one, two):
    return lax.dot_general(one, two, (((1,), (1,)), ((), ())), preferred_element_type=F32)


def dot_tn(one, two):
    return lax.dot_general(one, two, (((0,), (0,)), ((), ())), preferred_element_type=F32)


def weight_tile(pack_ref, kind, tile, width):
    part = width // 4
    if kind == "hid":
        return pack_ref[tile % 2, tile // 2, 0, 8 * part : 8 * part + width, :]
    start = {"qkv": 0, "out": 3, "in": 4}[kind] * part
    at = start + tile * part
    pieces = [pack_ref[core, half, 0, pl.ds(at, part), :] for half in range(2) for core in range(2)]
    return jnp.concatenate(pieces, axis=0)


def head_lanes(shape, head):
    lanes = lax.broadcasted_iota(jnp.int32, shape, 1)
    return (lanes // HEAD_DIM) == head


def erf_parts(values):
    density = jnp.exp(-0.5 * values * values) * 0.3989422804014327
    phi = 0.5 * (1.0 + lax.erf(values * 0.7071067811865476))
    return phi, density


def forward_body(
    first_step, segs, fresh_ref, live_ref, text_ref, init_ref, prev_ref, labels_row_ref,
    labels_col_ref, pack_ref, vector_ref, gain_ref,
    x_ref, mixed_ref, heads_ref, hat_one_ref, first_ref, active_ref, slope_ref, hat_two_ref,
    stats_ref, out_ref, acts_ref,
    y_scr, bias_scr, sum_scr,
):
    step = pl.program_id(0) + first_step
    layer = step % 2
    seg = (step // 2) % segs
    item = step // (2 * segs)
    rows, width = y_scr.shape
    hidden = 4 * width

    @pl.when(pl.program_id(0) == 0)
    def _():
        y_scr[...] = prev_ref[...]

    @pl.when(layer == 0)
    def _():
        fresh = fresh_ref[item * segs + seg] > 0
        text = text_ref[0, 0]
        last = y_scr[rows - 16 : rows, :].astype(F32)
        head_rows = pltpu.roll(last, 10, 0)
        number = lax.broadcasted_iota(jnp.int32, (16, width), 0)
        top = jnp.where(fresh, init_ref[0], head_rows)
        low = jnp.where(fresh, init_ref[1], last)
        x_ref[0] = text
        x_ref[0, 0:16, :] = jnp.where(number < 10, top, text[0:16].astype(F32)).astype(BF16)
        x_ref[0, rows - 16 : rows, :] = jnp.where(
            number >= 6, low, text[rows - 16 : rows].astype(F32)
        ).astype(BF16)

    @pl.when(layer == 1)
    def _():
        x_ref[0] = y_scr[...]

    row_side = labels_row_ref[0, 0]
    col_side = labels_col_ref[0, 0]
    allowed = (row_side == col_side) | (row_side < 0) | (col_side < 0)
    bias_scr[...] = jnp.where(allowed, 0.0, MASKED)

    vector = lambda at, size: vector_ref[0, :, at : at + size]
    inputs = x_ref[0]
    for tile in range(3):
        mixed = dot_nn(inputs, weight_tile(pack_ref, "qkv", tile, width))
        if tile == 0:
            mixed = mixed + vector(0, width)
        if tile == 2:
            mixed = mixed + vector(width, width)
        mixed_ref[0, :, tile * width : (tile + 1) * width] = mixed.astype(BF16)

    group = 4 * HEAD_DIM
    stat_lane = lax.broadcasted_iota(jnp.int32, (rows, 128), 1)
    stats = jnp.zeros((rows, 128), F32)
    for number in range(width // group):
        at = number * group
        queries = mixed_ref[0, :, at : at + group] * BF16(HEAD_DIM**-0.5)
        keys = mixed_ref[0, :, width + at : width + at + group]
        values = mixed_ref[0, :, 2 * width + at : 2 * width + at + group]
        total = jnp.zeros((rows, group), F32)
        for head in range(4):
            mine = head_lanes((rows, group), head)
            scores = dot_nt(jnp.where(mine, queries, 0), keys) + bias_scr[...]
            peak = jnp.max(scores, axis=-1, keepdims=True)
            expo = jnp.exp(scores - peak)
            norm = jnp.sum(expo, axis=-1, keepdims=True)
            probs = (expo * (1.0 / norm)).astype(BF16)
            total = total + dot_nn(probs, jnp.where(mine, values, 0))
            stats = jnp.where(stat_lane == number * 4 + head, peak + jnp.log(norm), stats)
        heads_ref[0, :, at : at + group] = total.astype(BF16)

    attn = dot_nn(heads_ref[0], weight_tile(pack_ref, "out", 0, width)) + vector(2 * width, width)
    resid = inputs.astype(F32) + attn
    offset = resid - jnp.mean(resid, axis=-1, keepdims=True)
    scale = lax.rsqrt(jnp.mean(offset * offset, axis=-1, keepdims=True) + EPS)
    hat = offset * scale
    hat_one_ref[0] = hat.astype(BF16)
    stats = jnp.where(stat_lane == HEADS, scale, stats)
    first = hat * gain_ref[0, :, 0:width] + vector(3 * width, width)
    first_b = first.astype(BF16)
    first_ref[0] = first_b
    sum_scr[...] = first + vector(4 * width + hidden, width)

    def ff_tile(tile, _):
        at = pl.multiple_of(tile * width, width)
        inner = dot_nn(first_b, weight_tile(pack_ref, "in", tile, width))
        inner = inner + vector_ref[0, :, pl.ds(4 * width + at, width)]
        phi, density = erf_parts(inner)
        active = (inner * phi).astype(BF16)
        active_ref[0, :, pl.ds(at, width)] = active
        slope_ref[0, :, pl.ds(at, width)] = (phi + inner * density).astype(BF16)
        sum_scr[...] += dot_nn(active, weight_tile(pack_ref, "hid", tile, width))
        return _

    lax.fori_loop(0, 4, ff_tile, 0)
    second = sum_scr[...]
    offset = second - jnp.mean(second, axis=-1, keepdims=True)
    scale = lax.rsqrt(jnp.mean(offset * offset, axis=-1, keepdims=True) + EPS)
    hat = offset * scale
    hat_two_ref[0] = hat.astype(BF16)
    stats_ref[0] = jnp.where(stat_lane == HEADS + 1, scale, stats)
    result = (hat * gain_ref[0, :, width : 2 * width] + vector(5 * width + hidden, width)).astype(BF16)
    y_scr[...] = result
    out_ref[0] = result

    @pl.when(layer == 1)
    def _():
        live = live_ref[item * segs + seg] > 0
        acts_ref[0, 0] = jnp.where(live, result, 0)


def forward_steps(first_step, count, fresh, live, text, init, prev, labels, pack, vectors, gains):
    items, segs, rows, width = text.shape
    hidden = 4 * width
    at = lambda t: t + first_step
    by_seg = lambda t, *_: (at(t) // (2 * segs), (at(t) // 2) % segs, 0, 0)
    by_layer3 = lambda t, *_: (at(t) % 2, 0, 0)
    by_step = lambda t, *_: (t, 0, 0)
    whole = lambda shape: pl.BlockSpec(shape, lambda t, *_: (0,) * len(shape))
    saved = [
        ((rows, width), BF16),
        ((rows, 3 * width), BF16),
        ((rows, width), BF16),
        ((rows, width), BF16),
        ((rows, width), BF16),
        ((rows, hidden), BF16),
        ((rows, hidden), BF16),
        ((rows, width), BF16),
        ((rows, 128), F32),
        ((rows, width), BF16),
    ]
    labels_row = labels[:, :, :, None]
    labels_col = labels[:, :, None, :]
    grid_spec = pltpu.PrefetchScalarGridSpec(
        num_scalar_prefetch=2,
        grid=(count,),
        in_specs=[
            pl.BlockSpec((1, 1, rows, width), by_seg),
            whole(init.shape),
            whole(prev.shape),
            pl.BlockSpec((1, 1, rows, 1), by_seg),
            pl.BlockSpec((1, 1, 1, rows), by_seg),
            pl.BlockSpec((2, 2, 1) + pack.shape[3:], lambda t, *_: (0, 0, at(t) % 2, 0, 0)),
            pl.BlockSpec((1, 1, vectors.shape[2]), by_layer3),
            pl.BlockSpec((1, 1, gains.shape[2]), by_layer3),
        ],
        out_specs=[pl.BlockSpec((1,) + shape, by_step) for shape, _ in saved]
        + [pl.BlockSpec((1, 1, rows, width), by_seg)],
        scratch_shapes=[
            pltpu.VMEM((rows, width), BF16),
            pltpu.VMEM((rows, rows), F32),
            pltpu.VMEM((rows, width), F32),
        ],
    )
    return pl.pallas_call(
        functools.partial(forward_body, first_step, segs),
        grid_spec=grid_spec,
        out_shape=[jax.ShapeDtypeStruct((count,) + shape, kind) for shape, kind in saved]
        + [jax.ShapeDtypeStruct(text.shape, BF16)],
        compiler_params=pltpu.CompilerParams(vmem_limit_bytes=VMEM_BYTES),
        name="forward_steps",
    )(fresh, live, text, init, prev, labels_row, labels_col, pack, vectors, gains)


def norm_backward(grad, hat, scale, gain):
    scaled = grad * gain
    mean_one = jnp.mean(scaled, axis=-1, keepdims=True)
    mean_two = jnp.mean(scaled * hat, axis=-1, keepdims=True)
    return (scaled - mean_one - hat * mean_two) * scale


def column_sum(values):
    return jnp.sum(values, axis=0, keepdims=True)


def backward_body(
    top_step, segs, fresh_ref, live_ref, cot_ref, prev_ref, carry_in_ref, labels_row_ref,
    labels_col_ref, pack_ref, gain_ref, mixed_ref, heads_ref, hat_one_ref, slope_ref, hat_two_ref,
    stats_ref,
    branch_ref, inner_ref, attn_ref, mix_ref, grad_ref, sums_ref, inputs_ref, init_ref, carry_out_ref,
    g_scr, carry_scr, bias_scr, sum_scr, go_scr,
):
    step = top_step - pl.program_id(0)
    layer = step % 2
    seg = (step // 2) % segs
    item = step // (2 * segs)
    rows, width = g_scr.shape
    hidden = 4 * width

    @pl.when(pl.program_id(0) == 0)
    def _():
        g_scr[...] = prev_ref[...]
        carry_scr[...] = carry_in_ref[...]
        init_ref[...] = jnp.zeros_like(init_ref)

    @pl.when(layer == 1)
    def _():
        live = live_ref[item * segs + seg] > 0
        cot = jnp.where(live, cot_ref[0, 0], 0)
        g_scr[...] = cot
        carried = jnp.where(seg == segs - 1, 0.0, carry_scr[...])
        g_scr[rows - 16 : rows, :] = (cot[rows - 16 : rows].astype(F32) + carried).astype(BF16)

    row_side = labels_row_ref[0, 0]
    col_side = labels_col_ref[0, 0]
    allowed = (row_side == col_side) | (row_side < 0) | (col_side < 0)
    bias_scr[...] = jnp.where(allowed, 0.0, MASKED)

    stats = stats_ref[0]
    scale_one = stats[:, HEADS : HEADS + 1]
    scale_two = stats[:, HEADS + 1 : HEADS + 2]
    grad = g_scr[...].astype(F32)
    hat = hat_two_ref[0].astype(F32)
    gain = gain_ref[0]
    sums_ref[0, :, 0:width] = column_sum(grad * hat)
    sums_ref[0, :, width : 2 * width] = column_sum(grad)
    grad_second = norm_backward(grad, hat, scale_two, gain[:, width : 2 * width])
    branch = grad_second.astype(BF16)
    branch_ref[0] = branch
    sums_ref[0, :, 2 * width : 3 * width] = column_sum(branch.astype(F32))
    sum_scr[...] = grad_second

    def ff_tile(tile, _):
        at = pl.multiple_of(tile * width, width)
        active = dot_nt(branch, weight_tile(pack_ref, "hid", tile, width))
        inner = (active * slope_ref[0, :, pl.ds(at, width)].astype(F32)).astype(BF16)
        inner_ref[0, :, pl.ds(at, width)] = inner
        sums_ref[0, :, pl.ds(8 * width + at, width)] = column_sum(inner.astype(F32))
        sum_scr[...] += dot_nt(inner, weight_tile(pack_ref, "in", tile, width))
        return _

    lax.fori_loop(0, 4, ff_tile, 0)
    grad = sum_scr[...]
    hat = hat_one_ref[0].astype(F32)
    sums_ref[0, :, 3 * width : 4 * width] = column_sum(grad * hat)
    sums_ref[0, :, 4 * width : 5 * width] = column_sum(grad)
    resid = norm_backward(grad, hat, scale_one, gain[:, 0:width])
    sum_scr[...] = resid
    attn = resid.astype(BF16)
    attn_ref[0] = attn
    sums_ref[0, :, 5 * width : 6 * width] = column_sum(attn.astype(F32))
    go = dot_nt(attn, weight_tile(pack_ref, "out", 0, width)).astype(BF16)
    go_scr[...] = go
    product = go.astype(F32) * heads_ref[0].astype(F32)
    high = product.astype(BF16)
    low = (product - high.astype(F32)).astype(BF16)
    picks = (
        lax.broadcasted_iota(jnp.int32, (16, width), 1) // HEAD_DIM
        == lax.broadcasted_iota(jnp.int32, (16, width), 0)
    ).astype(BF16)
    centres = dot_nt(picks, high) + dot_nt(picks, low)
    logs = jnp.transpose(stats)

    group = 4 * HEAD_DIM
    for number in range(width // group):
        at = number * group
        queries = mixed_ref[0, :, at : at + group] * BF16(HEAD_DIM**-0.5)
        keys = mixed_ref[0, :, width + at : width + at + group]
        values = mixed_ref[0, :, 2 * width + at : 2 * width + at + group]
        outs = go_scr[:, at : at + group]
        grad_q = jnp.zeros((rows, group), F32)
        grad_k = jnp.zeros((rows, group), F32)
        grad_v = jnp.zeros((rows, group), F32)
        for head in range(4):
            mine = head_lanes((rows, group), head)
            row = number * 4 + head
            keys_h = jnp.where(mine, keys, 0)
            scores = dot_nt(keys_h, queries) + bias_scr[...]
            probs = jnp.exp(scores - logs[row : row + 1, :])
            grad_p = dot_nt(jnp.where(mine, values, 0), outs)
            grad_s = (probs * (grad_p - centres[row : row + 1, :])).astype(BF16)
            grad_v = grad_v + dot_nn(probs.astype(BF16), jnp.where(mine, outs, 0))
            grad_k = grad_k + dot_nn(grad_s, jnp.where(mine, queries, 0))
            grad_q = grad_q + dot_tn(grad_s, keys_h)
        mix_ref[0, :, at : at + group] = (grad_q * HEAD_DIM**-0.5).astype(BF16)
        mix_ref[0, :, width + at : width + at + group] = grad_k.astype(BF16)
        mix_ref[0, :, 2 * width + at : 2 * width + at + group] = grad_v.astype(BF16)

    sums_ref[0, :, 6 * width : 7 * width] = column_sum(mix_ref[0, :, 0:width].astype(F32))
    sums_ref[0, :, 7 * width : 8 * width] = column_sum(mix_ref[0, :, 2 * width : 3 * width].astype(F32))
    total = sum_scr[...]
    for tile in range(3):
        total = total + dot_nt(
            mix_ref[0, :, tile * width : (tile + 1) * width], weight_tile(pack_ref, "qkv", tile, width)
        )
    result = total.astype(BF16)
    g_scr[...] = result
    grad_ref[...] = result

    @pl.when(layer == 0)
    def _():
        inputs_ref[0, 0] = result
        fresh = fresh_ref[item * segs + seg] > 0
        number = lax.broadcasted_iota(jnp.int32, (16, width), 0)
        folded = result[rows - 16 : rows].astype(F32) + pltpu.roll(result[0:16].astype(F32), 6, 0)
        folded = jnp.where(number >= 6, folded, 0.0).astype(BF16).astype(F32)
        init_ref[...] += jnp.where(fresh, folded, 0.0)
        carry_scr[...] = jnp.where(fresh, 0.0, folded)

    carry_out_ref[...] = carry_scr[...]


def backward_steps(
    top_step, count, fresh, live, cot, prev, carry, labels, pack, gains, saved, inputs_so_far=None
):
    items, segs, rows, width = cot.shape
    hidden = 4 * width
    at = lambda t: top_step - t
    by_seg = lambda t, *_: (at(t) // (2 * segs), (at(t) // 2) % segs, 0, 0)
    by_layer3 = lambda t, *_: (at(t) % 2, 0, 0)
    by_step = lambda t, *_: (count - 1 - t, 0, 0)
    whole = lambda shape: pl.BlockSpec(shape, lambda t, *_: (0,) * len(shape))
    names = ("mixed", "heads", "hat_one", "slope", "hat_two", "stats")
    outs = [
        ((rows, width), BF16),
        ((rows, hidden), BF16),
        ((rows, width), BF16),
        ((rows, 3 * width), BF16),
    ]
    labels_row = labels[:, :, :, None]
    labels_col = labels[:, :, None, :]
    operands = [fresh, live, cot, prev, carry, labels_row, labels_col, pack, gains]
    operands += [saved[name] for name in names]
    in_specs = [
        pl.BlockSpec((1, 1, rows, width), by_seg),
        whole(prev.shape),
        whole(carry.shape),
        pl.BlockSpec((1, 1, rows, 1), by_seg),
        pl.BlockSpec((1, 1, 1, rows), by_seg),
        pl.BlockSpec((2, 2, 1) + pack.shape[3:], lambda t, *_: (0, 0, at(t) % 2, 0, 0)),
        pl.BlockSpec((1, 1, gains.shape[2]), by_layer3),
    ] + [pl.BlockSpec((1,) + saved[name].shape[1:], by_step) for name in names]
    body = functools.partial(backward_body, top_step, segs)
    aliases = {}
    if inputs_so_far is not None:
        operands.append(inputs_so_far)
        in_specs.append(pl.BlockSpec(memory_space=pl.ANY))
        aliases = {len(operands) - 1: len(outs) + 2}
        inner_body = body

        def body(*refs):
            cut = 2 + len(in_specs)
            return inner_body(*refs[: cut - 1], *refs[cut:])

    grid_spec = pltpu.PrefetchScalarGridSpec(
        num_scalar_prefetch=2,
        grid=(count,),
        in_specs=in_specs,
        out_specs=[pl.BlockSpec((1,) + shape, by_step) for shape, _ in outs]
        + [
            whole((rows, width)),
            pl.BlockSpec((1, 1, 12 * width), by_step),
            pl.BlockSpec((1, 1, rows, width), by_seg),
            whole((16, width)),
            whole((16, width)),
        ],
        scratch_shapes=[
            pltpu.VMEM((rows, width), BF16),
            pltpu.VMEM((16, width), F32),
            pltpu.VMEM((rows, rows), F32),
            pltpu.VMEM((rows, width), F32),
            pltpu.VMEM((rows, width), BF16),
        ],
    )
    return pl.pallas_call(
        body,
        grid_spec=grid_spec,
        out_shape=[jax.ShapeDtypeStruct((count,) + shape, kind) for shape, kind in outs]
        + [
            jax.ShapeDtypeStruct((rows, width), BF16),
            jax.ShapeDtypeStruct((count, 1, 12 * width), F32),
            jax.ShapeDtypeStruct(cot.shape, BF16),
            jax.ShapeDtypeStruct((16, width), F32),
            jax.ShapeDtypeStruct((16, width), F32),
        ],
        input_output_aliases=aliases,
        compiler_params=pltpu.CompilerParams(vmem_limit_bytes=VMEM_BYTES),
        name="backward_steps",
    )(*operands)


GRAD_NAMES = ("first", "inner", "active", "branch", "x", "mix", "heads", "attn")


def weight_grad_body(
    layer, segs_all, dp, *refs,
):
    sources = refs[:8]
    extra_ref, mine_ref, theirs_ref = refs[8:11]
    held = refs[11:19]
    wire, in_sems, extra_sem, out_sems = refs[19:23]
    core = lax.axis_index("dp") % 2
    rows = sources[0].shape[1]
    width = sources[0].shape[2]
    half = width // 2
    lanes = wire.shape[-1]
    thin = width // dp
    wide = 3 * thin

    def loads(number):
        return [
            pltpu.make_async_copy(
                sources[number].at[2 * at + layer],
                held[number].at[pl.ds(at * rows, rows)],
                in_sems.at[number, at],
            )
            for at in range(segs_all)
        ]

    for number in range(8):
        for copy in loads(number):
            copy.start()
    extra = pltpu.make_async_copy(extra_ref, wire.at[:, :, :, :, pl.ds(half, extra_ref.shape[4])], extra_sem)
    extra.start()

    def ready(*numbers):
        for number in numbers:
            for copy in loads(number):
                copy.wait()

    def stores(kind):
        return [
            pltpu.make_async_copy(wire.at[kind, core], mine_ref.at[kind], out_sems.at[kind, 0]),
            pltpu.make_async_copy(wire.at[kind, 1 - core], theirs_ref.at[kind], out_sems.at[kind, 1]),
        ]

    first, inner, active, branch, inputs, mix, heads, attn = held
    extra.wait()

    ready(0, 1)
    per_tile = width // lanes

    def in_tile(tile, _):
        right = inner[:, pl.ds(pl.multiple_of(tile * width, width), width)]
        for side in range(2):
            result = dot_tn(first[:, side * half : (side + 1) * half], right).astype(BF16)
            for at in range(per_tile):
                wire[1, at % 2, tile * (per_tile // 2) + at // 2, side, 0:half, :] = result[
                    :, at * lanes : (at + 1) * lanes
                ]
        return _

    lax.fori_loop(0, 4, in_tile, 0)
    for copy in stores(1):
        copy.start()

    ready(2, 3)
    def hid_tile(side, _):
        for part in range(4):
            left = active[:, pl.ds(pl.multiple_of(side * 4 * half + part * half, half), half)]
            result = dot_tn(left, branch[...]).astype(BF16)
            for at in range(dp):
                wire[2, at % 2, at // 2, side, 0:half, part * thin : (part + 1) * thin] = result[
                    :, at * thin : (at + 1) * thin
                ]
        return _
    lax.fori_loop(0, 2, hid_tile, 0)
    for copy in stores(2):
        copy.start()

    ready(4, 5, 6, 7)
    for side in range(2):
        left = inputs[:, side * half : (side + 1) * half]
        for tile in range(2):
            result = dot_tn(left, mix[:, tile * 3 * half : (tile + 1) * 3 * half]).astype(BF16)
            for at in range(dp // 2):
                place = tile * (dp // 2) + at
                wire[0, place % 2, place // 2, side, 0:half, 0:wide] = result[
                    :, at * wide : (at + 1) * wide
                ]
        result = dot_tn(heads[:, side * half : (side + 1) * half], attn[...]).astype(BF16)
        for at in range(dp):
            wire[0, at % 2, at // 2, side, 0:half, wide:lanes] = result[:, at * thin : (at + 1) * thin]
    for copy in stores(0):
        copy.start()
    for kind in range(3):
        for copy in stores(kind):
            copy.wait()


def weight_grads(layer, dp, saved, extras):
    sources = [saved[name] for name in GRAD_NAMES]
    steps, rows, width = sources[0].shape
    segs_all = steps // 2
    half = width // 2
    lanes = 4 * width // dp
    extra_rows = extras.shape[4]
    kind = jax.ShapeDtypeStruct((3, dp // 2, 2, half + extra_rows, lanes), BF16)
    any_spec = pl.BlockSpec(memory_space=pl.ANY)
    return pl.pallas_call(
        functools.partial(weight_grad_body, layer, segs_all, dp),
        in_specs=[any_spec] * 9,
        out_specs=[any_spec] * 2,
        out_shape=[kind, kind],
        scratch_shapes=[pltpu.VMEM((segs_all * rows, source.shape[2]), BF16) for source in sources]
        + [
            pltpu.VMEM((3, 2, dp // 2, 2, half + extra_rows, lanes), BF16),
            pltpu.SemaphoreType.DMA((8, segs_all)),
            pltpu.SemaphoreType.DMA,
            pltpu.SemaphoreType.DMA((3, 2)),
        ],
        compiler_params=pltpu.CompilerParams(vmem_limit_bytes=VMEM_BYTES),
        name="weight_grads",
    )(*sources, extras)


SAVED_NAMES = (
    "x", "mixed", "heads", "hat_one", "first", "active", "slope", "hat_two", "stats", "out",
)


def core_groups(dp):
    return [[2 * at, 2 * at + 1] for at in range(dp // 2)]


def other_core(block, dp):
    return lax.ppermute(block, "dp", [(at, at ^ 1) for at in range(dp)])


def pack_blocks(core, w_qkv, w_out, w_in, w_hid, biases, norm_gains):
    half, width = w_out.shape
    part = half // 2

    def own(block):
        size = block.shape[0] // 2
        return lax.dynamic_slice_in_dim(block, core * size, size, 0)

    tiles = []
    for block in (w_qkv, w_out, w_in):
        block = own(block)
        tiles += [block[:, at : at + width] for at in range(0, block.shape[1], width)]
    tiles.append(own(w_hid))
    vector = jnp.concatenate([biases, norm_gains])
    vector = jnp.pad(vector, (0, 16 * width - vector.shape[0])).reshape(16, width)
    return jnp.concatenate(tiles + [vector], axis=0)


def per_device(
    text_rows,
    memory_init,
    cotangent,
    w_qkv,
    w_out,
    w_in,
    w_hid,
    biases,
    norm_gains,
    boundaries,
    mem_resets,
    seg_counts,
):
    items, segs, text_len, width = text_rows.shape
    mem_rows = memory_init.shape[0]
    rows = text_len + 2 * mem_rows
    half = width // 2
    dp = lax.axis_size("dp")
    core = lax.axis_index("dp") % 2
    vector_len = biases.shape[1]

    packed = pack_blocks(core, w_qkv[0], w_out[0], w_in[0], w_hid[0], biases[0], norm_gains[0])
    gathered = lax.all_gather(packed, "section")
    small = gathered[:, -16:].reshape(4, 16 * width).astype(F32)
    pack = lax.all_gather(gathered, "dp", axis_index_groups=core_groups(dp))
    pack = pack.reshape(2, 2, 2, *pack.shape[2:])
    vectors = jnp.concatenate([small[:2, :vector_len], small[2:, :vector_len]], axis=1)[:, None]
    gains = small[:, vector_len : vector_len + width]
    gains = jnp.concatenate([gains[:2], gains[2:]], axis=1)[:, None]

    filler = jnp.full((items, segs, mem_rows), -1, jnp.int32)
    labels = jnp.concatenate([filler, jnp.cumsum(boundaries, axis=-1), filler], axis=-1)
    live = (jnp.arange(segs)[None] < seg_counts[:, None]).astype(jnp.int32).reshape(-1)
    fresh = ((jnp.arange(segs)[None] == 0) | (mem_resets > 0)).astype(jnp.int32).reshape(-1)
    text = jnp.pad(text_rows, ((0, 0), (0, 0), (mem_rows, mem_rows), (0, 0)))
    start = memory_init.astype(F32)
    init = jnp.stack(
        [jnp.pad(start, ((0, 16 - mem_rows), (0, 0))), jnp.pad(start, ((16 - mem_rows, 0), (0, 0)))]
    )

    steps = 2 * items * segs
    blank = jnp.zeros((rows, width), BF16)
    *saved, activations = forward_steps(
        0, steps, fresh, live, text, init, blank, labels, pack, vectors, gains
    )
    saved = dict(zip(SAVED_NAMES, saved))
    branch, inner, attn, mix, _, sums, input_grads, memory_grad, _ = backward_steps(
        steps - 1, steps, fresh, live, cotangent, blank, jnp.zeros((16, width), F32), labels, pack,
        gains, saved,
    )
    saved.update(branch=branch, inner=inner, attn=attn, mix=mix)

    lanes = 4 * width // dp
    memory_part = memory_grad[16 - mem_rows :].reshape(-1)
    memory_len = -(-memory_part.shape[0] // lanes) * lanes
    memory_part = jnp.pad(memory_part, (0, memory_len - memory_part.shape[0]))
    vector_part = vector_len // dp
    gain_part = width // dp
    used = memory_len + vector_part + gain_part
    extra_rows = -(-used // (3 * 16 * lanes)) * 16
    wires = []
    for layer in range(2):
        total = sums.reshape(steps // 2, 2, 12 * width)[:, layer].sum(axis=0)
        gain_two, shift_two, bias_hid, gain_one, shift_one, bias_o, bias_q, bias_v = [
            total[at * width : (at + 1) * width] for at in range(8)
        ]
        vector = jnp.concatenate(
            [bias_q, bias_v, bias_o, shift_one, total[8 * width :], bias_hid, shift_two]
        ).reshape(2, dp, vector_part)
        gain = jnp.stack([gain_one, gain_two]).reshape(2, dp, gain_part)
        extra = jnp.concatenate(
            [jnp.broadcast_to(memory_part, (2, dp, memory_len)), vector, gain], axis=-1
        )
        extra = jnp.pad(extra, ((0, 0), (0, 0), (0, 3 * extra_rows * lanes - used)))
        extra = extra.reshape(2, dp // 2, 2, 3, extra_rows, lanes).transpose(3, 2, 1, 0, 4, 5)
        wires.append(weight_grads(layer, dp, saved, extra.astype(BF16)))
    mine = jnp.stack([wires[0][0], wires[1][0]])
    theirs = other_core(jnp.stack([wires[0][1], wires[1][1]]), dp)
    both = mine.astype(F32) + theirs.astype(F32)
    both = both.transpose(3, 0, 2, 1, 4, 5).astype(BF16)
    both = both.reshape(4, dp // 2, 3, half + extra_rows, lanes)
    own = lax.psum_scatter(both, "section", scatter_dimension=0, tiled=True)[0]
    groups = [[2 * at + side for at in range(dp // 2)] for side in range(2)]
    own = lax.psum_scatter(
        own, "dp", scatter_dimension=0, axis_index_groups=groups, tiled=True
    )[0].astype(F32)

    thin = width // dp
    wide = 3 * thin
    body = own[:, :half]
    hid = body[2].reshape(half, 4, thin).transpose(1, 0, 2).reshape(4 * half, thin)
    flat = own[:, half:].reshape(-1)
    return (
        activations,
        input_grads,
        flat[: mem_rows * width].reshape(mem_rows, width),
        body[0, :, :wide][None],
        body[0, :, wide:][None],
        body[1][None],
        hid[None],
        flat[memory_len : memory_len + vector_part][None],
        flat[memory_len + vector_part : used][None],
    )


def solution(mesh):
    in_specs = (
        P(("section", "dp"), None, None, None),
        P(),
        P(("section", "dp"), None, None, None),
        P("section", None, None),
        P("section", None, None),
        P("section", None, None),
        P("section", None, None),
        P("section", None),
        P("section", None),
        P(("section", "dp"), None, None),
        P(("section", "dp"), None),
        P(("section", "dp")),
    )
    out_specs = (
        P(("section", "dp"), None, None, None),
        P(("section", "dp"), None, None, None),
        P(),
        P("section", None, "dp"),
        P("section", None, "dp"),
        P("section", None, "dp"),
        P("section", None, "dp"),
        P("section", "dp"),
        P("section", "dp"),
    )
    return jax.shard_map(
        per_device, mesh=mesh, in_specs=in_specs, out_specs=out_specs, check_vma=False
    )
```

time: 1110 us -> 678 us (0.61)
  matrix products: 239 us -> 0 us
  Pallas kernels: 0 us -> 161 us
  waiting for transfers between devices: 552 us -> 424 us
  local copies, waits for them, and re-layouts: 138 us -> 45.8 us
  blocking collectives: 74.3 us -> 0 us
  other arithmetic: 79.7 us -> 23.8 us
    dot_general x64 -> x0, matrix products: 239 us -> none  [the longest x8 66.8 us: weight_grads(): jnp.einsum('rd,re->de', left, right, preferred_element_type=fl_type)]
    pallas_call x0 -> x4, Pallas kernels: none -> 161 us  [the longest x1 64.5 us: backward_steps(): pl.pallas_call(body, grid_spec=grid_spec, out_shape=[jax.ShapeDtypeStruct...]
    unnamed x21 -> x5, waiting for transfers between devices: 209 us -> 140 us
    all_gather x4 -> x2, waiting for transfers between devices: 246 us -> 177 us  [the longest x1 139 us: per_device(): gathered = lax.all_gather(packed, 'section')]
    psum x1 -> x0, blocking collectives: 40.3 us -> none  [per_device(): lax.psum(memory_grad, ('section', 'dp'))]
    unnamed x573 -> x43, local copies, waits for them, and re-layouts: 51.6 us -> 12.1 us
    convert_element_type x12 -> x3, local copies, waits for them, and re-layouts: 37.1 us -> 8.26 us  [the longest x1 6.48 us: per_device(): both = both.transpose(3, 0, 2, 1, 4, 5).astype(BF16)]
    convert_element_type x22 -> x4, other arithmetic: 34.8 us -> 9.38 us  [the longest x1 7.28 us: per_device(): both = both.transpose(3, 0, 2, 1, 4, 5).astype(BF16)]
  transfers between devices with their start and end apart: 14 -> 5, of which waited for: 11 -> 5; matrix products, arithmetic and copies ran while one was open for 21% -> 1% of each run, Pallas kernels for 0% -> 0%
where the time goes in v2:
time: 678 us; the launch traced here: 670 us
  waiting for transfers between devices  424 us (63%)
  Pallas kernels  161 us (24%)
  local copies, waits for them, and re-layouts  45.8 us (7%)
  other arithmetic  23.8 us (4%)
  between operations  15.3 us (2%)
    unnamed x5, waiting for transfers between devices  140 us
    all_gather x1, waiting for transfers between devices, per_device(): gathered = lax.all_gather(packed, 'section')  139 us
    reduce_scatter x1, waiting for transfers between devices, per_device(): lax.psum_scatter(own, 'dp', scatter_dimension=0, axis_index_groups=groups...  85.4 us
    pallas_call x1, Pallas kernels, backward_steps(): pl.pallas_call(body, grid_spec=grid_spec, out_shape=[jax.ShapeDtypeStruct...  64.5 us
    pallas_call x1, Pallas kernels, forward_steps(): pl.pallas_call(functools.partial(forward_body, first_step, segs), grid_sp...  53.1 us
    pallas_call x2, Pallas kernels, weight_grads(): pl.pallas_call(functools.partial(weight_grad_body, layer, segs_all, dp),...  43 us
    all_gather x1, waiting for transfers between devices, per_device(): pack = lax.all_gather(gathered, 'dp', axis_index_groups=core_groups(dp))  38 us
    ppermute x1, waiting for transfers between devices, other_core(): return lax.ppermute(block, 'dp', [(at, at ^ 1) for at in range(dp)])  22 us
  transfers between devices with their start and end apart: 5, of which 5 were waited for; matrix products, arithmetic and copies ran while one was open for 1% of the time, Pallas kernels for 0%

profile of v2, /device:TPU:0, one launch (start us, length us, event | category | flops | bytes accessed | tf_op | source)
XLA Modules:
  0.0 670.3 jit_solution(6981768451419280784)
XLA Ops:
  7.3 1.4 dynamic-slice_bitcast_fusion.1
  8.7 0.7 slice_dynamic-update-slice_fusion.6
  9.4 0.7 slice_dynamic-update-slice_fusion.5
  10.1 0.7 slice_dynamic-update-slice_fusion.4
  11.0 0.8 bitcast_dynamic-update-slice_fusion.1
  11.7 0.8 slice_dynamic-update-slice_fusion.3
  12.5 0.7 slice_dynamic-update-slice_fusion.2
  13.2 0.7 slice_dynamic-update-slice_fusion.1
  13.9 0.7 slice_dynamic-update-slice_fusion
  14.8 2.4 bitcast_dynamic-update-slice_fusion
  17.9 139.2 %all-gather.5.cloned.1.call-done = bf16[9280,768]{1,0:T(8,128)(2,1)} async-done(((bf16[2320,768]{1,0:T(8,128)(2,1)}), bf16[9280,768]{1,0:T(8,128)(2,1)}) %all-gather.5.cloned.1.call-update) | async-done | bytes 14254096 | tf_op jit(solution)/shard_map/all_gather | solution.py:613
  157.8 0.6 reduce-window.6
  159.0 0.9 copy.68.labels_row_ref
  160.7 1.2 pad.28.text_ref
  162.4 0.7 fusion.10.labels_col_ref
  163.1 0.6 pad_maximum_fusion.1.init_ref
  164.3 0.9 convert_bitcast_fusion
  165.4 0.6 broadcast_in_dim.37.gain_ref
  166.0 0.7 copy.69.vector_ref
  166.7 38.0 %all-gather.7.cloned.1.call-done = bf16[8,2320,768]{2,1,0:T(8,128)(2,1)} async-done(((bf16[4,2320,768]{2,1,0:T(8,128)(2,1)}), bf16[8,2320,768]{2,1,0:T(8,128)(2,1)}) %all-gather.7.cloned.1.call-update) | async-done | bytes 28508176 | tf_op jit(solution)/shard_map/all_gather | solution.py:615
  204.7 0.8 broadcast_in_dim.33.prev_ref
  205.5 53.1 %forward_steps.1 = (bf16[4,320,768]{2,1,0:T(8,128)(2,1)}, bf16[4,320,2304]{2,1,0:T(8,128)(2,1)}, bf16[4,320,768]{2,1,0:T(8,128)(2,1)}, bf16[4,320,768]{2,1,0:T(8...) custom-call(s32[2]{0:T(128)} %fusion.4.fresh_ref, ...), custom_call_target="tpu_custom_call" | custom-call | tf_op jit(solution)/shard_map/forward_steps/pallas_call | solution.py:207
  258.7 0.6 broadcast_in_dim.38.carry_in_ref
  259.3 64.5 %backward_steps.1 = (bf16[4,320,768]{2,1,0:T(8,128)(2,1)}, bf16[4,320,3072]{2,1,0:T(8,128)(2,1)}, bf16[4,320,768]{2,1,0:T(8,128)(2,1)}, bf16[4,320,2304]{2,1,0:T...) custom-call(s32[2]{0:T(128)} %fusion.4.fresh_ref, ...), custom_call_target="tpu_custom_call" | custom-call | tf_op jit(solution)/shard_map/backward_steps/pallas_call | solution.py:417
  323.8 1.3 reduce.5
  327.8 0.8 slice.283
  328.9 0.9 copy.86
  330.6 0.9 copy.85
  331.5 21.3 %weight_grads.2 = (bf16[3,4,2,400,384]{4,3,2,1,0:T(8,128)(2,1)}, bf16[3,4,2,400,384]{4,3,2,1,0:T(8,128)(2,1)}) custom-call(bf16[4,320,768]{2,1,0:T(8,128)(2,1)} %get-tuple-element.38.refs_0_, bf16[4,320,3072]{2,1,0:T(8,128)(2,1)} %get-tuple-element.39.refs_1_, bf16[4,320,3072]{2,1,0:T(8,128)(2,1)} %get-tuple-element.40.refs_2_, ...), custom_call_target="tpu_custom_call" | custom-call | tf_op jit(solution)/shard_map/weight_grads/pallas_call | solution.py:542
  352.9 21.6 %weight_grads.3 = (bf16[3,4,2,400,384]{4,3,2,1,0:T(8,128)(2,1)}, bf16[3,4,2,400,384]{4,3,2,1,0:T(8,128)(2,1)}) custom-call(bf16[4,320,768]{2,1,0:T(8,128)(2,1)} %get-tuple-element.38.refs_0_, bf16[4,320,3072]{2,1,0:T(8,128)(2,1)} %get-tuple-element.39.refs_1_, bf16[4,320,3072]{2,1,0:T(8,128)(2,1)} %get-tuple-element.40.refs_2_, ...), custom_call_target="tpu_custom_call" | custom-call | tf_op jit(solution)/shard_map/weight_grads/pallas_call | solution.py:542
  374.5 9.1 %pad_maximum_fusion = bf16[2,3,4,2,400,384]{5,4,3,2,1,0:T(8,128)(2,1)S(1)} fusion(bf16[1,3,4,2,400,384]{5,4,3,2,1,0:T(8,128)(2,1)} %bitcast.75, bf16[1,3,4,2,400,384]{5,4,3,2,1,0:T(8,128)(2,1)} %bitcast.74), kind=kLoop, calls=%fused_computation.2 | loop fusion | flops 7372800 | bytes 29491200 | tf_op jit(solution)/shard_map/stack | solution.py:668
  383.9 22.0 %collective-permute-done = bf16[2,3,4,2,400,384]{5,4,3,2,1,0:T(8,128)(2,1)S(1)} collective-permute-done((bf16[2,3,4,2,400,384]{5,4,3,2,1,0:T(8,128)(2,1)S(1)}, bf16[2,3,4,2,400,384]{5,4,3,2,1,0:T(8,128)(2,1)S(1)}, u32[]{:S(2)}, u32[]{:S(2)}) %collective-permute-start) | collective-permute-done | bytes 14745632 | tf_op jit(solution)/shard_map/ppermute | solution.py:569
  405.9 7.3 %fusion = bf16[2,2,4,3,400,384]{5,4,0,2,3,1:T(8,128)(2,1)S(1)} fusion(bf16[2,3,4,2,400,384]{5,4,3,2,1,0:T(8,128)(2,1)S(1)} %collective-permute-done, bf16[1,3,4,2,400,384]{5,4,3,2,1,0:T(8,128)(2,1)} %bitcast.73, bf16[1,3,4,2,400,384]{5,4,3,2,1,0:T(8,128)(2,1)S(1)} %bitcast.72), kind=kLoop, calls=%fused_computation.1 | loop fusion | flops 36864000 | bytes 44236800 | tf_op jit(solution)/shard_map/convert_element_type | solution.py:670
  413.2 6.5 copy.73
  419.7 139.7 %reduce-scatter.7.cloned.1.call-done = bf16[1,4,3,400,384]{4,3,2,1,0:T(8,128)(2,1)} async-done(((bf16[4,4,3,400,384]{4,3,2,1,0:T(8,128)(2,1)}), bf16[1,4,3,400,384]{4,3,2,1,0:T(8,128)(2,1)}) %reduce-scatter.7.cloned.1.call-update) | async-done | bytes 3686416
  559.5 6.4 copy.74
  565.9 85.4 %reduce-scatter.5.cloned.1.call-done = bf16[1,3,400,384]{2,3,1,0:T(8,128)(2,1)} async-done(((bf16[4,3,400,384]{2,3,1,0:T(8,128)(2,1)}), bf16[1,3,400,384]{2,3,1,0:T(8,128)(2,1)}) %reduce-scatter.5.cloned.1.call-update) | async-done | bytes 921616 | tf_op jit(solution)/shard_map/reduce_scatter | solution.py:674
  651.3 1.6 bitcast_convert_fusion
  652.9 0.9 fusion.5
  653.9 0.8 copy.75
  654.7 0.9 slice.216
  655.6 0.9 reshape.169
  657.7 0.8 slice.259
  658.5 0.7 slice.260
  659.2 1.4 copy.76
  660.6 1.1 broadcast_in_dim_reshape.3
  661.7 1.0 copy.78
  662.7 0.6 slice.258
  (95 shorter events, 8.8 us)
Async XLA Ops:
  7.2 3.7 copy-start.1
  7.2 3.8 copy-start.2
  7.2 149.9 %all-gather.5.cloned.1.call-start = ((), (), s32[]{:S(2)}) async-start(), calls=%async_computation.3 | async-start | bytes 17817600 | tf_op jit(solution)/shard_map/all_gather | solution.py:613
  8.6 6.0 copy-start.4
  8.7 6.1 copy-start.5
  17.8 186.9 %all-gather.7.cloned.1.call-start = ((), (), s32[]{:S(2)}) async-start(), calls=%async_computation.4 | async-start | bytes 42762240 | tf_op jit(solution)/shard_map/all_gather | solution.py:615
  157.1 0.7 copy-start.6
  157.1 2.8 copy-start.3
  157.1 3.5 copy-start
  157.2 6.6 copy-start.7
  157.2 402.3 %reduce-scatter.7.cloned.1.call-start = ((), (), s32[]{:S(2)}) async-start(), calls=%async_computation.5 | async-start | bytes 18432000
  374.5 31.4 %slice-start = ((s8[7372800]{0:T(1024)(128)(4,1)}), s8[4194304]{0:T(1024)(128)(4,1)S(1)}, s32[]{:S(2)}) async-start(s8[7372800]{0:T(1024)(128)(4,1)} %bitcast.70), calls=%async_computation.6 | async-start | bytes 8388608
  374.5 31.4 %slice-start.1 = ((s8[7372800]{0:T(1024)(128)(4,1)}), s8[3178496]{0:T(1024)(128)(4,1)S(1)}, s32[]{:S(2)}) async-start(s8[7372800]{0:T(1024)(128)(4,1)} %bitcast.70), calls=%async_computation.7 | async-start | bytes 6356992
  383.6 22.3 %collective-permute-start = (bf16[2,3,4,2,400,384]{5,4,3,2,1,0:T(8,128)(2,1)S(1)}, bf16[2,3,4,2,400,384]{5,4,3,2,1,0:T(8,128)(2,1)S(1)}, u32[]{:S(2)}, u32[]{:S(2)}) collective-permute-start(bf16[2,3,4,2,400,384]{5,4,3,2,1,0:T(8,128)(2,1)S(1)} %pad_maximum_fusion), channel_id=1, source_target_pairs={{0,1},{1,0},{2,3},{3,2},{4,5},{5,4},{6,7},{7,6},{8,9},{9,8},{10,11... | collective-permute-start | bytes 44236808 | tf_op jit(solution)/shard_map/ppermute | solution.py:569
  419.7 231.6 %reduce-scatter.5.cloned.1.call-start = ((), (), s32[]{:S(2)}) async-start(), calls=%async_computation.2 | async-start | bytes 5898240 | tf_op jit(solution)/shard_map/reduce_scatter | solution.py:674
Sparse Core Ops, SparseCore 0:
  18.0 139.1 all-gather.4
  158.7 45.9 all-gather.6
  419.8 139.6 reduce-scatter.6
  566.0 85.2 reduce-scatter.4

commit v3 on v2

--- a/solution.py
+++ b/solution.py
@@ -556,6 +556,392 @@
     )(*sources, extras)
 
 
+MESH = pl.DeviceIdType.MESH
+
+
+def add_into(ref, other):
+    ref[...] = (ref[...].astype(F32) + other[...].astype(F32)).astype(BF16)
+
+
+def grad_reduce_body(dp, segs_all, *refs):
+    sources = refs[:8]
+    extra_ref = refs[8]
+    qkv_out, out_out, in_out, hid_out, extra_out = refs[9:14]
+    held = refs[14:22]
+    mine, theirs, landed, xp, xq, yq, yp, from_low, from_high = refs[22:31]
+    in_sems, extra_sems, core_sems, free_sem, xp_sems, xq_sems, yq_sems, yp_sems, up_sems, down_sems = refs[31:41]
+    section, place = lax.axis_index("section"), lax.axis_index("dp")
+    x, y = section % 2, section // 2
+    core, z = place % 2, place // 2
+    depth = dp // 2
+    cut = depth // 2
+    rows, width = sources[0].shape[1:]
+    half = width // 2
+    lanes = mine.shape[-1]
+    thin = width // dp
+    wide = 3 * thin
+    x_dev = (y * 2 + 1 - x, place)
+    y_dev = ((1 - y) * 2 + x, place)
+    core_dev = (section, z * 2 + 1 - core)
+    up_dev = (section, (z + 1) % depth * 2 + core)
+    down_dev = (section, (z + depth - 1) % depth * 2 + core)
+    kinds = (1, 2, 0)
+    used = {1: (0, 1), 2: (2, 3), 0: (4, 5, 6, 7)}
+    first, inner, active, branch, inputs, mix, heads, attn = held
+
+    def loads(side, kind):
+        layer = (1 - x) if side == 0 else x
+        return [
+            pltpu.make_async_copy(
+                sources[number].at[2 * at + layer],
+                held[number].at[pl.ds(at * rows, rows)],
+                in_sems.at[number, at],
+            )
+            for number in used[kind]
+            for at in range(segs_all)
+        ]
+
+    for kind in kinds:
+        for copy in loads(0, kind):
+            copy.start()
+
+    barrier = pltpu.get_barrier_semaphore()
+    for device in (x_dev, y_dev, core_dev):
+        pl.semaphore_signal(barrier, inc=1, device_id=device, device_id_type=MESH)
+
+    @pl.when(z < depth - 1)
+    def _():
+        pl.semaphore_signal(barrier, inc=1, device_id=up_dev, device_id_type=MESH)
+
+    @pl.when(z > 0)
+    def _():
+        pl.semaphore_signal(barrier, inc=1, device_id=down_dev, device_id_type=MESH)
+
+    pl.semaphore_wait(barrier, 3 + jnp.where(z > 0, 1, 0) + jnp.where(z < depth - 1, 1, 0))
+
+    def remote(source, target, sems, index, device):
+        return pltpu.make_async_remote_copy(
+            src_ref=source, dst_ref=target, send_sem=sems.at[(0, *index)], recv_sem=sems.at[(1, *index)],
+            device_id=device, device_id_type=MESH,
+        )
+
+    def core_copy(unit):
+        return remote(theirs.at[unit % 2], landed.at[unit % 2], core_sems, (unit,), core_dev)
+
+    def xp_copy(kind):
+        return remote(mine.at[0, kind, pl.ds(0, cut)], xp.at[kind], xp_sems, (kind,), x_dev)
+
+    def yq_copy(side, kind):
+        return remote(
+            mine.at[side, kind, pl.ds(cut, depth - cut), 1 - y], yq.at[side, kind], yq_sems,
+            (side, kind), y_dev,
+        )
+
+    def xq_copy(kind):
+        return remote(mine.at[0, kind, pl.ds(cut, depth - cut), y], xq.at[kind], xq_sems, (kind,), x_dev)
+
+    def yp_copy(kind):
+        return remote(mine.at[1, kind, pl.ds(0, cut), 1 - y], yp.at[kind], yp_sems, (kind,), y_dev)
+
+    def up_copy(kind, at):
+        return remote(mine.at[1, kind, at, y], from_low.at[kind, at], up_sems, (kind, at), up_dev)
+
+    def down_copy(kind, at):
+        return remote(mine.at[1, kind, at, y], from_high.at[kind, at], down_sems, (kind, at), down_dev)
+
+    def multiply(side, kind, unit):
+        slot = unit % 2
+
+        def put(at, block, piece, start, stop):
+            if isinstance(at, int):
+                chunk_core, chunk_z = at % 2, at // 2
+            else:
+                chunk_core, chunk_z = at
+
+            @pl.when(core == chunk_core)
+            def _():
+                mine[side, kind, chunk_z, block, 0:half, start:stop] = piece
+
+            @pl.when(core != chunk_core)
+            def _():
+                theirs[slot, chunk_z, block, 0:half, start:stop] = piece
+
+        if kind == 1:
+            per_tile = width // lanes
+
+            def in_tile(tile, _):
+                right = inner[:, pl.ds(pl.multiple_of(tile * width, width), width)]
+                for block in range(2):
+                    result = dot_tn(first[:, block * half : (block + 1) * half], right).astype(BF16)
+                    for at in range(per_tile):
+                        put(
+                            (at % 2, tile * (per_tile // 2) + at // 2), block,
+                            result[:, at * lanes : (at + 1) * lanes], 0, lanes,
+                        )
+                return _
+
+            lax.fori_loop(0, 4, in_tile, 0)
+        elif kind == 2:
+
+            def hid_tile(block, _):
+                for part in range(4):
+                    left = active[:, pl.ds(pl.multiple_of((block * 4 + part) * half, half), half)]
+                    result = dot_tn(left, branch[...]).astype(BF16)
+                    for at in range(dp):
+                        put(
+                            at, block, result[:, at * thin : (at + 1) * thin], part * thin,
+                            (part + 1) * thin,
+                        )
+                return _
+
+            lax.fori_loop(0, 2, hid_tile, 0)
+        else:
+            for block in range(2):
+                left = inputs[:, block * half : (block + 1) * half]
+                for tile in range(2):
+                    result = dot_tn(left, mix[:, tile * 3 * half : (tile + 1) * 3 * half]).astype(BF16)
+                    for at in range(depth):
+                        put(
+                            tile * depth + at, block, result[:, at * wide : (at + 1) * wide], 0, wide
+                        )
+                result = dot_tn(heads[:, block * half : (block + 1) * half], attn[...]).astype(BF16)
+                for at in range(dp):
+                    put(at, block, result[:, at * thin : (at + 1) * thin], wide, lanes)
+
+    def after_core(side, kind, unit):
+        core_copy(unit).wait_recv()
+
+        def add(at, _):
+            add_into(mine.at[side, kind, at], landed.at[unit % 2, at])
+            return _
+
+        lax.fori_loop(0, depth, add, 0)
+        if unit + 2 < 6:
+            pl.semaphore_signal(free_sem, inc=1, device_id=core_dev, device_id_type=MESH)
+        if side == 0:
+            xp_copy(kind).start()
+        yq_copy(side, kind).start()
+
+    def forward_q(kind):
+        yq_copy(0, kind).wait_recv()
+
+        def add(at, _):
+            add_into(mine.at[0, kind, cut + at, y], yq.at[0, kind, at])
+            return _
+
+        lax.fori_loop(0, depth - cut, add, 0)
+        xq_copy(kind).start()
+
+    def forward_p(kind):
+        xp_copy(kind).wait_recv()
+
+        def add(at, _):
+            add_into(mine.at[1, kind, at], xp.at[kind, at])
+            return _
+
+        lax.fori_loop(0, cut, add, 0)
+        yp_copy(kind).start()
+
+    def finish_plane(kind):
+        yq_copy(1, kind).wait_recv()
+        xq_copy(kind).wait_recv()
+
+        def add_two(at, _):
+            ref = mine.at[1, kind, cut + at, y]
+            total = ref[...].astype(F32) + yq[1, kind, at].astype(F32) + xq[kind, at].astype(F32)
+            ref[...] = total.astype(BF16)
+            return _
+
+        lax.fori_loop(0, depth - cut, add_two, 0)
+        yp_copy(kind).wait_recv()
+
+        def add(at, _):
+            add_into(mine.at[1, kind, at, y], yp.at[kind, at])
+            return _
+
+        lax.fori_loop(0, cut, add, 0)
+
+    def line(kind):
+        def hop(count, _):
+            high, low = depth - 1 - count, count
+
+            @pl.when(z < high)
+            def _():
+                @pl.when(z > 0)
+                def _():
+                    up_copy(kind, high).wait_recv()
+                    add_into(mine.at[1, kind, high, y], from_low.at[kind, high])
+
+                up_copy(kind, high).start()
+
+            @pl.when(z > low)
+            def _():
+                @pl.when(z < depth - 1)
+                def _():
+                    down_copy(kind, low).wait_recv()
+                    add_into(mine.at[1, kind, low, y], from_high.at[kind, low])
+
+                down_copy(kind, low).start()
+
+            return 0
+
+        lax.fori_loop(0, depth - 1, hop, 0)
+
+    def finish(kind):
+        @pl.when(z > 0)
+        def _():
+            up_copy(kind, z).wait_recv()
+            add_into(mine.at[1, kind, z, y], from_low.at[kind, z])
+
+        @pl.when(z < depth - 1)
+        def _():
+            down_copy(kind, z).wait_recv()
+            add_into(mine.at[1, kind, z, y], from_high.at[kind, z])
+
+        total = mine[1, kind, z, y].astype(F32)
+        extra_out[kind] = total[half:, :]
+        if kind == 0:
+            qkv_out[0] = total[:half, 0:wide]
+            out_out[0] = total[:half, wide:lanes]
+        elif kind == 1:
+            in_out[0] = total[:half]
+        else:
+            for part in range(4):
+                hid_out[0, part * half : (part + 1) * half, :] = total[:half, part * thin : (part + 1) * thin]
+
+    units = [(side, kind) for side in range(2) for kind in kinds]
+    for unit, (side, kind) in enumerate(units):
+        layer = (1 - x) if side == 0 else x
+        for copy in loads(side, kind):
+            copy.wait()
+        if unit >= 2:
+            core_copy(unit - 2).wait_send()
+        extra_rows = extra_ref.shape[5]
+        extras = [
+            pltpu.make_async_copy(
+                extra_ref.at[layer, kind, core], mine.at[side, kind, :, :, pl.ds(half, extra_rows)],
+                extra_sems.at[0],
+            ),
+            pltpu.make_async_copy(
+                extra_ref.at[layer, kind, 1 - core], theirs.at[unit % 2, :, :, pl.ds(half, extra_rows)],
+                extra_sems.at[1],
+            ),
+        ]
+        for copy in extras:
+            copy.start()
+        multiply(side, kind, unit)
+        for copy in extras:
+            copy.wait()
+        if unit >= 2:
+            pl.semaphore_wait(free_sem, 1)
+        core_copy(unit).start()
+        if side == 0:
+            for copy in loads(1, kind):
+                copy.start()
+        if unit >= 1:
+            after_core(*units[unit - 1], unit - 1)
+        if unit == 4:
+            forward_q(kinds[0])
+        if unit == 5:
+            forward_q(kinds[1])
+    after_core(*units[5], 5)
+    forward_p(kinds[0])
+    forward_q(kinds[2])
+    forward_p(kinds[1])
+    forward_p(kinds[2])
+    finish_plane(kinds[0])
+    line(kinds[0])
+    finish_plane(kinds[1])
+    line(kinds[1])
+    finish(kinds[0])
+    finish_plane(kinds[2])
+    line(kinds[2])
+    finish(kinds[1])
+    finish(kinds[2])
+    core_copy(4).wait_send()
+    core_copy(5).wait_send()
+    for kind in kinds:
+        xp_copy(kind).wait_send()
+        xq_copy(kind).wait_send()
+        yp_copy(kind).wait_send()
+        for side in range(2):
+            yq_copy(side, kind).wait_send()
+
+        def sent(at, _):
+            @pl.when(at > z)
+            def _():
+                up_copy(kind, at).wait_send()
+
+            @pl.when(at < z)
+            def _():
+                down_copy(kind, at).wait_send()
+
+            return 0
+
+        lax.fori_loop(0, depth, sent, 0)
+
+
+def grad_reduce_shapes(dp, steps, rows, width, extra_rows):
+    half = width // 2
+    lanes = 4 * width // dp
+    depth = dp // 2
+    cut = depth // 2
+    tall = half + extra_rows
+    held = [width, 4 * width, 4 * width, width, width, 3 * width, width, width]
+    return [pltpu.VMEM((steps // 2 * rows, columns), BF16) for columns in held] + [
+        pltpu.VMEM(shape + (tall, lanes), BF16)
+        for shape in (
+            (2, 3, depth, 2), (2, depth, 2), (2, depth, 2), (3, cut, 2), (3, depth - cut),
+            (2, 3, depth - cut), (3, cut), (3, depth), (3, depth),
+        )
+    ]
+
+
+def padded_bytes(shapes):
+    total = 0
+    for shape in shapes:
+        *lead, tall, lanes = shape.shape
+        size = 2 * tall * -(-lanes // 128) * 128
+        for count in lead:
+            size *= count
+        total += size
+    return total
+
+
+def grad_reduce(dp, saved, extras):
+    sources = [saved[name] for name in GRAD_NAMES]
+    steps, rows, width = sources[0].shape
+    segs_all = steps // 2
+    half = width // 2
+    lanes = 4 * width // dp
+    thin = width // dp
+    extra_rows = extras.shape[5]
+    depth = dp // 2
+    any_spec = pl.BlockSpec(memory_space=pl.ANY)
+    dma = pltpu.SemaphoreType.DMA
+    return pl.pallas_call(
+        functools.partial(grad_reduce_body, dp, segs_all),
+        in_specs=[any_spec] * 9,
+        out_specs=[pl.BlockSpec(memory_space=pltpu.VMEM)] * 5,
+        out_shape=[
+            jax.ShapeDtypeStruct(shape, F32)
+            for shape in (
+                (1, half, 3 * thin), (1, half, thin), (1, half, lanes), (1, 4 * half, thin),
+                (3, extra_rows, lanes),
+            )
+        ],
+        scratch_shapes=grad_reduce_shapes(dp, steps, rows, width, extra_rows)
+        + [
+            dma((8, segs_all)), dma((2,)), dma((2, 6)), pltpu.SemaphoreType.REGULAR, dma((2, 3)),
+            dma((2, 3)), dma((2, 2, 3)), dma((2, 3)), dma((2, 3, depth)), dma((2, 3, depth)),
+        ],
+        compiler_params=pltpu.CompilerParams(
+            vmem_limit_bytes=VMEM_BYTES, collective_id=0, has_side_effects=True
+        ),
+        name="grad_reduce",
+    )(*sources, extras)
+
+
 SAVED_NAMES = (
     "x", "mixed", "heads", "hat_one", "first", "active", "slope", "hat_two", "stats", "out",
 )
@@ -648,7 +1034,7 @@
     gain_part = width // dp
     used = memory_len + vector_part + gain_part
     extra_rows = -(-used // (3 * 16 * lanes)) * 16
-    wires = []
+    extras = []
     for layer in range(2):
         total = sums.reshape(steps // 2, 2, 12 * width)[:, layer].sum(axis=0)
         gain_two, shift_two, bias_hid, gain_one, shift_one, bias_o, bias_q, bias_v = [
@@ -663,33 +1049,46 @@
         )
         extra = jnp.pad(extra, ((0, 0), (0, 0), (0, 3 * extra_rows * lanes - used)))
         extra = extra.reshape(2, dp // 2, 2, 3, extra_rows, lanes).transpose(3, 2, 1, 0, 4, 5)
-        wires.append(weight_grads(layer, dp, saved, extra.astype(BF16)))
+        extras.append(extra.astype(BF16))
+    extras = jnp.stack(extras)
+    reduce = grad_reduce
+    if padded_bytes(grad_reduce_shapes(dp, steps, rows, width, extra_rows)) > 60 * 2**20:
+        reduce = grad_reduce_apart
+    *grads, flat = reduce(dp, saved, extras)
+    flat = flat.reshape(-1)
+    return (
+        activations,
+        input_grads,
+        flat[: mem_rows * width].reshape(mem_rows, width),
+        *grads,
+        flat[memory_len : memory_len + vector_part][None],
+        flat[memory_len + vector_part : used][None],
+    )
+
+
+def grad_reduce_apart(dp, saved, extras):
+    wires = [weight_grads(layer, dp, saved, extras[layer]) for layer in range(2)]
     mine = jnp.stack([wires[0][0], wires[1][0]])
     theirs = other_core(jnp.stack([wires[0][1], wires[1][1]]), dp)
     both = mine.astype(F32) + theirs.astype(F32)
     both = both.transpose(3, 0, 2, 1, 4, 5).astype(BF16)
-    both = both.reshape(4, dp // 2, 3, half + extra_rows, lanes)
+    tall, lanes = both.shape[-2:]
+    both = both.reshape(4, dp // 2, 3, tall, lanes)
     own = lax.psum_scatter(both, "section", scatter_dimension=0, tiled=True)[0]
     groups = [[2 * at + side for at in range(dp // 2)] for side in range(2)]
     own = lax.psum_scatter(
         own, "dp", scatter_dimension=0, axis_index_groups=groups, tiled=True
     )[0].astype(F32)
-
-    thin = width // dp
-    wide = 3 * thin
+    half = tall - extras.shape[5]
+    thin = lanes // 4
     body = own[:, :half]
     hid = body[2].reshape(half, 4, thin).transpose(1, 0, 2).reshape(4 * half, thin)
-    flat = own[:, half:].reshape(-1)
     return (
-        activations,
-        input_grads,
-        flat[: mem_rows * width].reshape(mem_rows, width),
-        body[0, :, :wide][None],
-        body[0, :, wide:][None],
+        body[0, :, : 3 * thin][None],
+        body[0, :, 3 * thin :][None],
         body[1][None],
         hid[None],
-        flat[memory_len : memory_len + vector_part][None],
-        flat[memory_len + vector_part : used][None],
+        own[:, half:],
     )
 
 

time: 678 us -> 549 us (0.81)
  waiting for transfers between devices: 424 us -> 177 us
  Pallas kernels: 161 us -> 311 us
  other arithmetic: 23.8 us -> 7.09 us
  local copies, waits for them, and re-layouts: 45.8 us -> 31.3 us
    pallas_call x2 -> x1, Pallas kernels: 43 us -> 193 us  [grad_reduce(): pl.pallas_call(functools.partial(grad_reduce_body, dp, segs_all), in_spec...]
    unnamed x5 -> x2, waiting for transfers between devices: 140 us -> 0.03 us
    reduce_scatter x1 -> x0, waiting for transfers between devices: 85.4 us -> none  [per_device(): lax.psum_scatter(own, 'dp', scatter_dimension=0, axis_index_groups=groups...]
    ppermute x1 -> x0, waiting for transfers between devices: 22 us -> none  [other_core(): return lax.ppermute(block, 'dp', [(at, at ^ 1) for at in range(dp)])]
    convert_element_type x2 -> x0, other arithmetic: 8.87 us -> none  [the longest x1 7.28 us: per_device(): both = both.transpose(3, 0, 2, 1, 4, 5).astype(BF16)]
    convert_element_type x3 -> x2, local copies, waits for them, and re-layouts: 8.26 us -> 0.14 us  [per_device(): extras.append(extra.astype(BF16))]
    another operation x4, other arithmetic: 9.85 us -> 2.04 us  [the longest x1 1.24 us: per_device(): extras = jnp.stack(extras)]
    unnamed x43 -> x44, local copies, waits for them, and re-layouts: 12.1 us -> 17.8 us
  transfers between devices with their start and end apart: 5 -> 2, of which waited for: 5 -> 2; matrix products, arithmetic and copies ran while one was open for 1% -> 2% of each run, Pallas kernels for 0% -> 0%
where the time goes in v3:
time: 549 us; the launch traced here: 542 us
  Pallas kernels  311 us (57%)
  waiting for transfers between devices  177 us (32%)
  local copies, waits for them, and re-layouts  31.3 us (6%)
  between operations  15.2 us (3%)
  other arithmetic  7.09 us (1%)
    pallas_call x1, Pallas kernels, grad_reduce(): pl.pallas_call(functools.partial(grad_reduce_body, dp, segs_all), in_spec...  193 us
    all_gather x1, waiting for transfers between devices, per_device(): gathered = lax.all_gather(packed, 'section')  139 us
    pallas_call x1, Pallas kernels, backward_steps(): pl.pallas_call(body, grid_spec=grid_spec, out_shape=[jax.ShapeDtypeStruct...  64.8 us
    pallas_call x1, Pallas kernels, forward_steps(): pl.pallas_call(functools.partial(forward_body, first_step, segs), grid_sp...  53.1 us
    all_gather x1, waiting for transfers between devices, per_device(): pack = lax.all_gather(gathered, 'dp', axis_index_groups=core_groups(dp))  38 us
    unnamed x44, local copies, waits for them, and re-layouts  17.8 us
  transfers between devices with their start and end apart: 2, of which 2 were waited for; matrix products, arithmetic and copies ran while one was open for 2% of the time, Pallas kernels for 0%

profile of v3, /device:TPU:0, one launch (start us, length us, event | category | flops | bytes accessed | tf_op | source)
XLA Modules:
  0.0 542.1 jit_solution(9036572080056264813)
XLA Ops:
  7.3 1.4 dynamic-slice_bitcast_fusion.1
  8.7 0.7 slice_dynamic-update-slice_fusion.6
  9.4 0.7 slice_dynamic-update-slice_fusion.5
  10.1 0.7 slice_dynamic-update-slice_fusion.4
  10.9 0.7 bitcast_dynamic-update-slice_fusion.1
  11.7 0.8 slice_dynamic-update-slice_fusion.3
  12.4 0.7 slice_dynamic-update-slice_fusion.2
  13.2 0.7 slice_dynamic-update-slice_fusion.1
  13.9 0.8 slice_dynamic-update-slice_fusion
  14.8 2.4 bitcast_dynamic-update-slice_fusion
  17.2 0.6 constant_dynamic-update-slice_fusion
  17.9 139.2 %all-gather.5.cloned.1.call-done = bf16[9280,768]{1,0:T(8,128)(2,1)} async-done(((bf16[2320,768]{1,0:T(8,128)(2,1)}), bf16[9280,768]{1,0:T(8,128)(2,1)}) %all-gather.5.cloned.1.call-update) | async-done | bytes 14254096 | tf_op jit(solution)/shard_map/all_gather | solution.py:999
  157.2 0.6 copy-done.7
  157.8 0.6 reduce-window.6
  158.5 0.2 slice_reduce_fusion.2
  159.0 0.9 copy.42.labels_row_ref
  160.7 1.2 pad.28.text_ref
  161.9 0.5 compare_convert_fusion.live_ref
  162.4 0.7 fusion.8.labels_col_ref
  163.1 0.6 pad_maximum_fusion.1.init_ref
  163.7 0.5 fusion.3.fresh_ref
  164.3 0.9 convert_bitcast_fusion
  165.4 0.6 broadcast_in_dim.37.gain_ref
  166.0 0.7 copy.43.vector_ref
  166.7 38.0 %all-gather.7.cloned.1.call-done = bf16[8,2320,768]{2,1,0:T(8,128)(2,1)} async-done(((bf16[4,2320,768]{2,1,0:T(8,128)(2,1)}), bf16[8,2320,768]{2,1,0:T(8,128)(2,1)}) %all-gather.7.cloned.1.call-update) | async-done | bytes 28508176 | tf_op jit(solution)/shard_map/all_gather | solution.py:1001
  204.7 0.8 broadcast_in_dim.33.prev_ref
  205.5 53.1 %forward_steps.1 = (bf16[4,320,768]{2,1,0:T(8,128)(2,1)}, bf16[4,320,2304]{2,1,0:T(8,128)(2,1)}, bf16[4,320,768]{2,1,0:T(8,128)(2,1)}, bf16[4,320,768]{2,1,0:T(8...) custom-call(s32[2]{0:T(128)} %fusion.3.fresh_ref, ...), custom_call_target="tpu_custom_call" | custom-call | tf_op jit(solution)/shard_map/forward_steps/pallas_call | solution.py:207
  258.6 0.6 broadcast_in_dim.38.carry_in_ref
  259.3 64.8 %backward_steps.1 = (bf16[4,320,768]{2,1,0:T(8,128)(2,1)}, bf16[4,320,3072]{2,1,0:T(8,128)(2,1)}, bf16[4,320,768]{2,1,0:T(8,128)(2,1)}, bf16[4,320,2304]{2,1,0:T...) custom-call(s32[2]{0:T(128)} %fusion.3.fresh_ref, ...), custom_call_target="tpu_custom_call" | custom-call | tf_op jit(solution)/shard_map/backward_steps/pallas_call | solution.py:417
  324.1 1.3 reduce.5
  325.5 0.2 slice_reduce_fusion.1
  326.0 0.2 dynamic-update-slice.6
  326.2 0.3 dynamic-update-slice
  326.5 0.2 dynamic-update-slice.7
  327.3 0.2 dynamic-update-slice.10
  327.5 0.4 dynamic-update-slice.11
  328.0 0.8 slice.253
  330.2 1.2 pad_maximum_fusion.refs_8_
  331.4 193.3 %grad_reduce.1 = (f32[1,384,288]{2,1,0:T(8,128)}, f32[1,384,96]{2,1,0:T(8,128)}, f32[1,384,384]{2,1,0:T(8,128)}, f32[1,1536,96]{2,1,0:T(8,128)}, f32[3,16,384]{2,1,0:T(8,128)}) custom-call(bf16[4,320,768]{2,1,0:T(8,128)(2,1)} %get-tuple-element.39.refs_0_, bf16[4,320,3072]{2,1,0:T(8,128)(2,1)} %get-tuple-element.40.refs_1_, ...), custom_call_target="tpu_custom_call" | custom-call | tf_op jit(solution)/shard_map/grad_reduce/pallas_call | solution.py:922
  524.7 1.0 slice.195
  525.7 0.9 reshape.163
  526.5 0.6 slice.233
  527.1 0.6 slice_bitcast_fusion.1
  527.7 2.2 copy.49
  529.9 2.0 copy.47
  532.0 1.7 copy.48
  533.7 0.6 slice.232
  534.3 0.8 copy.81
  (75 shorter events, 3.4 us)
Async XLA Ops:
  7.2 3.7 copy-start.1
  7.2 3.7 copy-start.3
  7.2 149.9 %all-gather.5.cloned.1.call-start = ((), (), s32[]{:S(2)}) async-start(), calls=%async_computation | async-start | bytes 17817600 | tf_op jit(solution)/shard_map/all_gather | solution.py:999
  8.6 6.0 %copy-start.5 = (bf16[1,3840]{1,0:T(2,128)(2,1)S(1)}, bf16[1,3840]{1,0:T(2,128)(2,1)}, u32[]{:S(2)}) copy-start(bf16[1,3840]{1,0:T(2,128)(2,1)} %param.19) | copy-start | bytes 23044
  8.7 6.1 %copy-start.6 = (bf16[1,768]{1,0:T(2,128)(2,1)S(1)}, bf16[1,768]{1,0:T(2,128)(2,1)}, u32[]{:S(2)}) copy-start(bf16[1,768]{1,0:T(2,128)(2,1)} %param.20) | copy-start | bytes 4612
  17.8 186.9 %all-gather.7.cloned.1.call-start = ((), (), s32[]{:S(2)}) async-start(), calls=%async_computation.1 | async-start | bytes 42762240 | tf_op jit(solution)/shard_map/all_gather | solution.py:1001
  157.1 0.7 copy-start.7
  157.1 2.8 copy-start.4
  157.1 3.5 copy-start
  157.1 6.6 %copy-start.8 = (s32[1,2]{1,0:T(1,128)S(1)}, s32[1,2]{1,0:T(1,128)}, u32[]{:S(2)}) copy-start(s32[1,2]{1,0:T(1,128)} %param.22) | copy-start | bytes 28
  524.7 9.6 %copy-start.2 = (f32[1,384,384]{2,1,0:T(8,128)S(1)}, f32[1,384,384]{2,1,0:T(8,128)}, u32[]{:S(2)}) copy-start(f32[1,384,384]{2,1,0:T(8,128)} %get-tuple-element.116) | copy-start | bytes 1769476
Sparse Core Ops, SparseCore 0:
  18.0 139.1 all-gather.4
  158.7 45.9 all-gather.6

commit v4 on v3

--- a/solution.py
+++ b/solution.py
@@ -14,6 +14,7 @@
 VMEM_BYTES = 63 * 2**20
 F32 = jnp.float32
 BF16 = jnp.bfloat16
+MESH = pl.DeviceIdType.MESH
 
 
 def dot_nn(one, two):
@@ -28,14 +29,32 @@
     return lax.dot_general(one, two, (((0,), (0,)), ((), ())), preferred_element_type=F32)
 
 
-def weight_tile(pack_ref, kind, tile, width):
-    part = width // 4
+def weight_tile(refs, kind, tile, layer):
+    qkv_ref, out_ref, in_ref, hid_ref = refs
+    width = out_ref.shape[-1]
     if kind == "hid":
-        return pack_ref[tile % 2, tile // 2, 0, 8 * part : 8 * part + width, :]
-    start = {"qkv": 0, "out": 3, "in": 4}[kind] * part
-    at = start + tile * part
-    pieces = [pack_ref[core, half, 0, pl.ds(at, part), :] for half in range(2) for core in range(2)]
+        quarters = hid_ref.shape[0] // 2
+        pieces = [
+            hid_ref[(tile % 2) * quarters + at, core, tile // 2, layer]
+            for at in range(quarters)
+            for core in range(2)
+        ]
+    else:
+        ref = {"qkv": qkv_ref, "out": out_ref, "in": in_ref}[kind]
+        at = tile * width if isinstance(tile, int) else pl.multiple_of(tile * width, width)
+        pieces = [ref[core, half, layer, :, pl.ds(at, width)] for half in range(2) for core in range(2)]
     return jnp.concatenate(pieces, axis=0)
+
+
+def weight_specs(shapes, layer_of):
+    specs = []
+    for shape in shapes:
+        lead = len(shape) - 3
+        block = shape[:lead] + (1,) + shape[lead + 1 :]
+        specs.append(
+            pl.BlockSpec(block, lambda t, *_, lead=lead: (0,) * lead + (layer_of(t), 0, 0))
+        )
+    return specs
 
 
 def head_lanes(shape, head):
@@ -49,37 +68,41 @@
     return phi, density
 
 
-def forward_body(
-    first_step, segs, fresh_ref, live_ref, text_ref, init_ref, prev_ref, labels_row_ref,
-    labels_col_ref, pack_ref, vector_ref, gain_ref,
+def vector_rows(vec_ref, layer):
+    low, high = vec_ref[0, layer].astype(F32), vec_ref[1, layer].astype(F32)
+    row = lambda block, at: block[at : at + 1]
+    return dict(
+        bias_q=row(low, 0), bias_v=row(low, 1), bias_o=row(low, 2), shift_one=row(low, 3),
+        bias_hid=row(high, 3), shift_two=row(high, 4), gain_one=row(low, 5), gain_two=row(high, 5),
+    )
+
+
+def norm_forward(values):
+    offset = values - jnp.mean(values, axis=-1, keepdims=True)
+    scale = lax.rsqrt(jnp.mean(offset * offset, axis=-1, keepdims=True) + EPS)
+    return offset * scale, scale
+
+
+def forward_layer(
+    step, layer, at_layer, before_mix, before_out, fresh_ref, live_ref, text_ref, init_ref,
+    labels_row_ref, labels_col_ref, weights, vec_ref,
     x_ref, mixed_ref, heads_ref, hat_one_ref, first_ref, active_ref, slope_ref, hat_two_ref,
-    stats_ref, out_ref, acts_ref,
-    y_scr, bias_scr, sum_scr,
+    stats_ref, acts_ref, y_scr, bias_scr, sum_scr, bias_in_scr,
 ):
-    step = pl.program_id(0) + first_step
-    layer = step % 2
-    seg = (step // 2) % segs
-    item = step // (2 * segs)
     rows, width = y_scr.shape
-    hidden = 4 * width
-
-    @pl.when(pl.program_id(0) == 0)
-    def _():
-        y_scr[...] = prev_ref[...]
 
     @pl.when(layer == 0)
     def _():
-        fresh = fresh_ref[item * segs + seg] > 0
-        text = text_ref[0, 0]
+        fresh = fresh_ref[0] > 0
         last = y_scr[rows - 16 : rows, :].astype(F32)
         head_rows = pltpu.roll(last, 10, 0)
         number = lax.broadcasted_iota(jnp.int32, (16, width), 0)
         top = jnp.where(fresh, init_ref[0], head_rows)
         low = jnp.where(fresh, init_ref[1], last)
-        x_ref[0] = text
-        x_ref[0, 0:16, :] = jnp.where(number < 10, top, text[0:16].astype(F32)).astype(BF16)
+        x_ref[0] = text_ref[0, 0]
+        x_ref[0, 0:16, :] = jnp.where(number < 10, top, text_ref[0, 0, 0:16, :].astype(F32)).astype(BF16)
         x_ref[0, rows - 16 : rows, :] = jnp.where(
-            number >= 6, low, text[rows - 16 : rows].astype(F32)
+            number >= 6, low, text_ref[0, 0, rows - 16 : rows, :].astype(F32)
         ).astype(BF16)
 
     @pl.when(layer == 1)
@@ -91,14 +114,18 @@
     allowed = (row_side == col_side) | (row_side < 0) | (col_side < 0)
     bias_scr[...] = jnp.where(allowed, 0.0, MASKED)
 
-    vector = lambda at, size: vector_ref[0, :, at : at + size]
+    before_mix()
+    vec = vector_rows(vec_ref, at_layer)
+    low, high = vec_ref[0, at_layer].astype(F32), vec_ref[1, at_layer].astype(F32)
+    for part, row in enumerate((low[4:5], high[0:1], high[1:2], high[2:3])):
+        bias_in_scr[part] = row
     inputs = x_ref[0]
     for tile in range(3):
-        mixed = dot_nn(inputs, weight_tile(pack_ref, "qkv", tile, width))
+        mixed = dot_nn(inputs, weight_tile(weights, "qkv", tile, at_layer))
         if tile == 0:
-            mixed = mixed + vector(0, width)
+            mixed = mixed + vec["bias_q"]
         if tile == 2:
-            mixed = mixed + vector(width, width)
+            mixed = mixed + vec["bias_v"]
         mixed_ref[0, :, tile * width : (tile + 1) * width] = mixed.astype(BF16)
 
     group = 4 * HEAD_DIM
@@ -120,98 +147,112 @@
             total = total + dot_nn(probs, jnp.where(mine, values, 0))
             stats = jnp.where(stat_lane == number * 4 + head, peak + jnp.log(norm), stats)
         heads_ref[0, :, at : at + group] = total.astype(BF16)
-
-    attn = dot_nn(heads_ref[0], weight_tile(pack_ref, "out", 0, width)) + vector(2 * width, width)
-    resid = inputs.astype(F32) + attn
-    offset = resid - jnp.mean(resid, axis=-1, keepdims=True)
-    scale = lax.rsqrt(jnp.mean(offset * offset, axis=-1, keepdims=True) + EPS)
-    hat = offset * scale
+    stats_ref[0] = stats
+
+    before_out()
+    attn = dot_nn(heads_ref[0], weight_tile(weights, "out", 0, at_layer)) + vec["bias_o"]
+    hat, scale = norm_forward(x_ref[0].astype(F32) + attn)
     hat_one_ref[0] = hat.astype(BF16)
-    stats = jnp.where(stat_lane == HEADS, scale, stats)
-    first = hat * gain_ref[0, :, 0:width] + vector(3 * width, width)
-    first_b = first.astype(BF16)
-    first_ref[0] = first_b
-    sum_scr[...] = first + vector(4 * width + hidden, width)
+    stats = jnp.where(stat_lane == HEADS, scale, stats_ref[0])
+    first = hat * vec["gain_one"] + vec["shift_one"]
+    first_ref[0] = first.astype(BF16)
+    sum_scr[...] = first + vec["bias_hid"]
 
     def ff_tile(tile, _):
         at = pl.multiple_of(tile * width, width)
-        inner = dot_nn(first_b, weight_tile(pack_ref, "in", tile, width))
-        inner = inner + vector_ref[0, :, pl.ds(4 * width + at, width)]
+        inner = dot_nn(first_ref[0], weight_tile(weights, "in", tile, at_layer)) + bias_in_scr[tile]
         phi, density = erf_parts(inner)
         active = (inner * phi).astype(BF16)
         active_ref[0, :, pl.ds(at, width)] = active
         slope_ref[0, :, pl.ds(at, width)] = (phi + inner * density).astype(BF16)
-        sum_scr[...] += dot_nn(active, weight_tile(pack_ref, "hid", tile, width))
+        sum_scr[...] += dot_nn(active, weight_tile(weights, "hid", tile, at_layer))
         return _
 
     lax.fori_loop(0, 4, ff_tile, 0)
-    second = sum_scr[...]
-    offset = second - jnp.mean(second, axis=-1, keepdims=True)
-    scale = lax.rsqrt(jnp.mean(offset * offset, axis=-1, keepdims=True) + EPS)
-    hat = offset * scale
+    hat, scale = norm_forward(sum_scr[...])
     hat_two_ref[0] = hat.astype(BF16)
     stats_ref[0] = jnp.where(stat_lane == HEADS + 1, scale, stats)
-    result = (hat * gain_ref[0, :, width : 2 * width] + vector(5 * width + hidden, width)).astype(BF16)
+    result = (hat * vec["gain_two"] + vec["shift_two"]).astype(BF16)
     y_scr[...] = result
-    out_ref[0] = result
 
     @pl.when(layer == 1)
     def _():
-        live = live_ref[item * segs + seg] > 0
-        acts_ref[0, 0] = jnp.where(live, result, 0)
-
-
-def forward_steps(first_step, count, fresh, live, text, init, prev, labels, pack, vectors, gains):
+        acts_ref[0, 0] = jnp.where(live_ref[0] > 0, result, 0)
+
+
+def saved_shapes(rows, width):
+    return dict(
+        x=((rows, width), BF16),
+        mixed=((rows, 3 * width), BF16),
+        heads=((rows, width), BF16),
+        hat_one=((rows, width), BF16),
+        first=((rows, width), BF16),
+        active=((rows, 4 * width), BF16),
+        slope=((rows, 4 * width), BF16),
+        hat_two=((rows, width), BF16),
+        stats=((rows, 128), F32),
+    )
+
+
+def forward_io(text, fresh, live, init, labels):
     items, segs, rows, width = text.shape
-    hidden = 4 * width
-    at = lambda t: t + first_step
-    by_seg = lambda t, *_: (at(t) // (2 * segs), (at(t) // 2) % segs, 0, 0)
-    by_layer3 = lambda t, *_: (at(t) % 2, 0, 0)
-    by_step = lambda t, *_: (t, 0, 0)
-    whole = lambda shape: pl.BlockSpec(shape, lambda t, *_: (0,) * len(shape))
-    saved = [
-        ((rows, width), BF16),
-        ((rows, 3 * width), BF16),
-        ((rows, width), BF16),
-        ((rows, width), BF16),
-        ((rows, width), BF16),
-        ((rows, hidden), BF16),
-        ((rows, hidden), BF16),
-        ((rows, width), BF16),
-        ((rows, 128), F32),
-        ((rows, width), BF16),
+    count = 2 * items * segs
+    saved = saved_shapes(rows, width)
+    by_seg = lambda t: (t // (2 * segs), (t // 2) % segs, 0, 0)
+    by_flag = lambda t: (t // 2, 0, 0)
+    operands = [fresh, live, text, init, labels[:, :, :, None], labels[:, :, None, :]]
+    in_specs = [
+        pl.BlockSpec((1, 1, width), by_flag),
+        pl.BlockSpec((1, 1, width), by_flag),
+        pl.BlockSpec((1, 1, rows, width), by_seg),
+        pl.BlockSpec(init.shape, lambda t: (0, 0, 0)),
+        pl.BlockSpec((1, 1, rows, 1), by_seg),
+        pl.BlockSpec((1, 1, 1, rows), by_seg),
     ]
-    labels_row = labels[:, :, :, None]
-    labels_col = labels[:, :, None, :]
-    grid_spec = pltpu.PrefetchScalarGridSpec(
-        num_scalar_prefetch=2,
+    out_specs = [pl.BlockSpec((1,) + shape, lambda t: (t, 0, 0)) for shape, _ in saved.values()]
+    out_specs.append(pl.BlockSpec((1, 1, rows, width), by_seg))
+    out_shape = [jax.ShapeDtypeStruct((count,) + shape, kind) for shape, kind in saved.values()]
+    out_shape.append(jax.ShapeDtypeStruct(text.shape, BF16))
+    scratch = [
+        pltpu.VMEM((rows, width), BF16),
+        pltpu.VMEM((rows, rows), F32),
+        pltpu.VMEM((rows, width), F32),
+        pltpu.VMEM((4, 1, width), F32),
+    ]
+    return count, operands, in_specs, out_specs, out_shape, scratch
+
+
+def nothing():
+    pass
+
+
+def forward_body(*refs):
+    step = pl.program_id(0)
+    y_scr = refs[21]
+
+    @pl.when(step == 0)
+    def _():
+        y_scr[...] = jnp.zeros_like(y_scr)
+
+    forward_layer(step, step % 2, 0, nothing, nothing, *refs[:6], refs[6:10], *refs[10:])
+
+
+def forward_steps(text, fresh, live, init, labels, weights, vec):
+    count, operands, in_specs, out_specs, out_shape, scratch = forward_io(text, fresh, live, init, labels)
+    layer_of = lambda t: t % 2
+    *saved, acts = pl.pallas_call(
+        forward_body,
         grid=(count,),
-        in_specs=[
-            pl.BlockSpec((1, 1, rows, width), by_seg),
-            whole(init.shape),
-            whole(prev.shape),
-            pl.BlockSpec((1, 1, rows, 1), by_seg),
-            pl.BlockSpec((1, 1, 1, rows), by_seg),
-            pl.BlockSpec((2, 2, 1) + pack.shape[3:], lambda t, *_: (0, 0, at(t) % 2, 0, 0)),
-            pl.BlockSpec((1, 1, vectors.shape[2]), by_layer3),
-            pl.BlockSpec((1, 1, gains.shape[2]), by_layer3),
-        ],
-        out_specs=[pl.BlockSpec((1,) + shape, by_step) for shape, _ in saved]
-        + [pl.BlockSpec((1, 1, rows, width), by_seg)],
-        scratch_shapes=[
-            pltpu.VMEM((rows, width), BF16),
-            pltpu.VMEM((rows, rows), F32),
-            pltpu.VMEM((rows, width), F32),
-        ],
-    )
-    return pl.pallas_call(
-        functools.partial(forward_body, first_step, segs),
-        grid_spec=grid_spec,
-        out_shape=[jax.ShapeDtypeStruct((count,) + shape, kind) for shape, kind in saved]
-        + [jax.ShapeDtypeStruct(text.shape, BF16)],
+        in_specs=in_specs
+        + weight_specs([weight.shape for weight in weights], layer_of)
+        + [pl.BlockSpec((2, 1) + vec.shape[2:], lambda t: (0, t % 2, 0, 0))],
+        out_specs=out_specs,
+        out_shape=out_shape,
+        scratch_shapes=scratch,
         compiler_params=pltpu.CompilerParams(vmem_limit_bytes=VMEM_BYTES),
         name="forward_steps",
-    )(fresh, live, text, init, prev, labels_row, labels_col, pack, vectors, gains)
+    )(*operands, *weights, vec)
+    return dict(zip(saved_shapes(*text.shape[2:]), saved)), acts
 
 
 def norm_backward(grad, hat, scale, gain):
@@ -226,29 +267,27 @@
 
 
 def backward_body(
-    top_step, segs, fresh_ref, live_ref, cot_ref, prev_ref, carry_in_ref, labels_row_ref,
-    labels_col_ref, pack_ref, gain_ref, mixed_ref, heads_ref, hat_one_ref, slope_ref, hat_two_ref,
-    stats_ref,
-    branch_ref, inner_ref, attn_ref, mix_ref, grad_ref, sums_ref, inputs_ref, init_ref, carry_out_ref,
+    count, segs, fresh_ref, live_ref, cot_ref, labels_row_ref, labels_col_ref, qkv_ref, w_out_ref,
+    in_ref, hid_ref, vec_ref, mixed_ref, heads_ref, hat_one_ref, slope_ref, hat_two_ref, stats_ref,
+    branch_ref, inner_ref, attn_ref, mix_ref, sums_ref, inputs_ref, init_ref,
     g_scr, carry_scr, bias_scr, sum_scr, go_scr,
 ):
-    step = top_step - pl.program_id(0)
+    step = count - 1 - pl.program_id(0)
     layer = step % 2
     seg = (step // 2) % segs
-    item = step // (2 * segs)
     rows, width = g_scr.shape
-    hidden = 4 * width
+    weights = (qkv_ref, w_out_ref, in_ref, hid_ref)
+    gain_one = vec_ref[0, 0].astype(F32)[5:6]
+    gain_two = vec_ref[1, 0].astype(F32)[5:6]
 
     @pl.when(pl.program_id(0) == 0)
     def _():
-        g_scr[...] = prev_ref[...]
-        carry_scr[...] = carry_in_ref[...]
+        carry_scr[...] = jnp.zeros_like(carry_scr)
         init_ref[...] = jnp.zeros_like(init_ref)
 
     @pl.when(layer == 1)
     def _():
-        live = live_ref[item * segs + seg] > 0
-        cot = jnp.where(live, cot_ref[0, 0], 0)
+        cot = jnp.where(live_ref[0] > 0, cot_ref[0, 0], 0)
         g_scr[...] = cot
         carried = jnp.where(seg == segs - 1, 0.0, carry_scr[...])
         g_scr[rows - 16 : rows, :] = (cot[rows - 16 : rows].astype(F32) + carried).astype(BF16)
@@ -263,10 +302,9 @@
     scale_two = stats[:, HEADS + 1 : HEADS + 2]
     grad = g_scr[...].astype(F32)
     hat = hat_two_ref[0].astype(F32)
-    gain = gain_ref[0]
     sums_ref[0, :, 0:width] = column_sum(grad * hat)
     sums_ref[0, :, width : 2 * width] = column_sum(grad)
-    grad_second = norm_backward(grad, hat, scale_two, gain[:, width : 2 * width])
+    grad_second = norm_backward(grad, hat, scale_two, gain_two)
     branch = grad_second.astype(BF16)
     branch_ref[0] = branch
     sums_ref[0, :, 2 * width : 3 * width] = column_sum(branch.astype(F32))
@@ -274,11 +312,11 @@
 
     def ff_tile(tile, _):
         at = pl.multiple_of(tile * width, width)
-        active = dot_nt(branch, weight_tile(pack_ref, "hid", tile, width))
+        active = dot_nt(branch, weight_tile(weights, "hid", tile, 0))
         inner = (active * slope_ref[0, :, pl.ds(at, width)].astype(F32)).astype(BF16)
         inner_ref[0, :, pl.ds(at, width)] = inner
         sums_ref[0, :, pl.ds(8 * width + at, width)] = column_sum(inner.astype(F32))
-        sum_scr[...] += dot_nt(inner, weight_tile(pack_ref, "in", tile, width))
+        sum_scr[...] += dot_nt(inner, weight_tile(weights, "in", tile, 0))
         return _
 
     lax.fori_loop(0, 4, ff_tile, 0)
@@ -286,12 +324,12 @@
     hat = hat_one_ref[0].astype(F32)
     sums_ref[0, :, 3 * width : 4 * width] = column_sum(grad * hat)
     sums_ref[0, :, 4 * width : 5 * width] = column_sum(grad)
-    resid = norm_backward(grad, hat, scale_one, gain[:, 0:width])
+    resid = norm_backward(grad, hat, scale_one, gain_one)
     sum_scr[...] = resid
     attn = resid.astype(BF16)
     attn_ref[0] = attn
     sums_ref[0, :, 5 * width : 6 * width] = column_sum(attn.astype(F32))
-    go = dot_nt(attn, weight_tile(pack_ref, "out", 0, width)).astype(BF16)
+    go = dot_nt(attn, weight_tile(weights, "out", 0, 0)).astype(BF16)
     go_scr[...] = go
     product = go.astype(F32) * heads_ref[0].astype(F32)
     high = product.astype(BF16)
@@ -333,78 +371,57 @@
     total = sum_scr[...]
     for tile in range(3):
         total = total + dot_nt(
-            mix_ref[0, :, tile * width : (tile + 1) * width], weight_tile(pack_ref, "qkv", tile, width)
+            mix_ref[0, :, tile * width : (tile + 1) * width], weight_tile(weights, "qkv", tile, 0)
         )
     result = total.astype(BF16)
     g_scr[...] = result
-    grad_ref[...] = result
 
     @pl.when(layer == 0)
     def _():
         inputs_ref[0, 0] = result
-        fresh = fresh_ref[item * segs + seg] > 0
+        fresh = fresh_ref[0] > 0
         number = lax.broadcasted_iota(jnp.int32, (16, width), 0)
         folded = result[rows - 16 : rows].astype(F32) + pltpu.roll(result[0:16].astype(F32), 6, 0)
         folded = jnp.where(number >= 6, folded, 0.0).astype(BF16).astype(F32)
         init_ref[...] += jnp.where(fresh, folded, 0.0)
         carry_scr[...] = jnp.where(fresh, 0.0, folded)
 
-    carry_out_ref[...] = carry_scr[...]
-
-
-def backward_steps(
-    top_step, count, fresh, live, cot, prev, carry, labels, pack, gains, saved, inputs_so_far=None
-):
+
+def backward_steps(cot, fresh, live, labels, weights, vec, saved):
     items, segs, rows, width = cot.shape
-    hidden = 4 * width
-    at = lambda t: top_step - t
-    by_seg = lambda t, *_: (at(t) // (2 * segs), (at(t) // 2) % segs, 0, 0)
-    by_layer3 = lambda t, *_: (at(t) % 2, 0, 0)
-    by_step = lambda t, *_: (count - 1 - t, 0, 0)
-    whole = lambda shape: pl.BlockSpec(shape, lambda t, *_: (0,) * len(shape))
+    count = 2 * items * segs
+    at = lambda t: count - 1 - t
+    by_seg = lambda t: (at(t) // (2 * segs), (at(t) // 2) % segs, 0, 0)
+    by_flag = lambda t: (at(t) // 2, 0, 0)
+    by_step = lambda t: (at(t), 0, 0)
     names = ("mixed", "heads", "hat_one", "slope", "hat_two", "stats")
-    outs = [
-        ((rows, width), BF16),
-        ((rows, hidden), BF16),
-        ((rows, width), BF16),
-        ((rows, 3 * width), BF16),
-    ]
-    labels_row = labels[:, :, :, None]
-    labels_col = labels[:, :, None, :]
-    operands = [fresh, live, cot, prev, carry, labels_row, labels_col, pack, gains]
-    operands += [saved[name] for name in names]
-    in_specs = [
-        pl.BlockSpec((1, 1, rows, width), by_seg),
-        whole(prev.shape),
-        whole(carry.shape),
-        pl.BlockSpec((1, 1, rows, 1), by_seg),
-        pl.BlockSpec((1, 1, 1, rows), by_seg),
-        pl.BlockSpec((2, 2, 1) + pack.shape[3:], lambda t, *_: (0, 0, at(t) % 2, 0, 0)),
-        pl.BlockSpec((1, 1, gains.shape[2]), by_layer3),
-    ] + [pl.BlockSpec((1,) + saved[name].shape[1:], by_step) for name in names]
-    body = functools.partial(backward_body, top_step, segs)
-    aliases = {}
-    if inputs_so_far is not None:
-        operands.append(inputs_so_far)
-        in_specs.append(pl.BlockSpec(memory_space=pl.ANY))
-        aliases = {len(operands) - 1: len(outs) + 2}
-        inner_body = body
-
-        def body(*refs):
-            cut = 2 + len(in_specs)
-            return inner_body(*refs[: cut - 1], *refs[cut:])
-
-    grid_spec = pltpu.PrefetchScalarGridSpec(
-        num_scalar_prefetch=2,
+    outs = dict(
+        branch=(rows, width), inner=(rows, 4 * width), attn=(rows, width), mix=(rows, 3 * width),
+    )
+    *grads, sums, inputs, memory = pl.pallas_call(
+        functools.partial(backward_body, count, segs),
         grid=(count,),
-        in_specs=in_specs,
-        out_specs=[pl.BlockSpec((1,) + shape, by_step) for shape, _ in outs]
+        in_specs=[
+            pl.BlockSpec((1, 1, width), by_flag),
+            pl.BlockSpec((1, 1, width), by_flag),
+            pl.BlockSpec((1, 1, rows, width), by_seg),
+            pl.BlockSpec((1, 1, rows, 1), by_seg),
+            pl.BlockSpec((1, 1, 1, rows), by_seg),
+        ]
+        + weight_specs([weight.shape for weight in weights], lambda t: at(t) % 2)
+        + [pl.BlockSpec((2, 1) + vec.shape[2:], lambda t: (0, at(t) % 2, 0, 0))]
+        + [pl.BlockSpec((1,) + saved[name].shape[1:], by_step) for name in names],
+        out_specs=[pl.BlockSpec((1,) + shape, by_step) for shape in outs.values()]
         + [
-            whole((rows, width)),
             pl.BlockSpec((1, 1, 12 * width), by_step),
             pl.BlockSpec((1, 1, rows, width), by_seg),
-            whole((16, width)),
-            whole((16, width)),
+            pl.BlockSpec((16, width), lambda t: (0, 0)),
+        ],
+        out_shape=[jax.ShapeDtypeStruct((count,) + shape, BF16) for shape in outs.values()]
+        + [
+            jax.ShapeDtypeStruct((count, 1, 12 * width), F32),
+            jax.ShapeDtypeStruct(cot.shape, BF16),
+            jax.ShapeDtypeStruct((16, width), F32),
         ],
         scratch_shapes=[
             pltpu.VMEM((rows, width), BF16),
@@ -413,22 +430,321 @@
             pltpu.VMEM((rows, width), F32),
             pltpu.VMEM((rows, width), BF16),
         ],
-    )
-    return pl.pallas_call(
-        body,
-        grid_spec=grid_spec,
-        out_shape=[jax.ShapeDtypeStruct((count,) + shape, kind) for shape, kind in outs]
-        + [
-            jax.ShapeDtypeStruct((rows, width), BF16),
-            jax.ShapeDtypeStruct((count, 1, 12 * width), F32),
-            jax.ShapeDtypeStruct(cot.shape, BF16),
-            jax.ShapeDtypeStruct((16, width), F32),
-            jax.ShapeDtypeStruct((16, width), F32),
-        ],
-        input_output_aliases=aliases,
         compiler_params=pltpu.CompilerParams(vmem_limit_bytes=VMEM_BYTES),
         name="backward_steps",
-    )(*operands)
+    )(
+        fresh, live, cot, labels[:, :, :, None], labels[:, :, None, :], *weights, vec,
+        *[saved[name] for name in names],
+    )
+    return dict(zip(outs, grads)), sums, inputs, memory
+
+
+def gather_forward_body(count, *refs):
+    io = refs[:6]
+    sources = refs[6:10]
+    vec_source = refs[10]
+    outs = refs[11:21]
+    full_outs = refs[21:25]
+    vec_out = refs[25]
+    forward_scratch = refs[26:30]
+    weights = refs[30:34]
+    vec = refs[34]
+    (
+        load_sems, hid_load_sems, store_sems, x_sems, y_sems, fx_sems, fy_sems, core_sems,
+        line_core_sems, up_sems, down_sems, vec_sems, vec_load_sem,
+    ) = refs[35:]
+    step = pl.program_id(0)
+    section, place = lax.axis_index("section"), lax.axis_index("dp")
+    x, y = section % 2, section // 2
+    core, z = place % 2, place // 2
+    hid = weights[3]
+    depth = hid.shape[0]
+    x_dev = (y * 2 + 1 - x, place)
+    y_dev = ((1 - y) * 2 + x, place)
+    core_dev = (section, z * 2 + 1 - core)
+    up_dev = (section, (z + 1) % depth * 2 + core)
+    down_dev = (section, (z + depth - 1) % depth * 2 + core)
+    blocks = ((y, 1 - x), (1 - y, x), (1 - y, 1 - x))
+
+    def remote(source, target, sems, index, device):
+        return pltpu.make_async_remote_copy(
+            src_ref=source, dst_ref=target, send_sem=sems.at[(0, *index)], recv_sem=sems.at[(1, *index)],
+            device_id=device, device_id_type=MESH,
+        )
+
+    def slot(number, block, first=None, part=None):
+        lead = (z if first is None else first, core) if number == 3 else (core,)
+        view = weights[number].at[(*lead, *block)]
+        if part is not None:
+            tall = weights[number].shape[-2] // 2
+            view = view.at[pl.ds(part * tall, tall)]
+        return view
+
+    def own(number):
+        tall = weights[number].shape[-2]
+        at = (z * 2 + core) if number == 3 else core
+        return sources[number].at[0, pl.ds(pl.multiple_of(at * tall, tall), tall)]
+
+    def x_copy(number):
+        return remote(own(number), slot(number, (y, x)), x_sems, (number,), x_dev)
+
+    def y_copy(number):
+        return remote(own(number), slot(number, (y, x)), y_sems, (number,), y_dev)
+
+    def fy_copy(number):
+        piece = slot(number, blocks[0], part=0)
+        return remote(piece, piece, fy_sems, (number,), y_dev)
+
+    def fx_copy(number):
+        piece = slot(number, blocks[1], part=1)
+        return remote(piece, piece, fx_sems, (number,), x_dev)
+
+    def core_copy(number, kind):
+        piece = slot(number, blocks[kind]) if kind < 2 else slot(number, blocks[2], part=kind - 2)
+        return remote(piece, piece, core_sems, (number, kind), core_dev)
+
+    def line_core_copy(at, kind):
+        piece = slot(3, blocks[kind], first=at)
+        return remote(piece, piece, line_core_sems, (at, kind), core_dev)
+
+    def up_copy(at, kind):
+        piece = slot(3, blocks[kind], first=at)
+        return remote(piece, piece, up_sems, (at, kind), up_dev)
+
+    def down_copy(at, kind):
+        piece = slot(3, blocks[kind], first=at)
+        return remote(piece, piece, down_sems, (at, kind), down_dev)
+
+    def vec_copy(kind):
+        block = ((y, x), (y, x), (y, 1 - x))[kind]
+        source = vec_source if kind < 2 else vec.at[block]
+        return remote(source, vec.at[block], vec_sems, (kind,), (x_dev, y_dev, y_dev)[kind])
+
+    def loads():
+        copies = [
+            pltpu.make_async_copy(
+                sources[number].at[0, pl.ds(side * weights[number].shape[-2], weights[number].shape[-2])],
+                weights[number].at[side, y, x],
+                load_sems.at[number, side],
+            )
+            for number in range(3)
+            for side in range(2)
+        ]
+        tall = hid.shape[-2]
+        copies += [
+            pltpu.make_async_copy(
+                sources[3].at[0, pl.ds((at * 2 + side) * tall, tall)],
+                hid.at[at, side, y, x],
+                hid_load_sems.at[at, side],
+            )
+            for at in range(depth)
+            for side in range(2)
+        ]
+        return copies + [pltpu.make_async_copy(vec_source, vec.at[y, x], vec_load_sem)]
+
+    def full_stores():
+        copies = [
+            pltpu.make_async_copy(weights[number], full_outs[number], store_sems.at[number])
+            for number in range(4)
+        ]
+        return copies + [pltpu.make_async_copy(vec, vec_out, store_sems.at[4])]
+
+    def spread(kind):
+        @pl.when(z < depth - 1)
+        def _():
+            up_copy(z, kind).start()
+
+        @pl.when(z > 0)
+        def _():
+            down_copy(z, kind).start()
+
+        line_core_copy(z, kind).start()
+
+    def hop(distance):
+        @pl.when(z >= distance)
+        def _():
+            for kind in range(3):
+                up_copy(z - distance, kind).wait_recv()
+
+                @pl.when(z < depth - 1)
+                def _():
+                    up_copy(z - distance, kind).start()
+
+                line_core_copy(z - distance, kind).start()
+
+        @pl.when(z + distance < depth)
+        def _():
+            for kind in range(3):
+                down_copy(z + distance, kind).wait_recv()
+
+                @pl.when(z > 0)
+                def _():
+                    down_copy(z + distance, kind).start()
+
+                line_core_copy(z + distance, kind).start()
+
+    def direct(number):
+        x_copy(number).wait_recv()
+        fy_copy(number).start()
+        core_copy(number, 0).start()
+        y_copy(number).wait_recv()
+        fx_copy(number).start()
+        core_copy(number, 1).start()
+
+    def diagonal(number):
+        fy_copy(number).wait_recv()
+        core_copy(number, 2).start()
+        fx_copy(number).wait_recv()
+        core_copy(number, 3).start()
+
+    def complete(number):
+        for kind in range(4):
+            core_copy(number, kind).wait_recv()
+
+    def before_mix():
+        @pl.when(step == 0)
+        def _():
+            for copy in loads():
+                copy.start()
+            barrier = pltpu.get_barrier_semaphore()
+            for device in (x_dev, y_dev, core_dev):
+                pl.semaphore_signal(barrier, inc=1, device_id=device, device_id_type=MESH)
+
+            @pl.when(z < depth - 1)
+            def _():
+                pl.semaphore_signal(barrier, inc=1, device_id=up_dev, device_id_type=MESH)
+
+            @pl.when(z > 0)
+            def _():
+                pl.semaphore_signal(barrier, inc=1, device_id=down_dev, device_id_type=MESH)
+
+            pl.semaphore_wait(barrier, 3 + jnp.where(z > 0, 1, 0) + jnp.where(z < depth - 1, 1, 0))
+            x_copy(3).start()
+            y_copy(3).start()
+            vec_copy(0).start()
+            vec_copy(1).start()
+            for number in (0, 1):
+                x_copy(number).start()
+                y_copy(number).start()
+            x_copy(3).wait_recv()
+            fy_copy(3).start()
+            spread(0)
+            y_copy(3).wait_recv()
+            fx_copy(3).start()
+            spread(1)
+            vec_copy(0).wait_recv()
+            vec_copy(2).start()
+            x_copy(2).start()
+            y_copy(2).start()
+            fy_copy(3).wait_recv()
+            fx_copy(3).wait_recv()
+            spread(2)
+            direct(0)
+            direct(1)
+            hop(1)
+            diagonal(0)
+            diagonal(1)
+            vec_copy(1).wait_recv()
+            vec_copy(2).wait_recv()
+            complete(0)
+            for copy in loads():
+                copy.wait()
+
+    def before_out():
+        @pl.when(step == 0)
+        def _():
+            hop(2)
+            direct(2)
+            hop(3)
+            diagonal(2)
+            complete(1)
+            complete(2)
+            for at in range(depth):
+                for kind in range(3):
+                    line_core_copy(at, kind).wait_recv()
+
+        @pl.when(step == 1)
+        def _():
+            for copy in full_stores():
+                copy.start()
+
+    forward_layer(
+        step, step % 2, step % 2, before_mix, before_out, *io, weights, vec, *outs, *forward_scratch
+    )
+
+    @pl.when(step == count - 1)
+    def _():
+        for copy in full_stores():
+            copy.wait()
+        for number in range(4):
+            x_copy(number).wait_send()
+            y_copy(number).wait_send()
+            fx_copy(number).wait_send()
+            fy_copy(number).wait_send()
+            if number < 3:
+                for kind in range(4):
+                    core_copy(number, kind).wait_send()
+        for kind in range(3):
+            vec_copy(kind).wait_send()
+            for at in range(depth):
+                line_core_copy(at, kind).wait_send()
+
+                @pl.when((z >= at) & (z < depth - 1))
+                def _():
+                    up_copy(at, kind).wait_send()
+
+                @pl.when((z <= at) & (z > 0))
+                def _():
+                    down_copy(at, kind).wait_send()
+
+
+def full_weight_shapes(w_qkv, w_out, w_in, w_hid):
+    half, width = w_out.shape[1:]
+    return [(2, 2, 2, half // 2, block.shape[2]) for block in (w_qkv, w_out, w_in)] + [
+        (4, 2, 2, 2, w_hid.shape[1] // 8, width)
+    ]
+
+
+def gather_forward(text, fresh, live, init, labels, blocks, vec):
+    count, operands, in_specs, out_specs, out_shape, scratch = forward_io(text, fresh, live, init, labels)
+    shapes = full_weight_shapes(*blocks)
+    vec_shape = (2, 2) + vec.shape
+    any_spec = pl.BlockSpec(memory_space=pl.ANY)
+    dma = pltpu.SemaphoreType.DMA
+    depth = shapes[3][0]
+    saved_count = len(out_specs)
+    outs = pl.pallas_call(
+        functools.partial(gather_forward_body, count),
+        grid=(count,),
+        in_specs=in_specs + [any_spec] * 5,
+        out_specs=out_specs + [any_spec] * 5,
+        out_shape=out_shape + [jax.ShapeDtypeStruct(shape, BF16) for shape in (*shapes, vec_shape)],
+        scratch_shapes=scratch
+        + [pltpu.VMEM(shape, BF16) for shape in (*shapes, vec_shape)]
+        + [
+            dma((3, 2)), dma((depth, 2)), dma((5,)), dma((2, 4)), dma((2, 4)), dma((2, 4)), dma((2, 4)),
+            dma((2, 3, 4)), dma((2, depth, 3)), dma((2, depth, 3)), dma((2, depth, 3)), dma((2, 3)), dma,
+        ],
+        compiler_params=pltpu.CompilerParams(
+            vmem_limit_bytes=VMEM_BYTES, collective_id=1, has_side_effects=True
+        ),
+        name="gather_forward",
+    )(*operands, *blocks, vec)
+    saved = dict(zip(saved_shapes(*text.shape[2:]), outs))
+    return saved, outs[saved_count - 1], outs[saved_count : saved_count + 4], outs[saved_count + 4]
+
+
+def gather_apart(blocks, vec):
+    shapes = full_weight_shapes(*blocks)
+    full = []
+    for block, shape in zip(blocks, shapes):
+        gathered = lax.all_gather(block[0], "section")
+        lead = len(shape) - 4
+        gathered = gathered.reshape(2, 2, *shape[: lead], *shape[-2:])
+        order = (*range(2, 2 + lead), 0, 1, 2 + lead, 3 + lead)
+        full.append(gathered.transpose(order))
+    vec_full = lax.all_gather(vec, "section").reshape(2, 2, *vec.shape)
+    return full, vec_full
 
 
 GRAD_NAMES = ("first", "inner", "active", "branch", "x", "mix", "heads", "attn")
@@ -554,9 +870,6 @@
         compiler_params=pltpu.CompilerParams(vmem_limit_bytes=VMEM_BYTES),
         name="weight_grads",
     )(*sources, extras)
-
-
-MESH = pl.DeviceIdType.MESH
 
 
 def add_into(ref, other):
@@ -942,35 +1255,8 @@
     )(*sources, extras)
 
 
-SAVED_NAMES = (
-    "x", "mixed", "heads", "hat_one", "first", "active", "slope", "hat_two", "stats", "out",
-)
-
-
-def core_groups(dp):
-    return [[2 * at, 2 * at + 1] for at in range(dp // 2)]
-
-
 def other_core(block, dp):
     return lax.ppermute(block, "dp", [(at, at ^ 1) for at in range(dp)])
-
-
-def pack_blocks(core, w_qkv, w_out, w_in, w_hid, biases, norm_gains):
-    half, width = w_out.shape
-    part = half // 2
-
-    def own(block):
-        size = block.shape[0] // 2
-        return lax.dynamic_slice_in_dim(block, core * size, size, 0)
-
-    tiles = []
-    for block in (w_qkv, w_out, w_in):
-        block = own(block)
-        tiles += [block[:, at : at + width] for at in range(0, block.shape[1], width)]
-    tiles.append(own(w_hid))
-    vector = jnp.concatenate([biases, norm_gains])
-    vector = jnp.pad(vector, (0, 16 * width - vector.shape[0])).reshape(16, width)
-    return jnp.concatenate(tiles + [vector], axis=0)
 
 
 def per_device(
@@ -992,22 +1278,19 @@
     rows = text_len + 2 * mem_rows
     half = width // 2
     dp = lax.axis_size("dp")
-    core = lax.axis_index("dp") % 2
     vector_len = biases.shape[1]
 
-    packed = pack_blocks(core, w_qkv[0], w_out[0], w_in[0], w_hid[0], biases[0], norm_gains[0])
-    gathered = lax.all_gather(packed, "section")
-    small = gathered[:, -16:].reshape(4, 16 * width).astype(F32)
-    pack = lax.all_gather(gathered, "dp", axis_index_groups=core_groups(dp))
-    pack = pack.reshape(2, 2, 2, *pack.shape[2:])
-    vectors = jnp.concatenate([small[:2, :vector_len], small[2:, :vector_len]], axis=1)[:, None]
-    gains = small[:, vector_len : vector_len + width]
-    gains = jnp.concatenate([gains[:2], gains[2:]], axis=1)[:, None]
-
+    blocks = (w_qkv, w_out, w_in, w_hid)
+    vec = jnp.concatenate([biases[0], norm_gains[0]])
+    vec = jnp.pad(vec, (0, 16 * width - vec.shape[0])).reshape(16, width)
     filler = jnp.full((items, segs, mem_rows), -1, jnp.int32)
     labels = jnp.concatenate([filler, jnp.cumsum(boundaries, axis=-1), filler], axis=-1)
-    live = (jnp.arange(segs)[None] < seg_counts[:, None]).astype(jnp.int32).reshape(-1)
-    fresh = ((jnp.arange(segs)[None] == 0) | (mem_resets > 0)).astype(jnp.int32).reshape(-1)
+
+    def flags(values):
+        return jnp.broadcast_to(values.astype(jnp.int32).reshape(-1, 1, 1), (items * segs, 1, width))
+
+    live = flags(jnp.arange(segs)[None] < seg_counts[:, None])
+    fresh = flags((jnp.arange(segs)[None] == 0) | (mem_resets > 0))
     text = jnp.pad(text_rows, ((0, 0), (0, 0), (mem_rows, mem_rows), (0, 0)))
     start = memory_init.astype(F32)
     init = jnp.stack(
@@ -1015,16 +1298,15 @@
     )
 
     steps = 2 * items * segs
-    blank = jnp.zeros((rows, width), BF16)
-    *saved, activations = forward_steps(
-        0, steps, fresh, live, text, init, blank, labels, pack, vectors, gains
+    if dp == 8:
+        saved, activations, weights, vecs = gather_forward(text, fresh, live, init, labels, blocks, vec)
+    else:
+        weights, vecs = gather_apart(blocks, vec)
+        saved, activations = forward_steps(text, fresh, live, init, labels, weights, vecs)
+    grads, sums, input_grads, memory_grad = backward_steps(
+        cotangent, fresh, live, labels, weights, vecs, saved
     )
-    saved = dict(zip(SAVED_NAMES, saved))
-    branch, inner, attn, mix, _, sums, input_grads, memory_grad, _ = backward_steps(
-        steps - 1, steps, fresh, live, cotangent, blank, jnp.zeros((16, width), F32), labels, pack,
-        gains, saved,
-    )
-    saved.update(branch=branch, inner=inner, attn=attn, mix=mix)
+    saved.update(grads)
 
     lanes = 4 * width // dp
     memory_part = memory_grad[16 - mem_rows :].reshape(-1)

time: 549 us -> 450 us (0.82)
  waiting for transfers between devices: 177 us -> 0 us
  Pallas kernels: 311 us -> 415 us
  between operations: 15.2 us -> 1.7 us
  local copies, waits for them, and re-layouts: 31.3 us -> 19.7 us
    all_gather x2 -> x0, waiting for transfers between devices: 177 us -> none  [the longest x1 139 us: per_device(): gathered = lax.all_gather(packed, 'section')]
    pallas_call x2, Pallas kernels: 118 us -> 221 us  [the longest x1 157 us: gather_forward(): pl.pallas_call(functools.partial(gather_forward_body, count), grid=(count...]
    unnamed x44 -> x29, local copies, waits for them, and re-layouts: 17.8 us -> 10.3 us
  transfers between devices with their start and end apart: 2 -> 0, of which waited for: 2 -> 0; matrix products, arithmetic and copies ran while one was open for 2% -> 0% of each run, Pallas kernels for 0% -> 0%
where the time goes in v4:
time: 450 us; the launch traced here: 443 us
  Pallas kernels  415 us (92%)
  local copies, waits for them, and re-layouts  19.7 us (4%)
  other arithmetic  6.36 us (1%)
    pallas_call x1, Pallas kernels, grad_reduce(): pl.pallas_call(functools.partial(grad_reduce_body, dp, segs_all), in_spec...  194 us
    pallas_call x1, Pallas kernels, gather_forward(): pl.pallas_call(functools.partial(gather_forward_body, count), grid=(count...  157 us
    pallas_call x1, Pallas kernels, backward_steps(): pl.pallas_call(functools.partial(backward_body, count, segs), grid=(count...  64 us
    unnamed x29, local copies, waits for them, and re-layouts  10.3 us

profile of v4, /device:TPU:0, one launch (start us, length us, event | category | flops | bytes accessed | tf_op | source)
XLA Modules:
  0.0 442.6 jit_solution(6316984474947782587)
XLA Ops:
  0.6 0.7 pad.31
  1.4 0.6 reduce-window.6
  2.0 0.2 slice_reduce_fusion.2
  2.2 0.2 reduce-window.9
  2.6 0.9 copy.30.refs_4_.labels_row_ref
  3.5 0.7 fusion.6.refs_5_.labels_col_ref
  4.1 0.7 convert_element_type.39
  4.9 0.6 pad_maximum_fusion.1.refs_3_
  6.2 0.7 broadcast_in_dim.38.refs_1_.live_ref
  6.9 0.7 fusion.3
  7.6 0.7 broadcast_in_dim.37.refs_0_.fresh_ref
  8.2 1.3 copy.27
  9.5 1.2 pad.28.refs_2_
  10.8 0.7 reshape.151.refs_10_
  11.4 157.0 %gather_forward.1 = (bf16[4,320,768]{2,1,0:T(8,128)(2,1)}, bf16[4,320,2304]{2,1,0:T(8,128)(2,1)}, bf16[4,320,768]{2,1,0:T(8,128)(2,1)}, bf16[4,320,768]{2,1,0:T(...) custom-call(s32[2,1,768]{2,1,0:T(1,128)} %broadcast_in_dim.37.refs_0, ...), custom_call_target="tpu_custom_call" | custom-call | tf_op jit(solution)/shard_map/gather_forward/pallas_call | solution.py:716
  168.4 64.0 %backward_steps.1 = (bf16[4,320,768]{2,1,0:T(8,128)(2,1)}, bf16[4,320,3072]{2,1,0:T(8,128)(2,1)}, bf16[4,320,768]{2,1,0:T(8,128)(2,1)}, bf16[4,320,2304]{2,1,0:T...) custom-call(s32[2,1,768]{2,1,0:T(1,128)} %broadcast_in_dim.37.refs_0_.fresh_ref, ...), custom_call_target="tpu_custom_call" | custom-call | tf_op jit(solution)/shard_map/backward_steps/pallas_call | solution.py:401
  232.4 1.3 reduce.5
  233.7 0.1 reshape.153
  233.9 0.2 slice_reduce_fusion.1
  234.1 0.1 stack.39
  234.2 0.1 stack.40
  234.3 0.3 dynamic-update-slice.6
  234.6 0.2 dynamic-update-slice.7
  234.8 0.2 dynamic-update-slice.8
  235.0 0.3 dynamic-update-slice
  235.3 0.2 dynamic-update-slice.1
  235.6 0.2 dynamic-update-slice.2
  235.8 0.2 dynamic-update-slice.10
  236.0 0.4 dynamic-update-slice.11
  236.4 0.1 reshape.154
  236.5 0.8 slice.182
  237.3 0.1 concatenate.31
  237.6 0.1 stack.43
  237.7 0.1 stack.44
  237.8 0.2 dynamic-update-slice.4
  238.1 0.2 dynamic-update-slice.5
  238.3 0.1 reshape.155
  238.4 0.1 concatenate.33
  238.7 1.1 pad_maximum_fusion.refs_8_
  239.8 193.8 %grad_reduce.1 = (f32[1,384,288]{2,1,0:T(8,128)}, f32[1,384,96]{2,1,0:T(8,128)}, f32[1,384,384]{2,1,0:T(8,128)}, f32[1,1536,96]{2,1,0:T(8,128)}, f32[3,16,384]{2,1,0:T(8,128)}) custom-call(bf16[4,320,768]{2,1,0:T(8,128)(2,1)} %get-tuple-element.49.refs_0_, bf16[4,320,3072]{2,1,0:T(8,128)(2,1)} %get-tuple-element.50.refs_1_, ...), custom_call_target="tpu_custom_call" | custom-call | tf_op jit(solution)/shard_map/grad_reduce/pallas_call | solution.py:1235
  433.7 2.3 copy.36
  436.0 2.1 copy.34
  438.1 0.8 copy.35
  438.9 0.6 slice.169
  439.5 0.6 slice.170
  440.1 0.6 slice_bitcast_fusion.1
  440.7 0.9 copy.59
  441.6 0.8 copy.60
  (44 shorter events, 0.9 us)
Async XLA Ops:
  4.9 5.8 %copy-start.4 = (bf16[1,3840]{1,0:T(2,128)(2,1)S(1)}, bf16[1,3840]{1,0:T(2,128)(2,1)}, u32[]{:S(2)}) copy-start(bf16[1,3840]{1,0:T(2,128)(2,1)} %param.19) | copy-start | bytes 23044
  4.9 5.8 %copy-start.5 = (bf16[1,768]{1,0:T(2,128)(2,1)S(1)}, bf16[1,768]{1,0:T(2,128)(2,1)}, u32[]{:S(2)}) copy-start(bf16[1,768]{1,0:T(2,128)(2,1)} %param.20) | copy-start | bytes 4612
  433.6 4.4 %copy-start.3 = (f32[1,384,96]{2,1,0:T(8,128)S(1)}, f32[1,384,96]{2,1,0:T(8,128)}, u32[]{:S(2)}) copy-start(f32[1,384,96]{2,1,0:T(8,128)} %get-tuple-element.76) | copy-start | bytes 442372
  433.7 5.2 %copy-start.2 = (f32[3,16,384]{2,1,0:T(8,128)S(1)}, f32[3,16,384]{2,1,0:T(8,128)}, u32[]{:S(2)}) copy-start(f32[3,16,384]{2,1,0:T(8,128)} %get-tuple-element.58) | copy-start | bytes 221188
  433.7 7.0 %copy-start = (bf16[1,2,320,768]{3,2,1,0:T(8,128)(2,1)S(1)}, bf16[1,2,320,768]{3,2,1,0:T(8,128)(2,1)}, u32[]{:S(2)}) copy-start(bf16[1,2,320,768]{3,2,1,0:T(8,128)(2,1)} %get-tuple-element.108) | copy-start | bytes 2949124
  436.0 5.7 %copy-start.1 = (f32[1,384,384]{2,1,0:T(8,128)S(1)}, f32[1,384,384]{2,1,0:T(8,128)}, u32[]{:S(2)}) copy-start(f32[1,384,384]{2,1,0:T(8,128)} %get-tuple-element.113) | copy-start | bytes 1769476

commit v5 on v4

--- a/solution.py
+++ b/solution.py
@@ -30,17 +30,24 @@
 
 
 def weight_tile(refs, kind, tile, layer):
-    qkv_ref, out_ref, in_ref, hid_ref = refs
-    width = out_ref.shape[-1]
-    if kind == "hid":
-        quarters = hid_ref.shape[0] // 2
+    qkv_ref, in_ref, end_ref = refs
+    quarters, _, _, _, tall, width = end_ref.shape
+    thin = tall // 5
+    if kind == "out":
         pieces = [
-            hid_ref[(tile % 2) * quarters + at, core, tile // 2, layer]
-            for at in range(quarters)
+            end_ref[quarter, core, half, layer, 0:thin]
+            for half in range(2)
+            for quarter in range(quarters)
+            for core in range(2)
+        ]
+    elif kind == "hid":
+        pieces = [
+            end_ref[(tile % 2) * (quarters // 2) + at, core, tile // 2, layer, thin:tall]
+            for at in range(quarters // 2)
             for core in range(2)
         ]
     else:
-        ref = {"qkv": qkv_ref, "out": out_ref, "in": in_ref}[kind]
+        ref = qkv_ref if kind == "qkv" else in_ref
         at = tile * width if isinstance(tile, int) else pl.multiple_of(tile * width, width)
         pieces = [ref[core, half, layer, :, pl.ds(at, width)] for half in range(2) for core in range(2)]
     return jnp.concatenate(pieces, axis=0)
@@ -68,13 +75,34 @@
     return phi, density
 
 
-def vector_rows(vec_ref, layer):
-    low, high = vec_ref[0, layer].astype(F32), vec_ref[1, layer].astype(F32)
-    row = lambda block, at: block[at : at + 1]
+def vector_rows(vec_ref, layer, width):
+    row = lambda half, at: vec_ref[half, layer, :, at * width : (at + 1) * width]
     return dict(
-        bias_q=row(low, 0), bias_v=row(low, 1), bias_o=row(low, 2), shift_one=row(low, 3),
-        bias_hid=row(high, 3), shift_two=row(high, 4), gain_one=row(low, 5), gain_two=row(high, 5),
+        bias_q=row(0, 0), bias_v=row(0, 1), bias_o=row(0, 2), shift_one=row(0, 3),
+        bias_in=(row(0, 4), row(1, 0), row(1, 1), row(1, 2)),
+        bias_hid=row(1, 3), shift_two=row(1, 4), gain_one=row(0, 5), gain_two=row(1, 5),
     )
+
+
+def ones_where(shape, condition):
+    rows = lax.broadcasted_iota(jnp.int32, shape, 0)
+    columns = lax.broadcasted_iota(jnp.int32, shape, 1)
+    return condition(rows, columns).astype(BF16)
+
+
+def document_bias(bounds, rows, mem):
+    text = bounds.shape[1]
+    eight = jnp.broadcast_to(bounds, (8, text)).astype(BF16)
+    upto = ones_where((text, rows), lambda r, c: r <= c - mem)
+    below = ones_where((rows, text), lambda r, c: c <= r - mem)
+    columns = dot_nn(eight, upto)[0:1]
+    lines = dot_nt(below, eight)[:, 0:1]
+    place = lax.broadcasted_iota(jnp.int32, (1, rows), 1)
+    columns = jnp.where((place < mem) | (place >= mem + text), -1.0, columns)
+    place = lax.broadcasted_iota(jnp.int32, (rows, 1), 0)
+    lines = jnp.where((place < mem) | (place >= mem + text), -1.0, lines)
+    allowed = (lines == columns) | (lines < 0) | (columns < 0)
+    return jnp.where(allowed, 0.0, MASKED)
 
 
 def norm_forward(values):
@@ -84,41 +112,36 @@
 
 
 def forward_layer(
-    step, layer, at_layer, before_mix, before_out, fresh_ref, live_ref, text_ref, init_ref,
-    labels_row_ref, labels_col_ref, weights, vec_ref,
+    step, segs, at_layer, before_mix, before_out, resets_ref, counts_ref, text_ref, init_ref,
+    bounds_ref, weights, vec_ref,
     x_ref, mixed_ref, heads_ref, hat_one_ref, first_ref, active_ref, slope_ref, hat_two_ref,
     stats_ref, acts_ref, y_scr, bias_scr, sum_scr, bias_in_scr,
 ):
     rows, width = y_scr.shape
+    text_len, mem = text_ref.shape[2], init_ref.shape[0]
+    layer, seg, item = step % 2, (step // 2) % segs, step // (2 * segs)
 
     @pl.when(layer == 0)
     def _():
-        fresh = fresh_ref[0] > 0
-        last = y_scr[rows - 16 : rows, :].astype(F32)
-        head_rows = pltpu.roll(last, 10, 0)
-        number = lax.broadcasted_iota(jnp.int32, (16, width), 0)
-        top = jnp.where(fresh, init_ref[0], head_rows)
-        low = jnp.where(fresh, init_ref[1], last)
-        x_ref[0] = text_ref[0, 0]
-        x_ref[0, 0:16, :] = jnp.where(number < 10, top, text_ref[0, 0, 0:16, :].astype(F32)).astype(BF16)
-        x_ref[0, rows - 16 : rows, :] = jnp.where(
-            number >= 6, low, text_ref[0, 0, rows - 16 : rows, :].astype(F32)
-        ).astype(BF16)
+        fresh = (seg == 0) | (resets_ref[item, seg] > 0)
+        place = ones_where((rows, text_len), lambda r, c: r - mem == c)
+        start = ones_where((rows, mem), lambda r, c: (r == c) | (r - mem - text_len == c))
+        again = ones_where(
+            (rows, rows),
+            lambda r, c: ((r < mem) & (r + mem + text_len == c)) | ((r >= mem + text_len) & (r == c)),
+        )
+        memory = jnp.where(fresh, dot_nn(start, init_ref[...]), dot_nn(again, y_scr[...]))
+        x_ref[0] = (dot_nn(place, text_ref[0, 0]) + memory).astype(BF16)
+        bias_scr[...] = document_bias(bounds_ref[0, pl.ds(seg, 1), :], rows, mem)
 
     @pl.when(layer == 1)
     def _():
         x_ref[0] = y_scr[...]
 
-    row_side = labels_row_ref[0, 0]
-    col_side = labels_col_ref[0, 0]
-    allowed = (row_side == col_side) | (row_side < 0) | (col_side < 0)
-    bias_scr[...] = jnp.where(allowed, 0.0, MASKED)
-
     before_mix()
-    vec = vector_rows(vec_ref, at_layer)
-    low, high = vec_ref[0, at_layer].astype(F32), vec_ref[1, at_layer].astype(F32)
-    for part, row in enumerate((low[4:5], high[0:1], high[1:2], high[2:3])):
-        bias_in_scr[part] = row
+    vec = vector_rows(vec_ref, at_layer, width)
+    for part in range(4):
+        bias_in_scr[part] = vec["bias_in"][part]
     inputs = x_ref[0]
     for tile in range(3):
         mixed = dot_nn(inputs, weight_tile(weights, "qkv", tile, at_layer))
@@ -177,7 +200,7 @@
 
     @pl.when(layer == 1)
     def _():
-        acts_ref[0, 0] = jnp.where(live_ref[0] > 0, result, 0)
+        acts_ref[0, 0] = jnp.where(seg < counts_ref[item], result, 0)
 
 
 def saved_shapes(rows, width):
@@ -194,57 +217,57 @@
     )
 
 
-def forward_io(text, fresh, live, init, labels):
-    items, segs, rows, width = text.shape
-    count = 2 * items * segs
+def forward_io(text, resets, counts, init, bounds):
+    items, segs, text_len, width = text.shape
+    rows = text_len + 2 * init.shape[0]
+    steps = 2 * items * segs
     saved = saved_shapes(rows, width)
     by_seg = lambda t: (t // (2 * segs), (t // 2) % segs, 0, 0)
-    by_flag = lambda t: (t // 2, 0, 0)
-    operands = [fresh, live, text, init, labels[:, :, :, None], labels[:, :, None, :]]
+    operands = [resets, counts, text, init, bounds]
     in_specs = [
-        pl.BlockSpec((1, 1, width), by_flag),
-        pl.BlockSpec((1, 1, width), by_flag),
-        pl.BlockSpec((1, 1, rows, width), by_seg),
-        pl.BlockSpec(init.shape, lambda t: (0, 0, 0)),
-        pl.BlockSpec((1, 1, rows, 1), by_seg),
-        pl.BlockSpec((1, 1, 1, rows), by_seg),
+        pl.BlockSpec(memory_space=pltpu.SMEM),
+        pl.BlockSpec(memory_space=pltpu.SMEM),
+        pl.BlockSpec((1, 1, text_len, width), by_seg),
+        pl.BlockSpec(init.shape, lambda t: (0, 0)),
+        pl.BlockSpec((1, segs, text_len), lambda t: (t // (2 * segs), 0, 0)),
     ]
     out_specs = [pl.BlockSpec((1,) + shape, lambda t: (t, 0, 0)) for shape, _ in saved.values()]
     out_specs.append(pl.BlockSpec((1, 1, rows, width), by_seg))
-    out_shape = [jax.ShapeDtypeStruct((count,) + shape, kind) for shape, kind in saved.values()]
-    out_shape.append(jax.ShapeDtypeStruct(text.shape, BF16))
+    out_shape = [jax.ShapeDtypeStruct((steps,) + shape, kind) for shape, kind in saved.values()]
+    out_shape.append(jax.ShapeDtypeStruct((items, segs, rows, width), BF16))
     scratch = [
         pltpu.VMEM((rows, width), BF16),
         pltpu.VMEM((rows, rows), F32),
         pltpu.VMEM((rows, width), F32),
         pltpu.VMEM((4, 1, width), F32),
     ]
-    return count, operands, in_specs, out_specs, out_shape, scratch
+    return steps, saved, operands, in_specs, out_specs, out_shape, scratch
 
 
 def nothing():
     pass
 
 
-def forward_body(*refs):
+def forward_body(segs, *refs):
     step = pl.program_id(0)
-    y_scr = refs[21]
+    y_scr = refs[19]
 
     @pl.when(step == 0)
     def _():
         y_scr[...] = jnp.zeros_like(y_scr)
 
-    forward_layer(step, step % 2, 0, nothing, nothing, *refs[:6], refs[6:10], *refs[10:])
-
-
-def forward_steps(text, fresh, live, init, labels, weights, vec):
-    count, operands, in_specs, out_specs, out_shape, scratch = forward_io(text, fresh, live, init, labels)
-    layer_of = lambda t: t % 2
-    *saved, acts = pl.pallas_call(
-        forward_body,
-        grid=(count,),
+    forward_layer(step, segs, 0, nothing, nothing, *refs[:5], refs[5:8], *refs[8:])
+
+
+def forward_steps(text, resets, counts, init, bounds, weights, vec):
+    steps, saved, operands, in_specs, out_specs, out_shape, scratch = forward_io(
+        text, resets, counts, init, bounds
+    )
+    *outs, acts = pl.pallas_call(
+        functools.partial(forward_body, text.shape[1]),
+        grid=(steps,),
         in_specs=in_specs
-        + weight_specs([weight.shape for weight in weights], layer_of)
+        + weight_specs([weight.shape for weight in weights], lambda t: t % 2)
         + [pl.BlockSpec((2, 1) + vec.shape[2:], lambda t: (0, t % 2, 0, 0))],
         out_specs=out_specs,
         out_shape=out_shape,
@@ -252,7 +275,7 @@
         compiler_params=pltpu.CompilerParams(vmem_limit_bytes=VMEM_BYTES),
         name="forward_steps",
     )(*operands, *weights, vec)
-    return dict(zip(saved_shapes(*text.shape[2:]), saved)), acts
+    return dict(zip(saved, outs)), acts
 
 
 def norm_backward(grad, hat, scale, gain):
@@ -267,18 +290,19 @@
 
 
 def backward_body(
-    count, segs, fresh_ref, live_ref, cot_ref, labels_row_ref, labels_col_ref, qkv_ref, w_out_ref,
-    in_ref, hid_ref, vec_ref, mixed_ref, heads_ref, hat_one_ref, slope_ref, hat_two_ref, stats_ref,
-    branch_ref, inner_ref, attn_ref, mix_ref, sums_ref, inputs_ref, init_ref,
+    count, segs, mem, resets_ref, counts_ref, cot_ref, bounds_ref, acts_ref, qkv_ref, in_ref, end_ref,
+    vec_ref, mixed_ref, heads_ref, hat_one_ref, slope_ref, hat_two_ref, stats_ref,
+    branch_ref, inner_ref, attn_ref, mix_ref, sums_ref, inputs_ref, init_ref, acts_out_ref,
     g_scr, carry_scr, bias_scr, sum_scr, go_scr,
 ):
     step = count - 1 - pl.program_id(0)
     layer = step % 2
     seg = (step // 2) % segs
     rows, width = g_scr.shape
-    weights = (qkv_ref, w_out_ref, in_ref, hid_ref)
-    gain_one = vec_ref[0, 0].astype(F32)[5:6]
-    gain_two = vec_ref[1, 0].astype(F32)[5:6]
+    item = step // (2 * segs)
+    weights = (qkv_ref, in_ref, end_ref)
+    vec = vector_rows(vec_ref, 0, width)
+    gain_one, gain_two = vec["gain_one"], vec["gain_two"]
 
     @pl.when(pl.program_id(0) == 0)
     def _():
@@ -287,15 +311,12 @@
 
     @pl.when(layer == 1)
     def _():
-        cot = jnp.where(live_ref[0] > 0, cot_ref[0, 0], 0)
+        acts_out_ref[...] = acts_ref[...]
+        bias_scr[...] = document_bias(bounds_ref[0, pl.ds(seg, 1), :], rows, mem)
+        cot = jnp.where(seg < counts_ref[item], cot_ref[0, 0], 0)
         g_scr[...] = cot
         carried = jnp.where(seg == segs - 1, 0.0, carry_scr[...])
         g_scr[rows - 16 : rows, :] = (cot[rows - 16 : rows].astype(F32) + carried).astype(BF16)
-
-    row_side = labels_row_ref[0, 0]
-    col_side = labels_col_ref[0, 0]
-    allowed = (row_side == col_side) | (row_side < 0) | (col_side < 0)
-    bias_scr[...] = jnp.where(allowed, 0.0, MASKED)
 
     stats = stats_ref[0]
     scale_one = stats[:, HEADS : HEADS + 1]
@@ -379,34 +400,35 @@
     @pl.when(layer == 0)
     def _():
         inputs_ref[0, 0] = result
-        fresh = fresh_ref[0] > 0
+        fresh = (seg == 0) | (resets_ref[item, seg] > 0)
         number = lax.broadcasted_iota(jnp.int32, (16, width), 0)
-        folded = result[rows - 16 : rows].astype(F32) + pltpu.roll(result[0:16].astype(F32), 6, 0)
-        folded = jnp.where(number >= 6, folded, 0.0).astype(BF16).astype(F32)
+        folded = result[rows - 16 : rows].astype(F32) + pltpu.roll(
+            result[0:16].astype(F32), 16 - mem, 0
+        )
+        folded = jnp.where(number >= 16 - mem, folded, 0.0).astype(BF16).astype(F32)
         init_ref[...] += jnp.where(fresh, folded, 0.0)
         carry_scr[...] = jnp.where(fresh, 0.0, folded)
 
 
-def backward_steps(cot, fresh, live, labels, weights, vec, saved):
+def backward_steps(cot, resets, counts, bounds, mem, acts, weights, vec, saved):
     items, segs, rows, width = cot.shape
-    count = 2 * items * segs
-    at = lambda t: count - 1 - t
+    steps = 2 * items * segs
+    at = lambda t: steps - 1 - t
     by_seg = lambda t: (at(t) // (2 * segs), (at(t) // 2) % segs, 0, 0)
-    by_flag = lambda t: (at(t) // 2, 0, 0)
     by_step = lambda t: (at(t), 0, 0)
     names = ("mixed", "heads", "hat_one", "slope", "hat_two", "stats")
     outs = dict(
         branch=(rows, width), inner=(rows, 4 * width), attn=(rows, width), mix=(rows, 3 * width),
     )
-    *grads, sums, inputs, memory = pl.pallas_call(
-        functools.partial(backward_body, count, segs),
-        grid=(count,),
+    *grads, sums, inputs, memory, acts = pl.pallas_call(
+        functools.partial(backward_body, steps, segs, mem),
+        grid=(steps,),
         in_specs=[
-            pl.BlockSpec((1, 1, width), by_flag),
-            pl.BlockSpec((1, 1, width), by_flag),
+            pl.BlockSpec(memory_space=pltpu.SMEM),
+            pl.BlockSpec(memory_space=pltpu.SMEM),
             pl.BlockSpec((1, 1, rows, width), by_seg),
-            pl.BlockSpec((1, 1, rows, 1), by_seg),
-            pl.BlockSpec((1, 1, 1, rows), by_seg),
+            pl.BlockSpec((1,) + bounds.shape[1:], lambda t: (at(t) // (2 * segs), 0, 0)),
+            pl.BlockSpec((1, 1, rows, width), by_seg),
         ]
         + weight_specs([weight.shape for weight in weights], lambda t: at(t) % 2)
         + [pl.BlockSpec((2, 1) + vec.shape[2:], lambda t: (0, at(t) % 2, 0, 0))]
@@ -416,12 +438,14 @@
             pl.BlockSpec((1, 1, 12 * width), by_step),
             pl.BlockSpec((1, 1, rows, width), by_seg),
             pl.BlockSpec((16, width), lambda t: (0, 0)),
+            pl.BlockSpec((1, 1, rows, width), by_seg),
         ],
-        out_shape=[jax.ShapeDtypeStruct((count,) + shape, BF16) for shape in outs.values()]
+        out_shape=[jax.ShapeDtypeStruct((steps,) + shape, BF16) for shape in outs.values()]
         + [
-            jax.ShapeDtypeStruct((count, 1, 12 * width), F32),
+            jax.ShapeDtypeStruct((steps, 1, 12 * width), F32),
             jax.ShapeDtypeStruct(cot.shape, BF16),
             jax.ShapeDtypeStruct((16, width), F32),
+            jax.ShapeDtypeStruct(cot.shape, BF16),
         ],
         scratch_shapes=[
             pltpu.VMEM((rows, width), BF16),
@@ -432,38 +456,35 @@
         ],
         compiler_params=pltpu.CompilerParams(vmem_limit_bytes=VMEM_BYTES),
         name="backward_steps",
-    )(
-        fresh, live, cot, labels[:, :, :, None], labels[:, :, None, :], *weights, vec,
-        *[saved[name] for name in names],
-    )
-    return dict(zip(outs, grads)), sums, inputs, memory
-
-
-def gather_forward_body(count, *refs):
-    io = refs[:6]
-    sources = refs[6:10]
-    vec_source = refs[10]
-    outs = refs[11:21]
-    full_outs = refs[21:25]
-    vec_out = refs[25]
-    forward_scratch = refs[26:30]
-    weights = refs[30:34]
-    vec = refs[34]
+    )(resets, counts, cot, bounds, acts, *weights, vec, *[saved[name] for name in names])
+    return dict(zip(outs, grads)), sums, inputs, memory, acts
+
+
+def gather_forward_body(steps, segs, *refs):
+    io = refs[:5]
+    qkv_src, in_src, out_src, hid_src, vec_src = refs[5:10]
+    outs = refs[10:20]
+    full_outs = refs[20:24]
+    forward_scratch = refs[24:28]
+    weights = refs[28:31]
+    vec = refs[31]
     (
-        load_sems, hid_load_sems, store_sems, x_sems, y_sems, fx_sems, fy_sems, core_sems,
+        load_sems, end_load_sems, store_sems, x_sems, y_sems, fx_sems, fy_sems, core_sems, end_sems,
         line_core_sems, up_sems, down_sems, vec_sems, vec_load_sem,
-    ) = refs[35:]
+    ) = refs[32:]
     step = pl.program_id(0)
     section, place = lax.axis_index("section"), lax.axis_index("dp")
     x, y = section % 2, section // 2
     core, z = place % 2, place // 2
-    hid = weights[3]
-    depth = hid.shape[0]
+    end = weights[2]
+    depth, _, _, _, tall, _ = end.shape
+    thin = tall // 5
     x_dev = (y * 2 + 1 - x, place)
     y_dev = ((1 - y) * 2 + x, place)
     core_dev = (section, z * 2 + 1 - core)
     up_dev = (section, (z + 1) % depth * 2 + core)
     down_dev = (section, (z + depth - 1) % depth * 2 + core)
+    own_block = (y, x)
     blocks = ((y, 1 - x), (1 - y, x), (1 - y, 1 - x))
 
     def remote(source, target, sems, index, device):
@@ -472,82 +493,107 @@
             device_id=device, device_id_type=MESH,
         )
 
-    def slot(number, block, first=None, part=None):
-        lead = (z if first is None else first, core) if number == 3 else (core,)
-        view = weights[number].at[(*lead, *block)]
-        if part is not None:
-            tall = weights[number].shape[-2] // 2
-            view = view.at[pl.ds(part * tall, tall)]
-        return view
-
-    def own(number):
-        tall = weights[number].shape[-2]
-        at = (z * 2 + core) if number == 3 else core
-        return sources[number].at[0, pl.ds(pl.multiple_of(at * tall, tall), tall)]
-
-    def x_copy(number):
-        return remote(own(number), slot(number, (y, x)), x_sems, (number,), x_dev)
-
-    def y_copy(number):
-        return remote(own(number), slot(number, (y, x)), y_sems, (number,), y_dev)
+
+    def part_of(number, block, part):
+        rows = weights[number].shape[-2] // 2
+        return weights[number].at[core, block[0], block[1], pl.ds(part * rows, rows)]
+
+    def own_part(number, part):
+        rows = weights[number].shape[-2] // 2
+        at = pl.multiple_of((core * 2 + part) * rows, rows)
+        return (qkv_src, in_src)[number].at[0, pl.ds(at, rows)]
+
+    def x_copy(number, part):
+        return remote(own_part(number, part), part_of(number, own_block, part), x_sems, (number, part), x_dev)
+
+    def y_copy(number, part):
+        return remote(own_part(number, part), part_of(number, own_block, part), y_sems, (number, part), y_dev)
 
     def fy_copy(number):
-        piece = slot(number, blocks[0], part=0)
+        piece = part_of(number, blocks[0], 0)
         return remote(piece, piece, fy_sems, (number,), y_dev)
 
     def fx_copy(number):
-        piece = slot(number, blocks[1], part=1)
+        piece = part_of(number, blocks[1], 1)
         return remote(piece, piece, fx_sems, (number,), x_dev)
 
-    def core_copy(number, kind):
-        piece = slot(number, blocks[kind]) if kind < 2 else slot(number, blocks[2], part=kind - 2)
-        return remote(piece, piece, core_sems, (number, kind), core_dev)
+    def core_copy(number, kind, part):
+        piece = part_of(number, blocks[kind], part)
+        return remote(piece, piece, core_sems, (number, kind, part), core_dev)
+
+
+    def eighth(at, block, first=0, rows=None):
+        view = end.at[at, core, block[0], block[1]]
+        return view if rows is None else view.at[pl.ds(first, rows)]
+
+    def own_eighth(first):
+        source, rows = (out_src, thin) if first == 0 else (hid_src, tall - thin)
+        return source.at[0, pl.ds(pl.multiple_of((z * 2 + core) * rows, rows), rows)]
+
+    def end_copy(axis, first):
+        rows = thin if first == 0 else tall - thin
+        return remote(
+            own_eighth(first), eighth(z, own_block, first, rows), end_sems, (axis, 0 if first == 0 else 1),
+            (x_dev, y_dev)[axis],
+        )
+
+    low = tall // 32 * 16
+
+    def end_fy_copy():
+        piece = eighth(z, blocks[0], 0, low)
+        return remote(piece, piece, fy_sems, (2,), y_dev)
+
+    def end_fx_copy():
+        piece = eighth(z, blocks[1], low, tall - low)
+        return remote(piece, piece, fx_sems, (2,), x_dev)
 
     def line_core_copy(at, kind):
-        piece = slot(3, blocks[kind], first=at)
+        piece = eighth(at, blocks[kind])
         return remote(piece, piece, line_core_sems, (at, kind), core_dev)
 
     def up_copy(at, kind):
-        piece = slot(3, blocks[kind], first=at)
+        piece = eighth(at, blocks[kind])
         return remote(piece, piece, up_sems, (at, kind), up_dev)
 
     def down_copy(at, kind):
-        piece = slot(3, blocks[kind], first=at)
+        piece = eighth(at, blocks[kind])
         return remote(piece, piece, down_sems, (at, kind), down_dev)
 
     def vec_copy(kind):
-        block = ((y, x), (y, x), (y, 1 - x))[kind]
-        source = vec_source if kind < 2 else vec.at[block]
+        block = (own_block, own_block, blocks[0])[kind]
+        source = vec_src if kind < 2 else vec.at[block]
         return remote(source, vec.at[block], vec_sems, (kind,), (x_dev, y_dev, y_dev)[kind])
 
     def loads():
-        copies = [
-            pltpu.make_async_copy(
-                sources[number].at[0, pl.ds(side * weights[number].shape[-2], weights[number].shape[-2])],
-                weights[number].at[side, y, x],
-                load_sems.at[number, side],
-            )
-            for number in range(3)
-            for side in range(2)
+        copies = []
+        for number, source in enumerate((qkv_src, in_src)):
+            rows = weights[number].shape[-2]
+            for side in range(2):
+                copies.append(
+                    pltpu.make_async_copy(
+                        source.at[0, pl.ds(side * rows, rows)], weights[number].at[side, y, x],
+                        load_sems.at[number, side],
+                    )
+                )
+        for at in range(depth):
+            for side in range(2):
+                for number, (source, first, rows) in enumerate(
+                    ((out_src, 0, thin), (hid_src, thin, tall - thin))
+                ):
+                    copies.append(
+                        pltpu.make_async_copy(
+                            source.at[0, pl.ds((at * 2 + side) * rows, rows)],
+                            end.at[at, side, y, x, pl.ds(first, rows)],
+                            end_load_sems.at[at, side, number],
+                        )
+                    )
+        return copies + [pltpu.make_async_copy(vec_src, vec.at[y, x], vec_load_sem)]
+
+    def full_stores():
+        return [
+            pltpu.make_async_copy(source, target, store_sems.at[number])
+            for number, (source, target) in enumerate(zip((*weights, vec), full_outs))
         ]
-        tall = hid.shape[-2]
-        copies += [
-            pltpu.make_async_copy(
-                sources[3].at[0, pl.ds((at * 2 + side) * tall, tall)],
-                hid.at[at, side, y, x],
-                hid_load_sems.at[at, side],
-            )
-            for at in range(depth)
-            for side in range(2)
-        ]
-        return copies + [pltpu.make_async_copy(vec_source, vec.at[y, x], vec_load_sem)]
-
-    def full_stores():
-        copies = [
-            pltpu.make_async_copy(weights[number], full_outs[number], store_sems.at[number])
-            for number in range(4)
-        ]
-        return copies + [pltpu.make_async_copy(vec, vec_out, store_sems.at[4])]
 
     def spread(kind):
         @pl.when(z < depth - 1)
@@ -561,9 +607,10 @@
         line_core_copy(z, kind).start()
 
     def hop(distance):
-        @pl.when(z >= distance)
-        def _():
-            for kind in range(3):
+        for kind in range(3):
+
+            @pl.when(z >= distance)
+            def _():
                 up_copy(z - distance, kind).wait_recv()
 
                 @pl.when(z < depth - 1)
@@ -572,9 +619,8 @@
 
                 line_core_copy(z - distance, kind).start()
 
-        @pl.when(z + distance < depth)
-        def _():
-            for kind in range(3):
+            @pl.when(z + distance < depth)
+            def _():
                 down_copy(z + distance, kind).wait_recv()
 
                 @pl.when(z > 0)
@@ -583,29 +629,34 @@
 
                 line_core_copy(z + distance, kind).start()
 
-    def direct(number):
-        x_copy(number).wait_recv()
+    def near(number):
+        x_copy(number, 0).wait_recv()
         fy_copy(number).start()
-        core_copy(number, 0).start()
-        y_copy(number).wait_recv()
+        core_copy(number, 0, 0).start()
+        y_copy(number, 1).wait_recv()
         fx_copy(number).start()
-        core_copy(number, 1).start()
+        core_copy(number, 1, 1).start()
+
+    def rest(number):
+        x_copy(number, 1).wait_recv()
+        core_copy(number, 0, 1).start()
+        y_copy(number, 0).wait_recv()
+        core_copy(number, 1, 0).start()
 
     def diagonal(number):
         fy_copy(number).wait_recv()
-        core_copy(number, 2).start()
+        core_copy(number, 2, 0).start()
         fx_copy(number).wait_recv()
-        core_copy(number, 3).start()
+        core_copy(number, 2, 1).start()
 
     def complete(number):
-        for kind in range(4):
-            core_copy(number, kind).wait_recv()
+        for kind in range(3):
+            for part in range(2):
+                core_copy(number, kind, part).wait_recv()
 
     def before_mix():
         @pl.when(step == 0)
         def _():
-            for copy in loads():
-                copy.start()
             barrier = pltpu.get_barrier_semaphore()
             for device in (x_dev, y_dev, core_dev):
                 pl.semaphore_signal(barrier, inc=1, device_id=device, device_id_type=MESH)
@@ -619,31 +670,35 @@
                 pl.semaphore_signal(barrier, inc=1, device_id=down_dev, device_id_type=MESH)
 
             pl.semaphore_wait(barrier, 3 + jnp.where(z > 0, 1, 0) + jnp.where(z < depth - 1, 1, 0))
-            x_copy(3).start()
-            y_copy(3).start()
+            for first in (0, thin):
+                end_copy(0, first).start()
+                end_copy(1, first).start()
             vec_copy(0).start()
             vec_copy(1).start()
-            for number in (0, 1):
-                x_copy(number).start()
-                y_copy(number).start()
-            x_copy(3).wait_recv()
-            fy_copy(3).start()
-            spread(0)
-            y_copy(3).wait_recv()
-            fx_copy(3).start()
-            spread(1)
+            x_copy(0, 0).start()
+            y_copy(0, 1).start()
+            x_copy(0, 1).start()
+            y_copy(0, 0).start()
+            for copy in loads():
+                copy.start()
+            for axis in range(2):
+                for first in (0, thin):
+                    end_copy(axis, first).wait_recv()
+                (end_fy_copy, end_fx_copy)[axis]().start()
+                spread(axis)
             vec_copy(0).wait_recv()
             vec_copy(2).start()
-            x_copy(2).start()
-            y_copy(2).start()
-            fy_copy(3).wait_recv()
-            fx_copy(3).wait_recv()
+            end_fy_copy().wait_recv()
+            end_fx_copy().wait_recv()
             spread(2)
-            direct(0)
-            direct(1)
+            near(0)
+            x_copy(1, 0).start()
+            y_copy(1, 1).start()
+            rest(0)
+            x_copy(1, 1).start()
+            y_copy(1, 0).start()
             hop(1)
             diagonal(0)
-            diagonal(1)
             vec_copy(1).wait_recv()
             vec_copy(2).wait_recv()
             complete(0)
@@ -653,12 +708,12 @@
     def before_out():
         @pl.when(step == 0)
         def _():
+            near(1)
             hop(2)
-            direct(2)
+            rest(1)
+            diagonal(1)
             hop(3)
-            diagonal(2)
             complete(1)
-            complete(2)
             for at in range(depth):
                 for kind in range(3):
                     line_core_copy(at, kind).wait_recv()
@@ -668,22 +723,30 @@
             for copy in full_stores():
                 copy.start()
 
+    @pl.when(step == 0)
+    def _():
+        forward_scratch[0][...] = jnp.zeros_like(forward_scratch[0])
+
     forward_layer(
-        step, step % 2, step % 2, before_mix, before_out, *io, weights, vec, *outs, *forward_scratch
+        step, segs, step % 2, before_mix, before_out, *io, weights, vec, *outs, *forward_scratch
     )
 
-    @pl.when(step == count - 1)
+    @pl.when(step == steps - 1)
     def _():
         for copy in full_stores():
             copy.wait()
-        for number in range(4):
-            x_copy(number).wait_send()
-            y_copy(number).wait_send()
+        for number in range(2):
+            for part in range(2):
+                x_copy(number, part).wait_send()
+                y_copy(number, part).wait_send()
+                for kind in range(3):
+                    core_copy(number, kind, part).wait_send()
             fx_copy(number).wait_send()
             fy_copy(number).wait_send()
-            if number < 3:
-                for kind in range(4):
-                    core_copy(number, kind).wait_send()
+            for first in (0, thin):
+                end_copy(number, first).wait_send()
+        end_fx_copy().wait_send()
+        end_fy_copy().wait_send()
         for kind in range(3):
             vec_copy(kind).wait_send()
             for at in range(depth):
@@ -700,51 +763,52 @@
 
 def full_weight_shapes(w_qkv, w_out, w_in, w_hid):
     half, width = w_out.shape[1:]
-    return [(2, 2, 2, half // 2, block.shape[2]) for block in (w_qkv, w_out, w_in)] + [
-        (4, 2, 2, 2, w_hid.shape[1] // 8, width)
+    return [(2, 2, 2, half // 2, block.shape[2]) for block in (w_qkv, w_in)] + [
+        (4, 2, 2, 2, (half + w_hid.shape[1]) // 8, width)
     ]
 
 
-def gather_forward(text, fresh, live, init, labels, blocks, vec):
-    count, operands, in_specs, out_specs, out_shape, scratch = forward_io(text, fresh, live, init, labels)
+def gather_forward(text, resets, counts, init, bounds, blocks, vec):
+    steps, saved, operands, in_specs, out_specs, out_shape, scratch = forward_io(
+        text, resets, counts, init, bounds
+    )
     shapes = full_weight_shapes(*blocks)
-    vec_shape = (2, 2) + vec.shape
+    full = [pltpu.VMEM(shape, BF16) for shape in shapes] + [pltpu.VMEM((2, 2) + vec.shape, F32)]
     any_spec = pl.BlockSpec(memory_space=pl.ANY)
     dma = pltpu.SemaphoreType.DMA
-    depth = shapes[3][0]
-    saved_count = len(out_specs)
-    outs = pl.pallas_call(
-        functools.partial(gather_forward_body, count),
-        grid=(count,),
+    depth = shapes[2][0]
+    *outs, acts, qkv, w_in, end, vecs = pl.pallas_call(
+        functools.partial(gather_forward_body, steps, text.shape[1]),
+        grid=(steps,),
         in_specs=in_specs + [any_spec] * 5,
-        out_specs=out_specs + [any_spec] * 5,
-        out_shape=out_shape + [jax.ShapeDtypeStruct(shape, BF16) for shape in (*shapes, vec_shape)],
+        out_specs=out_specs + [any_spec] * 4,
+        out_shape=out_shape + [jax.ShapeDtypeStruct(ref.shape, ref.dtype) for ref in full],
         scratch_shapes=scratch
-        + [pltpu.VMEM(shape, BF16) for shape in (*shapes, vec_shape)]
+        + full
         + [
-            dma((3, 2)), dma((depth, 2)), dma((5,)), dma((2, 4)), dma((2, 4)), dma((2, 4)), dma((2, 4)),
-            dma((2, 3, 4)), dma((2, depth, 3)), dma((2, depth, 3)), dma((2, depth, 3)), dma((2, 3)), dma,
+            dma((2, 2)), dma((depth, 2, 2)), dma((4,)), dma((2, 2, 2)), dma((2, 2, 2)), dma((2, 3)),
+            dma((2, 3)), dma((2, 2, 3, 2)), dma((2, 2, 2)), dma((2, depth, 3)), dma((2, depth, 3)),
+            dma((2, depth, 3)), dma((2, 3)), dma,
         ],
         compiler_params=pltpu.CompilerParams(
             vmem_limit_bytes=VMEM_BYTES, collective_id=1, has_side_effects=True
         ),
         name="gather_forward",
-    )(*operands, *blocks, vec)
-    saved = dict(zip(saved_shapes(*text.shape[2:]), outs))
-    return saved, outs[saved_count - 1], outs[saved_count : saved_count + 4], outs[saved_count + 4]
+    )(*operands, blocks[0], blocks[2], blocks[1], blocks[3], vec)
+    return dict(zip(saved, outs)), acts, (qkv, w_in, end), vecs
 
 
 def gather_apart(blocks, vec):
-    shapes = full_weight_shapes(*blocks)
-    full = []
-    for block, shape in zip(blocks, shapes):
-        gathered = lax.all_gather(block[0], "section")
-        lead = len(shape) - 4
-        gathered = gathered.reshape(2, 2, *shape[: lead], *shape[-2:])
-        order = (*range(2, 2 + lead), 0, 1, 2 + lead, 3 + lead)
-        full.append(gathered.transpose(order))
-    vec_full = lax.all_gather(vec, "section").reshape(2, 2, *vec.shape)
-    return full, vec_full
+    w_qkv, w_out, w_in, w_hid = [
+        lax.all_gather(block[0], "section").reshape(2, 2, *block.shape[1:]) for block in blocks
+    ]
+    half, width = w_out.shape[2:]
+    full = [
+        block.reshape(2, 2, 2, half // 2, -1).transpose(2, 0, 1, 3, 4) for block in (w_qkv, w_in)
+    ]
+    ends = [block.reshape(2, 2, 4, 2, -1, width).transpose(2, 3, 0, 1, 4, 5) for block in (w_out, w_hid)]
+    vecs = lax.all_gather(vec, "section").reshape(2, 2, *vec.shape)
+    return (*full, jnp.concatenate(ends, axis=4)), vecs
 
 
 GRAD_NAMES = ("first", "inner", "active", "branch", "x", "mix", "heads", "attn")
@@ -876,13 +940,35 @@
     ref[...] = (ref[...].astype(F32) + other[...].astype(F32)).astype(BF16)
 
 
+def build_extra(sums_ref, memory_ref, extra):
+    steps = sums_ref.shape[0]
+    width = memory_ref.shape[1]
+    lanes = extra.shape[-1]
+    mem = 10
+    extra[...] = jnp.zeros_like(extra)
+    for layer in range(2):
+        total = sums_ref[layer]
+        for step in range(layer + 2, steps, 2):
+            total = total + sums_ref[step]
+        for block, parts in enumerate(((6, 7, 5, 4, 8, 3), (9, 10, 11, 2, 1, 0))):
+            for piece in range(width // lanes):
+                extra[layer, block, piece * mem : (piece + 1) * mem, :] = memory_ref[
+                    16 - mem : 16, piece * lanes : (piece + 1) * lanes
+                ]
+                for at, part in enumerate(parts):
+                    row = mem * (width // lanes) + at * (width // lanes) + piece
+                    first = part * width + piece * lanes
+                    extra[layer, block, row : row + 1, :] = total[:, first : first + lanes]
+
+
 def grad_reduce_body(dp, segs_all, *refs):
     sources = refs[:8]
-    extra_ref = refs[8]
-    qkv_out, out_out, in_out, hid_out, extra_out = refs[9:14]
-    held = refs[14:22]
-    mine, theirs, landed, xp, xq, yq, yp, from_low, from_high = refs[22:31]
-    in_sems, extra_sems, core_sems, free_sem, xp_sems, xq_sems, yq_sems, yp_sems, up_sems, down_sems = refs[31:41]
+    sums_ref, memory_ref = refs[8:10]
+    piece_out = refs[10]
+    held = refs[11:19]
+    mine, theirs, landed, xp, xq, yq, yp, from_low, from_high = refs[19:28]
+    extra = refs[28]
+    in_sems, core_sems, free_sem, xp_sems, xq_sems, yq_sems, yp_sems, up_sems, down_sems = refs[29:38]
     section, place = lax.axis_index("section"), lax.axis_index("dp")
     x, y = section % 2, section // 2
     core, z = place % 2, place // 2
@@ -918,6 +1004,8 @@
         for copy in loads(0, kind):
             copy.start()
 
+    build_extra(sums_ref, memory_ref, extra)
+    extra_rows = extra.shape[2] // 3
     barrier = pltpu.get_barrier_semaphore()
     for device in (x_dev, y_dev, core_dev):
         pl.semaphore_signal(barrier, inc=1, device_id=device, device_id_type=MESH)
@@ -1085,6 +1173,10 @@
                     up_copy(kind, high).wait_recv()
                     add_into(mine.at[1, kind, high, y], from_low.at[kind, high])
 
+                @pl.when((z == 0) & (count > 0))
+                def _():
+                    up_copy(kind, high + 1).wait_send()
+
                 up_copy(kind, high).start()
 
             @pl.when(z > low)
@@ -1094,6 +1186,10 @@
                     down_copy(kind, low).wait_recv()
                     add_into(mine.at[1, kind, low, y], from_high.at[kind, low])
 
+                @pl.when((z == depth - 1) & (count > 0))
+                def _():
+                    down_copy(kind, low - 1).wait_send()
+
                 down_copy(kind, low).start()
 
             return 0
@@ -1111,16 +1207,7 @@
             down_copy(kind, z).wait_recv()
             add_into(mine.at[1, kind, z, y], from_high.at[kind, z])
 
-        total = mine[1, kind, z, y].astype(F32)
-        extra_out[kind] = total[half:, :]
-        if kind == 0:
-            qkv_out[0] = total[:half, 0:wide]
-            out_out[0] = total[:half, wide:lanes]
-        elif kind == 1:
-            in_out[0] = total[:half]
-        else:
-            for part in range(4):
-                hid_out[0, part * half : (part + 1) * half, :] = total[:half, part * thin : (part + 1) * thin]
+        piece_out[kind] = mine[1, kind, z, y]
 
     units = [(side, kind) for side in range(2) for kind in kinds]
     for unit, (side, kind) in enumerate(units):
@@ -1129,22 +1216,12 @@
             copy.wait()
         if unit >= 2:
             core_copy(unit - 2).wait_send()
-        extra_rows = extra_ref.shape[5]
-        extras = [
-            pltpu.make_async_copy(
-                extra_ref.at[layer, kind, core], mine.at[side, kind, :, :, pl.ds(half, extra_rows)],
-                extra_sems.at[0],
-            ),
-            pltpu.make_async_copy(
-                extra_ref.at[layer, kind, 1 - core], theirs.at[unit % 2, :, :, pl.ds(half, extra_rows)],
-                extra_sems.at[1],
-            ),
-        ]
-        for copy in extras:
-            copy.start()
+        for block in range(2):
+            rows_now = extra[layer, block, kind * extra_rows : (kind + 1) * extra_rows, :].astype(BF16)
+            for at in range(depth):
+                mine[side, kind, at, block, half:, :] = rows_now
+                theirs[unit % 2, at, block, half:, :] = rows_now
         multiply(side, kind, unit)
-        for copy in extras:
-            copy.wait()
         if unit >= 2:
             pl.semaphore_wait(free_sem, 1)
         core_copy(unit).start()
@@ -1181,11 +1258,11 @@
             yq_copy(side, kind).wait_send()
 
         def sent(at, _):
-            @pl.when(at > z)
+            @pl.when((at > z) & ((z > 0) | (at == 1)))
             def _():
                 up_copy(kind, at).wait_send()
 
-            @pl.when(at < z)
+            @pl.when((at < z) & ((z < depth - 1) | (at == depth - 2)))
             def _():
                 down_copy(kind, at).wait_send()
 
@@ -1194,65 +1271,100 @@
         lax.fori_loop(0, depth, sent, 0)
 
 
-def grad_reduce_shapes(dp, steps, rows, width, extra_rows):
+def grad_reduce_shapes(dp, steps, rows, width):
     half = width // 2
     lanes = 4 * width // dp
     depth = dp // 2
     cut = depth // 2
+    extra_rows = 16
     tall = half + extra_rows
     held = [width, 4 * width, 4 * width, width, width, 3 * width, width, width]
-    return [pltpu.VMEM((steps // 2 * rows, columns), BF16) for columns in held] + [
-        pltpu.VMEM(shape + (tall, lanes), BF16)
-        for shape in (
-            (2, 3, depth, 2), (2, depth, 2), (2, depth, 2), (3, cut, 2), (3, depth - cut),
-            (2, 3, depth - cut), (3, cut), (3, depth), (3, depth),
-        )
-    ]
-
-
-def padded_bytes(shapes):
-    total = 0
-    for shape in shapes:
-        *lead, tall, lanes = shape.shape
-        size = 2 * tall * -(-lanes // 128) * 128
-        for count in lead:
-            size *= count
-        total += size
-    return total
-
-
-def grad_reduce(dp, saved, extras):
+    return (
+        [pltpu.VMEM((steps // 2 * rows, columns), BF16) for columns in held]
+        + [
+            pltpu.VMEM(shape + (tall, lanes), BF16)
+            for shape in (
+                (2, 3, depth, 2), (2, depth, 2), (2, depth, 2), (3, cut, 2), (3, depth - cut),
+                (2, 3, depth - cut), (3, cut), (3, depth), (3, depth),
+            )
+        ]
+        + [pltpu.VMEM((2, 2, 3 * extra_rows, lanes), F32)]
+    )
+
+
+def unpack_body(mem, piece_ref, qkv_ref, out_ref, in_ref, hid_ref, memory_ref, vec_ref):
+    half = qkv_ref.shape[1]
+    wide, thin, lanes = qkv_ref.shape[2], out_ref.shape[2], in_ref.shape[2]
+    width = memory_ref.shape[1]
+    qkv_ref[0] = piece_ref[0, 0:half, 0:wide].astype(F32)
+    out_ref[0] = piece_ref[0, 0:half, wide:lanes].astype(F32)
+    in_ref[0] = piece_ref[1, 0:half, :].astype(F32)
+    for part in range(4):
+        hid_ref[0, part * half : (part + 1) * half, :] = piece_ref[
+            2, 0:half, part * thin : (part + 1) * thin
+        ].astype(F32)
+    extra = jnp.concatenate([piece_ref[kind, half:, :].astype(F32) for kind in range(3)], axis=0)
+    pieces = width // lanes
+    for piece in range(pieces):
+        memory_ref[:, piece * lanes : (piece + 1) * lanes] = extra[piece * mem : (piece + 1) * mem, :]
+    for at in range(6 * pieces):
+        row = mem * pieces + at
+        vec_ref[:, at * lanes : (at + 1) * lanes] = extra[row : row + 1, :]
+
+
+def grad_reduce(dp, mem, saved, sums, memory):
     sources = [saved[name] for name in GRAD_NAMES]
     steps, rows, width = sources[0].shape
     segs_all = steps // 2
     half = width // 2
     lanes = 4 * width // dp
     thin = width // dp
-    extra_rows = extras.shape[5]
     depth = dp // 2
     any_spec = pl.BlockSpec(memory_space=pl.ANY)
     dma = pltpu.SemaphoreType.DMA
-    return pl.pallas_call(
+    shapes = grad_reduce_shapes(dp, steps, rows, width)
+    piece = pl.pallas_call(
         functools.partial(grad_reduce_body, dp, segs_all),
-        in_specs=[any_spec] * 9,
-        out_specs=[pl.BlockSpec(memory_space=pltpu.VMEM)] * 5,
-        out_shape=[
-            jax.ShapeDtypeStruct(shape, F32)
-            for shape in (
-                (1, half, 3 * thin), (1, half, thin), (1, half, lanes), (1, 4 * half, thin),
-                (3, extra_rows, lanes),
-            )
-        ],
-        scratch_shapes=grad_reduce_shapes(dp, steps, rows, width, extra_rows)
+        in_specs=[any_spec] * 8 + [pl.BlockSpec(memory_space=pltpu.VMEM)] * 2,
+        out_specs=pl.BlockSpec(memory_space=pltpu.VMEM),
+        out_shape=jax.ShapeDtypeStruct((3,) + shapes[8].shape[-2:], BF16),
+        scratch_shapes=shapes
         + [
-            dma((8, segs_all)), dma((2,)), dma((2, 6)), pltpu.SemaphoreType.REGULAR, dma((2, 3)),
-            dma((2, 3)), dma((2, 2, 3)), dma((2, 3)), dma((2, 3, depth)), dma((2, 3, depth)),
+            dma((8, segs_all)), dma((2, 6)), pltpu.SemaphoreType.REGULAR, dma((2, 3)), dma((2, 3)),
+            dma((2, 2, 3)), dma((2, 3)), dma((2, 3, depth)), dma((2, 3, depth)),
         ],
         compiler_params=pltpu.CompilerParams(
             vmem_limit_bytes=VMEM_BYTES, collective_id=0, has_side_effects=True
         ),
         name="grad_reduce",
-    )(*sources, extras)
+    )(*sources, sums, memory)
+    *grads, memory, vec = pl.pallas_call(
+        functools.partial(unpack_body, mem),
+        out_shape=[
+            jax.ShapeDtypeStruct(shape, F32)
+            for shape in (
+                (1, half, 3 * thin), (1, half, thin), (1, half, lanes), (1, 4 * half, thin),
+                (mem, width), (1, 6 * width),
+            )
+        ],
+        name="unpack",
+    )(piece)
+    place = lax.axis_index("dp")
+    bias_len = 5 * width // dp
+    bias = lax.dynamic_slice(vec, (0, place * bias_len), (1, bias_len))
+    gain = lax.dynamic_slice(vec, (0, 5 * width + place * thin), (1, thin))
+    return (memory, *grads, bias, gain)
+
+
+def padded_bytes(shapes):
+    total = 0
+    for shape in shapes:
+        *lead, tall, lanes = shape.shape
+        size = (4 if shape.dtype == F32 else 2) * tall * -(-lanes // 128) * 128
+        for count in lead:
+            size *= count
+        total += size
+    return total
 
 
 def other_core(block, dp):
@@ -1278,36 +1390,32 @@
     rows = text_len + 2 * mem_rows
     half = width // 2
     dp = lax.axis_size("dp")
-    vector_len = biases.shape[1]
-
     blocks = (w_qkv, w_out, w_in, w_hid)
-    vec = jnp.concatenate([biases[0], norm_gains[0]])
-    vec = jnp.pad(vec, (0, 16 * width - vec.shape[0])).reshape(16, width)
-    filler = jnp.full((items, segs, mem_rows), -1, jnp.int32)
-    labels = jnp.concatenate([filler, jnp.cumsum(boundaries, axis=-1), filler], axis=-1)
-
-    def flags(values):
-        return jnp.broadcast_to(values.astype(jnp.int32).reshape(-1, 1, 1), (items * segs, 1, width))
-
-    live = flags(jnp.arange(segs)[None] < seg_counts[:, None])
-    fresh = flags((jnp.arange(segs)[None] == 0) | (mem_resets > 0))
-    text = jnp.pad(text_rows, ((0, 0), (0, 0), (mem_rows, mem_rows), (0, 0)))
-    start = memory_init.astype(F32)
-    init = jnp.stack(
-        [jnp.pad(start, ((0, 16 - mem_rows), (0, 0))), jnp.pad(start, ((16 - mem_rows, 0), (0, 0)))]
-    )
-
+    vec = jnp.concatenate([biases, norm_gains], axis=1).astype(F32)
     steps = 2 * items * segs
     if dp == 8:
-        saved, activations, weights, vecs = gather_forward(text, fresh, live, init, labels, blocks, vec)
+        saved, acts, weights, vecs = gather_forward(
+            text_rows, mem_resets, seg_counts, memory_init, boundaries, blocks, vec
+        )
     else:
         weights, vecs = gather_apart(blocks, vec)
-        saved, activations = forward_steps(text, fresh, live, init, labels, weights, vecs)
-    grads, sums, input_grads, memory_grad = backward_steps(
-        cotangent, fresh, live, labels, weights, vecs, saved
+        saved, acts = forward_steps(
+            text_rows, mem_resets, seg_counts, memory_init, boundaries, weights, vecs
+        )
+    grads, sums, input_grads, memory_grad, acts = backward_steps(
+        cotangent, mem_resets, seg_counts, boundaries, mem_rows, acts, weights, vecs, saved
     )
     saved.update(grads)
-
+    reduce = grad_reduce
+    if padded_bytes(grad_reduce_shapes(dp, steps, rows, width)) > 60 * 2**20:
+        reduce = grad_reduce_apart
+    return (acts, input_grads, *reduce(dp, mem_rows, saved, sums, memory_grad))
+
+
+def grad_reduce_apart(dp, mem_rows, saved, sums, memory_grad):
+    steps, width = sums.shape[0], memory_grad.shape[1]
+    half = width // 2
+    vector_len = 5 * width
     lanes = 4 * width // dp
     memory_part = memory_grad[16 - mem_rows :].reshape(-1)
     memory_len = -(-memory_part.shape[0] // lanes) * lanes
@@ -1333,22 +1441,6 @@
         extra = extra.reshape(2, dp // 2, 2, 3, extra_rows, lanes).transpose(3, 2, 1, 0, 4, 5)
         extras.append(extra.astype(BF16))
     extras = jnp.stack(extras)
-    reduce = grad_reduce
-    if padded_bytes(grad_reduce_shapes(dp, steps, rows, width, extra_rows)) > 60 * 2**20:
-        reduce = grad_reduce_apart
-    *grads, flat = reduce(dp, saved, extras)
-    flat = flat.reshape(-1)
-    return (
-        activations,
-        input_grads,
-        flat[: mem_rows * width].reshape(mem_rows, width),
-        *grads,
-        flat[memory_len : memory_len + vector_part][None],
-        flat[memory_len + vector_part : used][None],
-    )
-
-
-def grad_reduce_apart(dp, saved, extras):
     wires = [weight_grads(layer, dp, saved, extras[layer]) for layer in range(2)]
     mine = jnp.stack([wires[0][0], wires[1][0]])
     theirs = other_core(jnp.stack([wires[0][1], wires[1][1]]), dp)
@@ -1361,16 +1453,18 @@
     own = lax.psum_scatter(
         own, "dp", scatter_dimension=0, axis_index_groups=groups, tiled=True
     )[0].astype(F32)
-    half = tall - extras.shape[5]
     thin = lanes // 4
     body = own[:, :half]
     hid = body[2].reshape(half, 4, thin).transpose(1, 0, 2).reshape(4 * half, thin)
+    flat = own[:, half:].reshape(-1)
     return (
+        flat[: mem_rows * width].reshape(mem_rows, width),
         body[0, :, : 3 * thin][None],
         body[0, :, 3 * thin :][None],
         body[1][None],
         hid[None],
-        own[:, half:],
+        flat[memory_len : memory_len + vector_part][None],
+        flat[memory_len + vector_part : used][None],
     )
 
 

time: 450 us -> 430 us (0.956)
  local copies, waits for them, and re-layouts: 19.7 us -> 9.86 us
  other arithmetic: 6.36 us -> 1.36 us
    pallas_call x2 -> x3, Pallas kernels: 221 us -> 210 us  [the longest x1 143 us: gather_forward(): pl.pallas_call(functools.partial(gather_forward_body, steps, text.shape[1...]
    pallas_call x1, Pallas kernels: 194 us -> 200 us  [grad_reduce(): pl.pallas_call(functools.partial(grad_reduce_body, dp, segs_all), in_spec...]
    unnamed x29 -> x6, local copies, waits for them, and re-layouts: 10.3 us -> 7.27 us
where the time goes in v5:
time: 430 us; the launch traced here: 424 us
  Pallas kernels  411 us (96%)
  local copies, waits for them, and re-layouts  9.86 us (2%)
    pallas_call x1, Pallas kernels, grad_reduce(): pl.pallas_call(functools.partial(grad_reduce_body, dp, segs_all), in_spec...  200 us
    pallas_call x1, Pallas kernels, gather_forward(): pl.pallas_call(functools.partial(gather_forward_body, steps, text.shape[1...  143 us
    pallas_call x1, Pallas kernels, backward_steps(): pl.pallas_call(functools.partial(backward_body, steps, segs, mem), grid=(...  64.6 us

profile of v5, /device:TPU:0, one launch (start us, length us, event | category | flops | bytes accessed | tf_op | source)
XLA Modules:
  0.0 423.6 jit_solution(207392572103764444)
XLA Ops:
  1.3 2.2 copy.21.refs_2_
  3.5 1.4 maximum_convert_fusion.refs_9_
  4.8 142.9 %gather_forward.1 = (bf16[4,320,768]{2,1,0:T(8,128)(2,1)}, bf16[4,320,2304]{2,1,0:T(8,128)(2,1)}, bf16[4,320,768]{2,1,0:T(8,128)(2,1)}, bf16[4,320,768]{2,1,0:T(...) custom-call(s32[1,2]{1,0:T(1,128)} %resets_ref.1, ...), custom_call_target="tpu_custom_call" | custom-call | tf_op jit(solution)/shard_map/gather_forward/pallas_call | solution.py:780
  147.8 64.6 %backward_steps.1 = (bf16[4,320,768]{2,1,0:T(8,128)(2,1)}, bf16[4,320,3072]{2,1,0:T(8,128)(2,1)}, bf16[4,320,768]{2,1,0:T(8,128)(2,1)}, bf16[4,320,2304]{2,1,0:T...) custom-call(s32[1,2]{1,0:T(1,128)} %resets_ref.1, ...), custom_call_target="tpu_custom_call" | custom-call | tf_op jit(solution)/shard_map/backward_steps/pallas_call | solution.py:423
  212.4 200.4 %grad_reduce.1.piece_ref = bf16[3,400,384]{2,1,0:T(8,128)(2,1)} custom-call(bf16[4,320,768]{2,1,0:T(8,128)(2,1)} %get-tuple-element.50.refs_0_, bf16[4,320,3072]{2,1,0:T(8,128)(2,1)} %get-tuple-element.51.refs_1_, bf16[4,320,3072]{2,1,0:T(8,128)(2,1)} %get-tuple-element.52.refs_2_, bf16[4,320,768]{2,1,0:T(8,128)(2,1)} %get-tuple-element.53.refs_3_, ...), custom_call_target="tpu_custom_call" | custom-call | tf_op jit(solution)/shard_map/grad_reduce/pallas_call | solution.py:1326
  412.8 2.7 unpack.1
  415.5 0.0 copy-start
  415.5 2.2 copy.24
  417.7 2.0 copy.22
  419.7 0.0 copy-done
  419.7 0.8 copy.23
  420.5 1.3 constant_dynamic-slice_fusion.1
  421.9 1.3 constant_dynamic-slice_fusion
Async XLA Ops:
  415.5 4.3 %copy-start = (f32[1,384,96]{2,1,0:T(8,128)S(1)}, f32[1,384,96]{2,1,0:T(8,128)}, u32[]{:S(2)}) copy-start(f32[1,384,96]{2,1,0:T(8,128)} %get-tuple-element.69) | copy-start | bytes 442372
